TPU v7x, 128 devices: a whole 4x4x4 slice. The times are simulated.
128 devices in a mesh: row: 16 (over x, y), col: 8 (over z, core).
Axes of the slice: x: 4, y: 4, z: 4, core: 2. Of those that a mesh axis runs over, the one named last changes fastest.
Arguments:
- coefficients: bfloat16 [10240, 32, 256], P('row'), may hold values from -0.59765625 to 0.59765625
- range_start: int32 [80], replicated, may hold values from 0 to 127
- range_end: int32 [80], replicated, may hold values from 129 to 256
- pair_list: int32 [1976, 2], replicated, may hold values from 0 to 79, as said below
Outputs:
- exchange_matrix: float32 [10240, 10, 8, 128], P('row', None, 'col')
Inputs may be any that keep to these rules, and one draw needn't show every extreme that they name: `pair_list`: 1976 distinct unordered block pairs, the smaller block first; every block is listed with itself.
All inputs are finite; a program needn't handle non-finite values.
Results may differ from a plain program's by a relative error of at most 0.0003.
Values may be sent and summed in bfloat16 or wider, within the bound.
No kernel may reach another device: no remote copies, remote signals or barrier semaphores. Data moves between devices by JAX's collectives and lax.ppermute only.
A program may use at most 192 MiB of HBM per device.

v0:
```python
import jax
import jax.numpy as jnp
from jax import lax
from jax.sharding import PartitionSpec as P

BLK = 128


def listed_matrix(pair_list, block_count):
    marked = (
        jnp.zeros((block_count, block_count), jnp.int32).at[pair_list[:, 0], pair_list[:, 1]].set(1)
    )
    return jnp.maximum(marked, marked.T)


def per_device(coefficients, range_start, range_end, pair_list):
    row_count = lax.axis_size("row")
    col_count = lax.axis_size("col")
    row_index = lax.axis_index("row")
    col_index = lax.axis_index("col")
    local_rows, aux_count, orbital_count = coefficients.shape
    block_local = local_rows // BLK
    block_count = block_local * row_count
    slot_count = -(-block_local // col_count)
    column_blocks = block_count // col_count
    flat_width = aux_count * orbital_count
    listed = listed_matrix(pair_list, block_count)
    first_block = row_index * block_local
    own_listed = lax.dynamic_slice_in_dim(listed, first_block, block_local, 0)
    own_start = lax.dynamic_slice_in_dim(range_start, first_block, block_local)
    own_end = lax.dynamic_slice_in_dim(range_end, first_block, block_local)
    orbital = jnp.arange(orbital_count, dtype=jnp.int32)
    inside = (orbital[None, :] >= own_start[:, None]) & (orbital[None, :] < own_end[:, None])
    masked = coefficients.reshape(block_local, BLK, aux_count, orbital_count) * inside[
        :, None, None, :
    ].astype(jnp.bfloat16)
    masked = masked.reshape(block_local, BLK, flat_width)
    own_rows = masked.reshape(block_local * BLK, flat_width)
    send_offset = (col_index - first_block) % col_count + col_count * jnp.arange(
        slot_count, dtype=jnp.int32
    )
    send_blocks = jnp.take(masked, jnp.minimum(send_offset, block_local - 1), axis=0)
    send_blocks = send_blocks * (send_offset < block_local)[:, None, None].astype(jnp.bfloat16)

    def one_column(column_block, position):
        source_row = position // slot_count
        slot_index = position % slot_count
        offset = (col_index - source_row * block_local) % col_count + slot_index * col_count
        present = offset < block_local
        target = source_row * block_local + jnp.minimum(offset, block_local - 1)
        weights = jnp.take(own_listed, target, axis=1)
        active = present
        active = active & (jnp.sum(weights) > 0)

        def compute_block():
            product = lax.dot_general(
                own_rows, column_block, (((1,), (1,)), ((), ())), preferred_element_type=jnp.float32
            )
            return product * jnp.repeat(weights.astype(jnp.float32), BLK)[:, None]

        def skip_block():
            return jnp.zeros((block_local * BLK, BLK), jnp.float32)

        return lax.cond(active, compute_block, skip_block)

    block_piece = lax.all_gather(send_blocks, "row", axis=0, tiled=True)
    positions = jnp.arange(block_piece.shape[0], dtype=jnp.int32)

    def single_entry(entry_pair):
        return one_column(entry_pair[0], entry_pair[1])

    columns = lax.map(single_entry, (block_piece, positions))
    target_cols = jnp.arange(column_blocks, dtype=jnp.int32) * col_count + col_index
    holder = target_cols // block_local
    holder_slot = (
        target_cols - holder * block_local - (col_index - holder * block_local) % col_count
    ) // col_count
    tile = jnp.take(columns, holder * slot_count + holder_slot, axis=0).transpose(1, 0, 2)
    return tile.reshape(block_local * BLK, column_blocks, 1, BLK)


def solution(mesh):
    in_specs = (P("row", None, None), P(), P(), P())
    out_specs = P("row", None, "col", None)
    return jax.shard_map(
        per_device, mesh=mesh, in_specs=in_specs, out_specs=out_specs, check_vma=False
    )
```

profile of v0, /device:TPU:1, one launch (start us, length us, event | category | flops | bytes accessed | tf_op | source)
XLA Modules:
  0.0 383.0 jit_solution(17388273904476339688)
XLA Ops:
  8.1 16.5 %reshape.225 = bf16[5,128,8192]{2,1,0:T(8,128)(2,1)} reshape(bf16[640,32,256]{2,1,0:T(8,128)(2,1)} %param.8) | data formatting | bytes 20971520 | tf_op jit(solution)/shard_map/reshape | solution.py:34
  28.1 10.2 %scatter_custom_fusion = s32[6400]{0:T(1024)S(1)} fusion(s32[1976]{0:T(1024)S(1)} %broadcast_select_fusion.1, s32[1976]{0:T(1024)S(1)} %broadcast.370, s32[]{:T(128)} %constant.197.clone.1), kind=kCustom, calls=%fused_computation.24 | custom fusion | bytes 25604
  45.1 20.7 %copy.17 = bf16[80,8,32,256]{3,1,2,0:T(8,128)(2,1)} copy(bf16[80,8,32,256]{3,2,1,0:T(8,128)(2,1)} %bitcast.41) | data formatting | bytes 20971520
  65.8 20.7 %copy.16 = bf16[80,8,32,256]{3,1,2,0:T(8,128)(2,1)} copy(bf16[80,8,32,256]{3,2,1,0:T(8,128)(2,1)} %bitcast.40) | data formatting | bytes 20971520
  86.5 13.2 %mul.110 = bf16[640,8192]{1,0:T(8,128)(2,1)} multiply(bf16[640,8192]{1,0:T(8,128)(2,1)} %bitcast.43, bf16[640,8192]{1,0:T(8,128)(2,1)} %bitcast.42) | non-fusion elementwise | flops 5242880 | bytes 31457280 | tf_op jit(solution)/shard_map/mul | solution.py:34
  99.8 128.3 %all-gather.2.cloned.1.call-done = bf16[16,128,8192]{2,1,0:T(8,128)(2,1)} async-done(((bf16[1,128,8192]{2,1,0:T(8,128)(2,1)}), bf16[16,128,8192]{2,1,0:T(8,128)(2,1)}) %all-gather.2.cloned.1.call-update) | async-done | bytes 33554448 | tf_op jit(solution)/shard_map/all_gather | solution.py:66
  228.2 138.9 %while.15 = (s32[]{:T(128)}, f32[16,640,128]{2,1,0:T(8,128)}, s32[16]{0:T(128)S(1)}, s32[]{:T(128)}, s32[5,80]{0,1:T(8,128)S(1)}, /*index=5*/bf16[16,128,8192]{2...) while((s32[]{:T(128)}, f32[16,640,128]{2,1,0:T(8,128)}, ...), condition=%wide.region_5.6_spmd, body=%wide.region_1.0_spmd.sunk | while | flops 1342259200 | bytes 14228012 | solution.py:72
  230.9 8.1 %conditional.2 = (f32[1,640,128]{1,2,0:T(8,128)S(1)}) conditional(s32[]{:T(128)} %convert_element_type.28, () %tuple.56, (bf16[16,128,8192]{2,1,0:T(8,128)(2,1)}, s32[]{:T(128)}, bf16[640,8192]{1,0:T(8,128)(2,1)}, s32[5]{0:T(128)S(1)}) %tuple.57), branch_computations={%region_3.3_spmd, %region_4.4_spmd} | conditional | flops 1342259200 | bytes 12916292 | solution.py:64
  242.5 8.1 %conditional.2 = (f32[1,640,128]{1,2,0:T(8,128)S(1)}) conditional(s32[]{:T(128)} %convert_element_type.28, () %tuple.56, (bf16[16,128,8192]{2,1,0:T(8,128)(2,1)}, s32[]{:T(128)}, bf16[640,8192]{1,0:T(8,128)(2,1)}, s32[5]{0:T(128)S(1)}) %tuple.57), branch_computations={%region_3.3_spmd, %region_4.4_spmd} | conditional | flops 1342259200 | bytes 12916292 | solution.py:64
  257.9 8.1 %conditional.2 = (f32[1,640,128]{1,2,0:T(8,128)S(1)}) conditional(s32[]{:T(128)} %convert_element_type.28, () %tuple.56, (bf16[16,128,8192]{2,1,0:T(8,128)(2,1)}, s32[]{:T(128)}, bf16[640,8192]{1,0:T(8,128)(2,1)}, s32[5]{0:T(128)S(1)}) %tuple.57), branch_computations={%region_3.3_spmd, %region_4.4_spmd} | conditional | flops 1342259200 | bytes 12916292 | solution.py:64
  258.0 8.0 %fusion.6 = f32[1,640,128]{1,2,0:T(8,128)S(1)} fusion(bf16[640,8192]{1,0:T(8,128)(2,1)} %get-tuple-element.146, bf16[16,128,8192]{2,1,0:T(8,128)(2,1)} %get-tuple-element.144, s32[]{:T(128)} %get-tuple-element.145, f32[640]{0:T(1024)S(1)} %broadcast_bitcast_fusion), kind=kOutput, calls=%fused_computation.6 | convolution fusion | flops 1342259200 | bytes 12913664 | tf_op jit(solution)/shard_map/while/body/eval_jaxpr/cond/branch_1_fun/dot_general | solution.py:56
  273.2 8.1 %conditional.2 = (f32[1,640,128]{1,2,0:T(8,128)S(1)}) conditional(s32[]{:T(128)} %convert_element_type.28, () %tuple.56, (bf16[16,128,8192]{2,1,0:T(8,128)(2,1)}, s32[]{:T(128)}, bf16[640,8192]{1,0:T(8,128)(2,1)}, s32[5]{0:T(128)S(1)}) %tuple.57), branch_computations={%region_3.3_spmd, %region_4.4_spmd} | conditional | flops 1342259200 | bytes 12916292 | solution.py:64
  273.3 8.0 %fusion.6 = f32[1,640,128]{1,2,0:T(8,128)S(1)} fusion(bf16[640,8192]{1,0:T(8,128)(2,1)} %get-tuple-element.146, bf16[16,128,8192]{2,1,0:T(8,128)(2,1)} %get-tuple-element.144, s32[]{:T(128)} %get-tuple-element.145, f32[640]{0:T(1024)S(1)} %broadcast_bitcast_fusion), kind=kOutput, calls=%fused_computation.6 | convolution fusion | flops 1342259200 | bytes 12913664 | tf_op jit(solution)/shard_map/while/body/eval_jaxpr/cond/branch_1_fun/dot_general | solution.py:56
  284.9 8.1 %conditional.2 = (f32[1,640,128]{1,2,0:T(8,128)S(1)}) conditional(s32[]{:T(128)} %convert_element_type.28, () %tuple.56, (bf16[16,128,8192]{2,1,0:T(8,128)(2,1)}, s32[]{:T(128)}, bf16[640,8192]{1,0:T(8,128)(2,1)}, s32[5]{0:T(128)S(1)}) %tuple.57), branch_computations={%region_3.3_spmd, %region_4.4_spmd} | conditional | flops 1342259200 | bytes 12916292 | solution.py:64
  285.0 8.0 %fusion.6 = f32[1,640,128]{1,2,0:T(8,128)S(1)} fusion(bf16[640,8192]{1,0:T(8,128)(2,1)} %get-tuple-element.146, bf16[16,128,8192]{2,1,0:T(8,128)(2,1)} %get-tuple-element.144, s32[]{:T(128)} %get-tuple-element.145, f32[640]{0:T(1024)S(1)} %broadcast_bitcast_fusion), kind=kOutput, calls=%fused_computation.6 | convolution fusion | flops 1342259200 | bytes 12913664 | tf_op jit(solution)/shard_map/while/body/eval_jaxpr/cond/branch_1_fun/dot_general | solution.py:56
  300.3 8.1 %conditional.2 = (f32[1,640,128]{1,2,0:T(8,128)S(1)}) conditional(s32[]{:T(128)} %convert_element_type.28, () %tuple.56, (bf16[16,128,8192]{2,1,0:T(8,128)(2,1)}, s32[]{:T(128)}, bf16[640,8192]{1,0:T(8,128)(2,1)}, s32[5]{0:T(128)S(1)}) %tuple.57), branch_computations={%region_3.3_spmd, %region_4.4_spmd} | conditional | flops 1342259200 | bytes 12916292 | solution.py:64
  300.4 8.0 %fusion.6 = f32[1,640,128]{1,2,0:T(8,128)S(1)} fusion(bf16[640,8192]{1,0:T(8,128)(2,1)} %get-tuple-element.146, bf16[16,128,8192]{2,1,0:T(8,128)(2,1)} %get-tuple-element.144, s32[]{:T(128)} %get-tuple-element.145, f32[640]{0:T(1024)S(1)} %broadcast_bitcast_fusion), kind=kOutput, calls=%fused_computation.6 | convolution fusion | flops 1342259200 | bytes 12913664 | tf_op jit(solution)/shard_map/while/body/eval_jaxpr/cond/branch_1_fun/dot_general | solution.py:56
  312.0 8.1 %conditional.2 = (f32[1,640,128]{1,2,0:T(8,128)S(1)}) conditional(s32[]{:T(128)} %convert_element_type.28, () %tuple.56, (bf16[16,128,8192]{2,1,0:T(8,128)(2,1)}, s32[]{:T(128)}, bf16[640,8192]{1,0:T(8,128)(2,1)}, s32[5]{0:T(128)S(1)}) %tuple.57), branch_computations={%region_3.3_spmd, %region_4.4_spmd} | conditional | flops 1342259200 | bytes 12916292 | solution.py:64
  327.3 8.1 %conditional.2 = (f32[1,640,128]{1,2,0:T(8,128)S(1)}) conditional(s32[]{:T(128)} %convert_element_type.28, () %tuple.56, (bf16[16,128,8192]{2,1,0:T(8,128)(2,1)}, s32[]{:T(128)}, bf16[640,8192]{1,0:T(8,128)(2,1)}, s32[5]{0:T(128)S(1)}) %tuple.57), branch_computations={%region_3.3_spmd, %region_4.4_spmd} | conditional | flops 1342259200 | bytes 12916292 | solution.py:64
  327.4 8.0 %fusion.6 = f32[1,640,128]{1,2,0:T(8,128)S(1)} fusion(bf16[640,8192]{1,0:T(8,128)(2,1)} %get-tuple-element.146, bf16[16,128,8192]{2,1,0:T(8,128)(2,1)} %get-tuple-element.144, s32[]{:T(128)} %get-tuple-element.145, f32[640]{0:T(1024)S(1)} %broadcast_bitcast_fusion), kind=kOutput, calls=%fused_computation.6 | convolution fusion | flops 1342259200 | bytes 12913664 | tf_op jit(solution)/shard_map/while/body/eval_jaxpr/cond/branch_1_fun/dot_general | solution.py:56
  342.7 8.1 %conditional.2 = (f32[1,640,128]{1,2,0:T(8,128)S(1)}) conditional(s32[]{:T(128)} %convert_element_type.28, () %tuple.56, (bf16[16,128,8192]{2,1,0:T(8,128)(2,1)}, s32[]{:T(128)}, bf16[640,8192]{1,0:T(8,128)(2,1)}, s32[5]{0:T(128)S(1)}) %tuple.57), branch_computations={%region_3.3_spmd, %region_4.4_spmd} | conditional | flops 1342259200 | bytes 12916292 | solution.py:64
  342.8 8.0 %fusion.6 = f32[1,640,128]{1,2,0:T(8,128)S(1)} fusion(bf16[640,8192]{1,0:T(8,128)(2,1)} %get-tuple-element.146, bf16[16,128,8192]{2,1,0:T(8,128)(2,1)} %get-tuple-element.144, s32[]{:T(128)} %get-tuple-element.145, f32[640]{0:T(1024)S(1)} %broadcast_bitcast_fusion), kind=kOutput, calls=%fused_computation.6 | convolution fusion | flops 1342259200 | bytes 12913664 | tf_op jit(solution)/shard_map/while/body/eval_jaxpr/cond/branch_1_fun/dot_general | solution.py:56
  354.4 8.1 %conditional.2 = (f32[1,640,128]{1,2,0:T(8,128)S(1)}) conditional(s32[]{:T(128)} %convert_element_type.28, () %tuple.56, (bf16[16,128,8192]{2,1,0:T(8,128)(2,1)}, s32[]{:T(128)}, bf16[640,8192]{1,0:T(8,128)(2,1)}, s32[5]{0:T(128)S(1)}) %tuple.57), branch_computations={%region_3.3_spmd, %region_4.4_spmd} | conditional | flops 1342259200 | bytes 12916292 | solution.py:64
  354.5 8.0 %fusion.6 = f32[1,640,128]{1,2,0:T(8,128)S(1)} fusion(bf16[640,8192]{1,0:T(8,128)(2,1)} %get-tuple-element.146, bf16[16,128,8192]{2,1,0:T(8,128)(2,1)} %get-tuple-element.144, s32[]{:T(128)} %get-tuple-element.145, f32[640]{0:T(1024)S(1)} %broadcast_bitcast_fusion), kind=kOutput, calls=%fused_computation.6 | convolution fusion | flops 1342259200 | bytes 12913664 | tf_op jit(solution)/shard_map/while/body/eval_jaxpr/cond/branch_1_fun/dot_general | solution.py:56
  (130 shorter events, 82.1 us)
Async XLA Ops:
  6.5 221.6 %all-gather.2.cloned.1.call-start = ((), (), s32[]{:S(2)}) async-start(), calls=%async_computation | async-start | bytes 35651584 | tf_op jit(solution)/shard_map/all_gather | solution.py:66
  24.6 3.2 copy-start
  24.6 3.3 copy-start.1
Sparse Core Ops, SparseCore 0:
  28.0 200.1 all-gather.1
where the time goes:
time: 386 us; the launch traced here: 383 us
  waiting for transfers between devices  128 us (33%)
  local copies, waits for them, and re-layouts  111 us (29%)
  matrix products  79.8 us (21%)
  other arithmetic  28.4 us (7%)
  loops' own time  21.8 us (6%)
  between operations  14 us (4%)
    all_gather x1, waiting for transfers between devices, per_device(): block_piece = lax.all_gather(send_blocks, 'row', axis=0, tiled=True)  128 us
    dot_general x10, matrix products, compute_block(): lax.dot_general(own_rows, column_block, (((1,), (1,)), ((), ())), preferr...  79.8 us
    unnamed x11, local copies, waits for them, and re-layouts  51.7 us
    another operation x1, loops' own time, per_device(): columns = lax.map(single_entry, (block_piece, positions))  21.4 us
    reshape x1, local copies, waits for them, and re-layouts, per_device(): coefficients.reshape(block_local, BLK, aux_count, orbital_count)  16.5 us
    dynamic_update_slice x32, local copies, waits for them, and re-layouts, per_device(): columns = lax.map(single_entry, (block_piece, positions))  14.7 us
    mul x1, other arithmetic, per_device(): coefficients.reshape(block_local, BLK, aux_count, orbital_count)  13.2 us
    select_n x16, other arithmetic, one_column(): weights = jnp.take(own_listed, target, axis=1)  11.3 us
  transfers between devices with their start and end apart: 1, of which 1 were waited for; matrix products, arithmetic and copies ran while one was open for 19% of the time, Pallas kernels for 0%

commit v1 on v0

v1 whole, which is shorter than its diff:
```python
import functools

import jax
import jax.numpy as jnp
import numpy as np
from jax import lax
from jax.experimental import pallas as pl
from jax.experimental.pallas import tpu as pltpu
from jax.sharding import PartitionSpec as P

BLK = 128
NX, NY, NZ, NCORE = 4, 4, 4, 2
NCOL = NZ * NCORE
NDEV = NX * NY * NCOL
LOCAL = 5
ROWS = LOCAL * BLK
NAUX, OCC = 32, 256
NSL = 8
SLW = NAUX * OCC // NSL
AXES = ("row", "col")

PARENT = (None, 0, 0, 1, 0, 1, 2, 3)
EMBED = (
    (3, 7, 8, 4, 8, 4, 8, 4, 8, 4, 0, 11, 0, 7, 0, 3, 3, 11, 3, 11),
    (3, 0, 3, 0, 3, 0, 2, 1, 11, 8, 11, 4, 11, 4, 11, 4, 11, 4, 11, 4),
    (10, 1, 10, 1, 10, 4, 10, 1, 10, 1, 11, 6, 2, 6, 6, 1, 2, 6, 2, 6),
    (2, 1, 7, 8, 2, 1, 2, 1, 7, 8, 6, 5, 6, 5, 6, 5, 6, 5, 6, 0),
)
ORDER = ((0, 1), (1, 1), (0, 2), (0, 3), (1, 2), (1, 3), (0, 4), (0, 5), (0, 6), (0, 7), (1, 4), (1, 5), (1, 6), (1, 7))
GROUPS = ((0, 1), (2, 3), (4,))
REACH = (5, 6, 7)


def dev(x, y, z, core):
    return ((x * NY + y) * NZ + z) * NCORE + core


def embeddings():
    found = []

    def grow(at):
        if len(at) == 8:
            found.append(tuple(at))
            return
        a, y = at[PARENT[len(at)]]
        for nxt in ((1 - a, y), (a, (y + 1) % NY), (a, (y - 1) % NY)):
            if nxt not in at:
                grow(at + [nxt])

    grow([(0, 0)])
    return found


def move(at, by):
    return ((at[0] + by[0]) % 2, (at[1] + by[1]) % NY)


@functools.cache
def plan():
    shapes = embeddings()
    pairs = {(h, e): [] for h in range(2) for e in range(1, 8)}
    where = [dict() for _ in range(NDEV)]
    for z in range(NZ):
        choice = iter(EMBED[z])
        for core in range(NCORE):
            col = z * NCORE + core
            for a in range(2):
                for y in range(NY):
                    if (col - LOCAL * (a * NY + y)) % NCOL >= LOCAL:
                        continue
                    for h in range(2):
                        spots = [move(p, (a, y)) for p in shapes[next(choice)]]
                        for g in range(2):
                            first = LOCAL * ((2 * g + a) * NY + y)
                            block = first + (col - first) % NCOL
                            ids = [dev(2 * g + p[0], p[1], z, core) for p in spots]
                            for e in range(8):
                                where[ids[e]].setdefault(block, [0, 0])[h] = e
                                if e:
                                    pairs[h, e].append((ids[PARENT[e]], ids[e]))
    rows = []
    blocks = []
    for d in range(NDEV):
        blocks.append(sorted(where[d], key=lambda b: (max(where[d][b]), b)))
    for d in range(NDEV):
        row, col = d // NCOL, d % NCOL
        x, y = row // NY, row % NY
        z, core = col // NCORE, col % NCORE
        mate_row = (NX - 1 - x) * NY + y
        mate = mate_row * NCOL + col
        first = LOCAL * row
        j = (col - first) % NCOL
        q = (z % 2) * 2 + core
        order = [q, q + 4, q ^ 2, (q ^ 2) + 4, q ^ 1, (q ^ 1) + 4, q ^ 3, (q ^ 3) + 4]
        mine = blocks[d]
        rows.append(
            [min(j, LOCAL - 1), q, first, LOCAL * mate_row]
            + order
            + [where[d][b][0] for b in mine]
            + [where[d][b][1] for b in mine]
            + [b // NCOL for b in mine]
            + [b // NCOL for b in blocks[mate]]
            + mine
        )
    return pairs, np.asarray(rows, np.int32)


T_SEND, T_Q, T_FIRST, T_MATE, T_ORDER, T_SEL, T_SLOT, T_MSLOT, T_BLOCK = 0, 1, 2, 3, 4, 12, 22, 27, 32


def shifted(dz=0, dcore=0):
    return [
        (dev(x, y, z, k), dev(x, y, (z + dz) % NZ, (k + dcore) % NCORE))
        for x in range(NX)
        for y in range(NY)
        for z in range(NZ)
        for k in range(NCORE)
    ]


def mates():
    return [(dev(x, y, z, k), dev(NX - 1 - x, y, z, k)) for x in range(NX) for y in range(NY) for z in range(NZ) for k in range(NCORE)]


def spread(x_ref, wide):
    for side, ref in enumerate(wide):
        values = x_ref[:, :, side * 128 : (side + 1) * 128]
        ref[...] = values.astype(jnp.float32).reshape(ref.shape)


def pick(wide, p, stride, inside):
    rows = jnp.concatenate([ref[pl.ds(p, BLK, stride=stride), :] for ref in wide], axis=1)
    return jnp.where(inside, rows, 0.0).astype(jnp.bfloat16)


def inside_of(start, end):
    orbital = lax.broadcasted_iota(jnp.int32, (BLK, OCC), 1)
    return (orbital >= start) & (orbital < end)


def send_kernel(tab, start, end, x_ref, out_ref, *wide):
    block = tab[T_FIRST] + tab[T_SEND]
    inside = inside_of(start[block], end[block])
    spread(x_ref, wide)
    for p in range(16):
        out_ref[p // 4, :, (p % 4) * OCC : (p % 4 + 1) * OCC] = pick(wide, p, 16, inside)


def send_half(scalars, coefficients, half):
    return pl.pallas_call(
        send_kernel,
        grid_spec=pltpu.PrefetchScalarGridSpec(
            num_scalar_prefetch=3,
            grid=(1,),
            in_specs=[pl.BlockSpec((BLK, 16, OCC), lambda i, tab, s, e: (tab[T_SEND], half, 0))],
            out_specs=pl.BlockSpec((4, BLK, SLW), lambda i, tab, s, e: (0, 0, 0)),
            scratch_shapes=[pltpu.VMEM((BLK * 16, 128), jnp.float32)] * 2,
        ),
        out_shape=jax.ShapeDtypeStruct((4, BLK, SLW), jnp.bfloat16),
        compiler_params=pltpu.CompilerParams(vmem_limit_bytes=32 << 20),
        cost_estimate=pl.CostEstimate(flops=0, bytes_accessed=4 << 20, transcendentals=0),
        name="send_half",
    )(*scalars, coefficients)


def rows_kernel(tab, start, end, x_ref, out_ref, *wide):
    block = tab[T_FIRST] + pl.program_id(0)
    inside = inside_of(start[block], end[block])
    spread(x_ref, wide)
    for p in range(16):
        out_ref[p // 4, :, (p % 4) * OCC : (p % 4 + 1) * OCC] = pick(wide, p, 16, inside)


def own_rows(scalars, coefficients):
    return pl.pallas_call(
        rows_kernel,
        grid_spec=pltpu.PrefetchScalarGridSpec(
            num_scalar_prefetch=3,
            grid=(LOCAL, 2),
            in_specs=[pl.BlockSpec((BLK, 16, OCC), lambda i, g, tab, s, e: (i, g, 0))],
            out_specs=pl.BlockSpec((4, BLK, SLW), lambda i, g, tab, s, e: (g, i, 0)),
            scratch_shapes=[pltpu.VMEM((BLK * 16, 128), jnp.float32)] * 2,
        ),
        out_shape=jax.ShapeDtypeStruct((NSL, ROWS, SLW), jnp.bfloat16),
        compiler_params=pltpu.CompilerParams(vmem_limit_bytes=32 << 20),
        cost_estimate=pl.CostEstimate(flops=0, bytes_accessed=20 << 20, transcendentals=0),
        name="own_rows",
    )(*scalars, coefficients)


def parts_kernel(tab, start, end, x_ref, low_ref, high_ref, *wide):
    block = tab[T_FIRST] + pl.program_id(0)
    inside = inside_of(start[block], end[block])
    spread(x_ref, wide)
    for m in range(4):
        p = 4 * tab[T_Q] + m
        low_ref[:, m * OCC : (m + 1) * OCC] = pick(wide, p, NAUX, inside)
        high_ref[:, m * OCC : (m + 1) * OCC] = pick(wide, p + 16, NAUX, inside)


def mate_parts(scalars, coefficients):
    part = jax.ShapeDtypeStruct((ROWS, SLW), jnp.bfloat16)
    return pl.pallas_call(
        parts_kernel,
        grid_spec=pltpu.PrefetchScalarGridSpec(
            num_scalar_prefetch=3,
            grid=(LOCAL,),
            in_specs=[pl.BlockSpec((BLK, NAUX, OCC), lambda i, tab, s, e: (i, 0, 0))],
            out_specs=[pl.BlockSpec((BLK, SLW), lambda i, tab, s, e: (i, 0))] * 2,
            scratch_shapes=[pltpu.VMEM((BLK * NAUX, 128), jnp.float32)] * 2,
        ),
        out_shape=[part, part],
        compiler_params=pltpu.CompilerParams(vmem_limit_bytes=32 << 20),
        cost_estimate=pl.CostEstimate(flops=0, bytes_accessed=13 << 20, transcendentals=0),
        name="mate_parts",
    )(*scalars, coefficients)


def product_kernel(positions, nodes, mate, n_left, tab, flags, *refs):
    left = refs[:n_left]
    cand = refs[n_left : n_left + 2 * nodes]
    out_ref, lhs, rhs, acc, left_sem, right_sem = refs[n_left + 2 * nodes :]
    n = len(positions)
    for i, k in enumerate(positions):
        for h in range(2):
            target = rhs.at[pl.ds(4 * h, 4), pl.ds(i * BLK, BLK), :]
            for e in range(nodes):

                @pl.when(tab[T_SEL + 5 * h + k] == e)
                def _(h=h, e=e, target=target, i=i):
                    pltpu.make_async_copy(cand[h * nodes + e], target, right_sem.at[i, h]).start()

    def left_copy(s):
        source = left[s] if n_left == NSL else left[0].at[s]
        return pltpu.make_async_copy(source, lhs.at[s], left_sem.at[s])

    for s in range(NSL):
        left_copy(s).start()
    for i in range(n):
        for h in range(2):
            target = rhs.at[pl.ds(4 * h, 4), pl.ds(i * BLK, BLK), :]
            pltpu.make_async_copy(cand[h * nodes], target, right_sem.at[i, h]).wait()
    for s in range(NSL):
        left_copy(s).wait()
        where = tab[T_ORDER + s] if mate else s
        term = lax.dot_general(lhs[s], rhs[where], (((1,), (1,)), ((), ())), preferred_element_type=jnp.float32)
        if s == 0:
            acc[...] = term
        else:
            acc[...] += term
    base = 25 if mate else 0
    for i, k in enumerate(positions):
        for a in range(LOCAL):
            weight = flags[base + LOCAL * k + a].astype(jnp.float32)
            out_ref[i, a * BLK : (a + 1) * BLK, :] = acc[a * BLK : (a + 1) * BLK, i * BLK : (i + 1) * BLK] * weight


def products(tab, flags, left, cand, positions, mate):
    nodes = len(cand[0])
    n = len(positions)
    anywhere = pl.BlockSpec(memory_space=pl.ANY)
    return pl.pallas_call(
        functools.partial(product_kernel, positions, nodes, mate, len(left)),
        grid_spec=pltpu.PrefetchScalarGridSpec(
            num_scalar_prefetch=2,
            grid=(1,),
            in_specs=[anywhere] * (len(left) + 2 * nodes),
            out_specs=pl.BlockSpec((n, ROWS, BLK), lambda i, tab, flags: (0, 0, 0)),
            scratch_shapes=[
                pltpu.VMEM((NSL, ROWS, SLW), jnp.bfloat16),
                pltpu.VMEM((NSL, n * BLK, SLW), jnp.bfloat16),
                pltpu.VMEM((ROWS, n * BLK), jnp.float32),
                pltpu.SemaphoreType.DMA((NSL,)),
                pltpu.SemaphoreType.DMA((n, 2)),
            ],
        ),
        out_shape=jax.ShapeDtypeStruct((n, ROWS, BLK), jnp.float32),
        compiler_params=pltpu.CompilerParams(vmem_limit_bytes=40 << 20),
        cost_estimate=pl.CostEstimate(
            flops=2 * ROWS * n * BLK * NSL * SLW, bytes_accessed=(10 + 2 * n) << 20, transcendentals=0
        ),
        name="products",
    )(tab, flags, *left, *cand[0], *cand[1])


def place_kernel(tab, *refs):
    *parts, out_ref = refs
    half = len(parts) // 2
    for side in range(2):
        base = T_MSLOT if side else T_SLOT
        for ref, positions in zip(parts[side * half : (side + 1) * half], GROUPS):
            for i, k in enumerate(positions):
                out_ref[pl.ds(tab[base + k], BLK, stride=10), :] = ref[i]


def place(tab, own, got):
    specs = [pl.BlockSpec((len(g), BLK, BLK), lambda i, tab: (0, i, 0)) for g in GROUPS]
    return pl.pallas_call(
        place_kernel,
        grid_spec=pltpu.PrefetchScalarGridSpec(
            num_scalar_prefetch=1,
            grid=(LOCAL,),
            in_specs=specs + specs,
            out_specs=pl.BlockSpec((BLK * 10, BLK), lambda i, tab: (i, 0)),
        ),
        out_shape=jax.ShapeDtypeStruct((ROWS * 10, BLK), jnp.float32),
        cost_estimate=pl.CostEstimate(flops=0, bytes_accessed=7 << 20, transcendentals=0),
        name="place",
    )(tab, *own, *got)


def listed_flags(pair_list, tab):
    first = jnp.min(pair_list, axis=1)
    second = jnp.max(pair_list, axis=1)
    codes = first * 256 + second
    heads = jnp.stack([tab[T_FIRST], tab[T_MATE]])
    a = heads[:, None, None] + jnp.arange(LOCAL, dtype=jnp.int32)[None, None, :]
    b = tab[T_BLOCK : T_BLOCK + 5][None, :, None]
    wanted = (jnp.minimum(a, b) * 256 + jnp.maximum(a, b)).reshape(-1)
    return jnp.any(codes[None, :] == wanted[:, None], axis=1).astype(jnp.int32)


def per_device(coefficients, range_start, range_end, pair_list):
    pairs, table = plan()
    here = lax.axis_index("row") * NCOL + lax.axis_index("col")
    tab = lax.dynamic_index_in_dim(jnp.asarray(table), here, 0, keepdims=False)
    scalars = (tab, range_start, range_end)

    roots = [send_half(scalars, coefficients, h) for h in range(2)]
    low, high = mate_parts(scalars, coefficients)
    held = {(h, 0): roots[h] for h in range(2)}
    for h, e in ORDER:
        held[h, e] = lax.ppermute(held[h, PARENT[e]], AXES, pairs[h, e])
    far = [lax.ppermute(v, AXES, mates()) for v in (low, high)]
    far += [lax.ppermute(far[0], AXES, shifted(dz=-1)), lax.ppermute(far[1], AXES, shifted(dz=1))]
    far += [lax.ppermute(v, AXES, shifted(dcore=1)) for v in far]

    flags = listed_flags(pair_list, tab)
    rows = own_rows(scalars, coefficients)
    own, got = [], []
    for positions, last in zip(GROUPS, REACH):
        cand = [[held[h, e] for e in range(last + 1)] for h in range(2)]
        sent = products(tab, flags, far, cand, positions, True)
        got.append(lax.ppermute(sent, AXES, mates()))
        own.append(products(tab, flags, [rows], cand, positions, False))
    return place(tab, own, got).reshape(ROWS, 10, 1, BLK)


def solution(mesh):
    in_specs = (P("row", None, None), P(), P(), P())
    out_specs = P("row", None, "col", None)
    return jax.shard_map(per_device, mesh=mesh, in_specs=in_specs, out_specs=out_specs, check_vma=False)
```

time: 386 us -> 224 us (0.58)
  waiting for transfers between devices: 128 us -> 38.7 us
  Pallas kernels: 0 us -> 86.1 us
  matrix products: 79.8 us -> 0 us
  local copies, waits for them, and re-layouts: 111 us -> 32.1 us
  starting transfers between devices: 0.01 us -> 62 us
  other arithmetic: 28.4 us -> 1.78 us
  loops' own time: 21.8 us -> 0 us
  between operations: 14 us -> 0.42 us
    all_gather x1 -> x0, waiting for transfers between devices: 128 us -> none  [per_device(): block_piece = lax.all_gather(send_blocks, 'row', axis=0, tiled=True)]
    pallas_call x0 -> x11, Pallas kernels: none -> 86.1 us  [the longest x6 55.6 us: products(): pl.pallas_call(functools.partial(product_kernel, positions, nodes, mate,...]
    dot_general x10 -> x0, matrix products: 79.8 us -> none  [compute_block(): lax.dot_general(own_rows, column_block, (((1,), (1,)), ((), ())), preferr...]
    ppermute x0 -> x25, starting transfers between devices: none -> 62 us  [the longest x14 29.7 us: per_device(): held[h, e] = lax.ppermute(held[h, PARENT[e]], AXES, pairs[h, e])]
    ppermute x0 -> x25, waiting for transfers between devices: none -> 38.7 us  [the longest x14 23.6 us: per_device(): held[h, e] = lax.ppermute(held[h, PARENT[e]], AXES, pairs[h, e])]
    another operation x17 -> x0, loops' own time: 21.8 us -> none  [the longest x1 21.4 us: per_device(): columns = lax.map(single_entry, (block_piece, positions))]
    reshape x2 -> x0, local copies, waits for them, and re-layouts: 21.6 us -> none  [the longest x1 16.5 us: per_device(): coefficients.reshape(block_local, BLK, aux_count, orbital_count)]
    unnamed x11 -> x70, local copies, waits for them, and re-layouts: 51.7 us -> 30.6 us
  transfers between devices with their start and end apart: 1 -> 25, of which waited for: 1 -> 6; matrix products, arithmetic and copies ran while one was open for 19% -> 1% of each run, Pallas kernels for 0% -> 36%
where the time goes in v1:
time: 224 us; the launch traced here: 221 us
  Pallas kernels  86.1 us (38%)
  starting transfers between devices  62 us (28%)
  waiting for transfers between devices  38.7 us (17%)
  local copies, waits for them, and re-layouts  32.1 us (14%)
    pallas_call x6, Pallas kernels, products(): pl.pallas_call(functools.partial(product_kernel, positions, nodes, mate,...  55.6 us
    unnamed x70, local copies, waits for them, and re-layouts  30.6 us
    ppermute x14, starting transfers between devices, per_device(): held[h, e] = lax.ppermute(held[h, PARENT[e]], AXES, pairs[h, e])  29.7 us
    ppermute x14, waiting for transfers between devices, per_device(): held[h, e] = lax.ppermute(held[h, PARENT[e]], AXES, pairs[h, e])  23.6 us
    pallas_call x1, Pallas kernels, own_rows(): pl.pallas_call(rows_kernel, grid_spec=pltpu.PrefetchScalarGridSpec(num_sc...  13.8 us
    ppermute x1, starting transfers between devices, per_device(): lax.ppermute(far[0], AXES, shifted(dz=-1))  10.7 us
    ppermute x2, waiting for transfers between devices, per_device(): far = [lax.ppermute(v, AXES, mates()) for v in (low, high)]  9.9 us
    ppermute x1, starting transfers between devices, per_device(): lax.ppermute(far[1], AXES, shifted(dz=1))  8.38 us
  transfers between devices with their start and end apart: 25, of which 6 were waited for; matrix products, arithmetic and copies ran while one was open for 1% of the time, Pallas kernels for 36%

profile of v1, /device:TPU:1, one launch (start us, length us, event | category | flops | bytes accessed | tf_op | source)
XLA Modules:
  0.0 221.1 jit_solution(14675026790805049304)
XLA Ops:
  0.7 4.0 %copy-done = bf16[640,32,256]{2,1,0:T(8,128)(2,1)S(1)} copy-done((bf16[640,32,256]{2,1,0:T(8,128)(2,1)S(1)}, bf16[640,32,256]{2,1,0:T(8,128)(2,1)}, u32[]{:S(2)}) %copy-start) | copy-done | bytes 10485784
  7.8 5.5 %collective-permute-start.3 = (bf16[4,128,1024]{2,1,0:T(8,128)(2,1)S(1)}, bf16[4,128,1024]{2,1,0:T(8,128)(2,1)S(1)}, u32[]{:S(2)}, u32[]{:S(2)}) collective-permute-start(bf16[4,128,1024]{2,1,0:T(8,128)(2,1)S(1)} %send_half.2.refs_1_.refs_8_), channel_id=1, source_target_pairs={{0,8},{64,72},{8,16},{72,80},{24,0},{88,64},{32,40},{96,104},{48,5... | collective-permute-start | bytes 3145736 | tf_op jit(solution)/shard_map/ppermute | solution.py:333
  20.3 7.4 %mate_parts.1 = (bf16[640,1024]{1,0:T(8,128)(2,1)S(1)}, bf16[640,1024]{1,0:T(8,128)(2,1)S(1)}) custom-call(s32[37]{0:T(128)S(1)} %get-tuple-element.12.tab, s32[80]{0:T(128)S(1)} %copy-done.27, s32[80]{0:T(128)S(1)} %copy-done.29, bf16[640,32,256]{2,1,0:T(8,128)(2,1)S(1)} %copy-done), custom_call_target="tpu_custom_call" | custom-call | bytes 13631488 | tf_op jit(solution)/shard_map/mate_parts/pallas_call | solution.py:203
  27.8 5.1 %collective-permute-done.3.refs_5_.refs_12_ = bf16[4,128,1024]{2,1,0:T(8,128)(2,1)S(1)} collective-permute-done((bf16[4,128,1024]{2,1,0:T(8,128)(2,1)S(1)}, bf16[4,128,1024]{2,1,0:T(8,128)(2,1)S(1)}, u32[]{:S(2)}, u32[]{:S(2)}) %collective-permute-start.3) | collective-permute-done | bytes 1048608 | tf_op jit(solution)/shard_map/ppermute | solution.py:333
  34.8 3.1 %collective-permute-done.1.refs_3_.refs_10_ = bf16[4,128,1024]{2,1,0:T(8,128)(2,1)} collective-permute-done((bf16[4,128,1024]{2,1,0:T(8,128)(2,1)S(1)}, bf16[4,128,1024]{2,1,0:T(8,128)(2,1)}, u32[]{:S(2)}, u32[]{:S(2)}) %collective-permute-start.1) | collective-permute-done | bytes 1048608 | tf_op jit(solution)/shard_map/ppermute | solution.py:333
  38.0 5.2 %collective-permute-start.5 = (bf16[4,128,1024]{2,1,0:T(8,128)(2,1)S(1)}, bf16[4,128,1024]{2,1,0:T(8,128)(2,1)S(1)}, u32[]{:S(2)}, u32[]{:S(2)}) collective-permute-start(bf16[4,128,1024]{2,1,0:T(8,128)(2,1)S(1)} %send_half.3.refs_7_.refs_8_.refs_9_.refs_14_.refs_15_.refs_16_), channel_id=1, source_target_pairs={{0,8},{64,72},{8,16},{72,80},{24,0},{88,64},{32,40},{96,104},{48,5... | collective-permute-start | bytes 3145736 | tf_op jit(solution)/shard_map/ppermute | solution.py:333
  43.2 15.3 %collective-permute-done.8.refs_11_.refs_12_.refs_13_.refs_18_.refs_19_.refs_20_ = bf16[4,128,1024]{2,1,0:T(8,128)(2,1)S(1)} collective-permute-done((bf16[4,128,1024]{2,1,0:T(8,128)(2,1)S(1)}, bf16[4,128,1024]{2,1,0:T(8,128)(2,1)S(1)}, u32[]{:S(2)}, u32[]{:S(2)}) %collective-permute-start.8) | collective-permute-done | bytes 1048608 | tf_op jit(solution)/shard_map/ppermute | solution.py:333
  62.6 10.7 %collective-permute-start.16 = (bf16[640,1024]{1,0:T(8,128)(2,1)S(1)}, bf16[640,1024]{1,0:T(8,128)(2,1)}, u32[]{:S(2)}, u32[]{:S(2)}) collective-permute-start(bf16[640,1024]{1,0:T(8,128)(2,1)S(1)} %collective-permute-done.14.refs_0_), channel_id=1, source_target_pairs={{0,6},{1,7},{2,0},{3,1},{4,2},{5,3},{6,4},{7,5},{8,14},{9,15},{10,... | collective-permute-start | bytes 3932168 | tf_op jit(solution)/shard_map/ppermute | solution.py:335
  74.5 9.9 %collective-permute-done.15.refs_1_ = bf16[640,1024]{1,0:T(8,128)(2,1)} collective-permute-done((bf16[640,1024]{1,0:T(8,128)(2,1)S(1)}, bf16[640,1024]{1,0:T(8,128)(2,1)}, u32[]{:S(2)}, u32[]{:S(2)}) %collective-permute-start.15) | collective-permute-done | bytes 1310752 | tf_op jit(solution)/shard_map/ppermute | solution.py:334
  84.4 8.4 %collective-permute-start.17 = (bf16[640,1024]{1,0:T(8,128)(2,1)}, bf16[640,1024]{1,0:T(8,128)(2,1)}, u32[]{:S(2)}, u32[]{:S(2)}) collective-permute-start(bf16[640,1024]{1,0:T(8,128)(2,1)} %collective-permute-done.15.refs_1_), channel_id=1, source_target_pairs={{0,2},{1,3},{2,4},{3,5},{4,6},{5,7},{6,0},{7,1},{8,10},{9,11},{10,... | collective-permute-start | bytes 3932168 | tf_op jit(solution)/shard_map/ppermute | solution.py:335
  99.6 13.8 %own_rows.1.refs_0_ = bf16[8,640,1024]{2,1,0:T(8,128)(2,1)S(1)} custom-call(s32[37]{0:T(128)S(1)} %get-tuple-element.12.tab, s32[80]{0:T(128)S(1)} %copy-done.27, s32[80]{0:T(128)S(1)} %copy-done.29, bf16[640,32,256]{2,1,0:T(8,128)(2,1)S(1)} %copy-done), custom_call_target="tpu_custom_call" | custom-call | bytes 20971520 | tf_op jit(solution)/shard_map/own_rows/pallas_call | solution.py:175
  113.4 4.0 %copy-done.1 = bf16[8,640,1024]{2,1,0:T(8,128)(2,1)} copy-done((bf16[8,640,1024]{2,1,0:T(8,128)(2,1)}, bf16[8,640,1024]{2,1,0:T(8,128)(2,1)S(1)}, u32[]{:S(2)}) %copy-start.1) | copy-done | bytes 10485784
  117.4 3.9 %collective-permute-done.17.refs_3_ = bf16[640,1024]{1,0:T(8,128)(2,1)} collective-permute-done((bf16[640,1024]{1,0:T(8,128)(2,1)}, bf16[640,1024]{1,0:T(8,128)(2,1)}, u32[]{:S(2)}, u32[]{:S(2)}) %collective-permute-start.17) | collective-permute-done | bytes 1310752 | tf_op jit(solution)/shard_map/ppermute | solution.py:335
  121.4 3.0 %collective-permute-start.21 = (bf16[640,1024]{1,0:T(8,128)(2,1)}, bf16[640,1024]{1,0:T(8,128)(2,1)}, u32[]{:S(2)}, u32[]{:S(2)}) collective-permute-start(bf16[640,1024]{1,0:T(8,128)(2,1)} %collective-permute-done.17.refs_3_), channel_id=1, source_target_pairs={{0,1},{1,0},{2,3},{3,2},{4,5},{5,4},{6,7},{7,6},{8,9},{9,8},{10,11... | collective-permute-start | bytes 3932168 | tf_op jit(solution)/shard_map/ppermute | solution.py:336
  130.7 2.4 %collective-permute-start.11 = (bf16[4,128,1024]{2,1,0:T(8,128)(2,1)}, bf16[4,128,1024]{2,1,0:T(8,128)(2,1)}, u32[]{:S(2)}, u32[]{:S(2)}) collective-permute-start(bf16[4,128,1024]{2,1,0:T(8,128)(2,1)} %collective-permute-done.6.refs_9_.refs_10_.refs_11_.refs_16_.refs_17_.refs_18_), channel_id=1, source_target_pairs={{24,56},{88,120},{40,32},{104,96},{56,48},{120,112},{0,24},{64,88}... | collective-permute-start | bytes 3145736 | tf_op jit(solution)/shard_map/ppermute | solution.py:333
  146.9 8.4 %products.9 = f32[2,640,128]{2,1,0:T(8,128)S(1)} custom-call(s32[37]{0:T(128)S(1)} %get-tuple-element.12.tab, s32[50]{0:T(128)S(1)} %convert_element_type.3.flags, bf16[640,1024]{1,0:T(8,128)(2,1)S(1)} %copy-done.21, bf16[640,1024]{1,0:T(8,128)(2,1)} %collective-permute-done.15.refs_1_, bf16[640,1024]{1,0:T(8,128)(2,1)} %collective-permute-done.16.refs_2_, ...), custom_call_target="tpu_custom_call" | custom-call | flops 2684354560 | bytes 14680064 | tf_op jit(solution)/shard_map/products/pallas_call | solution.py:262
  155.3 4.8 %collective-permute-start.22 = (f32[2,640,128]{2,1,0:T(8,128)S(1)}, f32[2,640,128]{2,1,0:T(8,128)S(1)}, u32[]{:S(2)}, u32[]{:S(2)}) collective-permute-start(f32[2,640,128]{2,1,0:T(8,128)S(1)} %products.9), channel_id=1, source_target_pairs={{0,96},{1,97},{2,98},{3,99},{4,100},{5,101},{6,102},{7,103},{8,104... | collective-permute-start | bytes 1966088 | tf_op jit(solution)/shard_map/ppermute | solution.py:344
  160.1 8.6 %products.10 = f32[2,640,128]{2,1,0:T(8,128)S(1)} custom-call(s32[37]{0:T(128)S(1)} %get-tuple-element.12.tab, s32[50]{0:T(128)S(1)} %convert_element_type.3.flags, bf16[640,1024]{1,0:T(8,128)(2,1)} %copy-done.20, bf16[640,1024]{1,0:T(8,128)(2,1)} %collective-permute-done.15.refs_1_, bf16[640,1024]{1,0:T(8,128)(2,1)} %collective-permute-done.16.refs_2_, ...), custom_call_target="tpu_custom_call" | custom-call | flops 2684354560 | bytes 14680064 | tf_op jit(solution)/shard_map/products/pallas_call | solution.py:262
  168.7 2.6 %collective-permute-start.23 = (f32[2,640,128]{2,1,0:T(8,128)S(1)}, f32[2,640,128]{2,1,0:T(8,128)}, u32[]{:S(2)}, u32[]{:S(2)}) collective-permute-start(f32[2,640,128]{2,1,0:T(8,128)S(1)} %products.10), channel_id=1, source_target_pairs={{0,96},{1,97},{2,98},{3,99},{4,100},{5,101},{6,102},{7,103},{8,104... | collective-permute-start | bytes 1966088 | tf_op jit(solution)/shard_map/ppermute | solution.py:344
  171.4 8.6 %products.7.refs_1_ = f32[2,640,128]{2,1,0:T(8,128)S(1)} custom-call(s32[37]{0:T(128)S(1)} %get-tuple-element.12.tab, s32[50]{0:T(128)S(1)} %convert_element_type.3.flags, bf16[8,640,1024]{2,1,0:T(8,128)(2,1)} %copy-done.1, bf16[4,128,1024]{2,1,0:T(8,128)(2,1)S(1)} %send_half.2.refs_1_.refs_8_, bf16[4,128,1024]{2,1,0:T(8,128)(2,1)S(1)} %copy-done.3, ...), custom_call_target="tpu_custom_call" | custom-call | flops 2684354560 | bytes 14680064 | tf_op jit(solution)/shard_map/products/pallas_call | solution.py:262
  181.8 10.5 %products.11 = f32[1,640,128]{2,1,0:T(8,128)S(1)} custom-call(s32[37]{0:T(128)S(1)} %get-tuple-element.12.tab, s32[50]{0:T(128)S(1)} %convert_element_type.3.flags, bf16[640,1024]{1,0:T(8,128)(2,1)} %copy-done.20, bf16[640,1024]{1,0:T(8,128)(2,1)} %collective-permute-done.15.refs_1_, bf16[640,1024]{1,0:T(8,128)(2,1)} %collective-permute-done.16.refs_2_, ...), custom_call_target="tpu_custom_call" | custom-call | flops 1342177280 | bytes 12582912 | tf_op jit(solution)/shard_map/products/pallas_call | solution.py:262
  193.3 8.8 %products.6.refs_0_ = f32[2,640,128]{2,1,0:T(8,128)S(1)} custom-call(s32[37]{0:T(128)S(1)} %get-tuple-element.12.tab, s32[50]{0:T(128)S(1)} %convert_element_type.3.flags, bf16[8,640,1024]{2,1,0:T(8,128)(2,1)} %copy-done.1, bf16[4,128,1024]{2,1,0:T(8,128)(2,1)S(1)} %send_half.2.refs_1_.refs_8_, bf16[4,128,1024]{2,1,0:T(8,128)(2,1)S(1)} %copy-done.3, ...), custom_call_target="tpu_custom_call" | custom-call | flops 2684354560 | bytes 14680064 | tf_op jit(solution)/shard_map/products/pallas_call | solution.py:262
  203.0 10.6 %products.8.refs_2_ = f32[1,640,128]{2,1,0:T(8,128)S(1)} custom-call(s32[37]{0:T(128)S(1)} %get-tuple-element.12.tab, s32[50]{0:T(128)S(1)} %convert_element_type.3.flags, bf16[8,640,1024]{2,1,0:T(8,128)(2,1)} %copy-done.1, bf16[4,128,1024]{2,1,0:T(8,128)(2,1)S(1)} %send_half.2.refs_1_.refs_8_, bf16[4,128,1024]{2,1,0:T(8,128)(2,1)S(1)} %copy-done.3, ...), custom_call_target="tpu_custom_call" | custom-call | flops 1342177280 | bytes 12582912 | tf_op jit(solution)/shard_map/products/pallas_call | solution.py:262
  215.3 5.8 %place.1 = f32[6400,128]{1,0:T(8,128)} custom-call(s32[37]{0:T(128)} %copy-done.25, f32[2,640,128]{2,1,0:T(8,128)} %copy-done.23, f32[2,640,128]{2,1,0:T(8,128)} %copy-done.22, f32[1,640,128]{2,1,0:T(8,128)} %copy-done.24, f32[2,640,128]{2,1,0:T(8,128)} %copy-done.32, f32[2,640,128]{2,1,0:T(8,128)} %collective-permute-done.23.refs_4_, f32[1,640,128]{2,1,0:T(8,128)} %copy-done.33), custom_call_target="tpu_custom_call" | custom-call | bytes 7340032 | tf_op jit(solution)/shard_map/place/pallas_call | solution.py:298
  (118 shorter events, 50.2 us)
Async XLA Ops:
  7.8 25.1 %collective-permute-start.3 = (bf16[4,128,1024]{2,1,0:T(8,128)(2,1)S(1)}, bf16[4,128,1024]{2,1,0:T(8,128)(2,1)S(1)}, u32[]{:S(2)}, u32[]{:S(2)}) collective-permute-start(bf16[4,128,1024]{2,1,0:T(8,128)(2,1)S(1)} %send_half.2.refs_1_.refs_8_), channel_id=1, source_target_pairs={{0,8},{64,72},{8,16},{72,80},{24,0},{88,64},{32,40},{96,104},{48,5... | collective-permute-start | bytes 3145736 | tf_op jit(solution)/shard_map/ppermute | solution.py:333
  13.3 24.7 %collective-permute-start.1 = (bf16[4,128,1024]{2,1,0:T(8,128)(2,1)S(1)}, bf16[4,128,1024]{2,1,0:T(8,128)(2,1)}, u32[]{:S(2)}, u32[]{:S(2)}) collective-permute-start(bf16[4,128,1024]{2,1,0:T(8,128)(2,1)S(1)} %send_half.2.refs_1_.refs_8_), channel_id=1, source_target_pairs={{0,24},{64,88},{8,40},{72,104},{24,56},{88,120},{32,0},{96,64},{48... | collective-permute-start | bytes 3145736 | tf_op jit(solution)/shard_map/ppermute | solution.py:333
  15.2 22.8 %collective-permute-start = (bf16[4,128,1024]{2,1,0:T(8,128)(2,1)S(1)}, bf16[4,128,1024]{2,1,0:T(8,128)(2,1)S(1)}, u32[]{:S(2)}, u32[]{:S(2)}) collective-permute-start(bf16[4,128,1024]{2,1,0:T(8,128)(2,1)S(1)} %send_half.2.refs_1_.refs_8_), channel_id=1, source_target_pairs={{0,32},{64,96},{8,0},{72,64},{24,16},{88,80},{32,56},{96,120},{48,... | collective-permute-start | bytes 3145736 | tf_op jit(solution)/shard_map/ppermute | solution.py:333
  18.4 40.1 %collective-permute-start.8 = (bf16[4,128,1024]{2,1,0:T(8,128)(2,1)S(1)}, bf16[4,128,1024]{2,1,0:T(8,128)(2,1)S(1)}, u32[]{:S(2)}, u32[]{:S(2)}) collective-permute-start(bf16[4,128,1024]{2,1,0:T(8,128)(2,1)S(1)} %send_half.3.refs_7_.refs_8_.refs_9_.refs_14_.refs_15_.refs_16_), channel_id=1, source_target_pairs={{0,32},{64,96},{8,0},{72,64},{24,16},{88,80},{32,56},{96,120},{48,... | collective-permute-start | bytes 3145736 | tf_op jit(solution)/shard_map/ppermute | solution.py:333
  27.7 34.8 %collective-permute-start.14 = (bf16[640,1024]{1,0:T(8,128)(2,1)S(1)}, bf16[640,1024]{1,0:T(8,128)(2,1)S(1)}, u32[]{:S(2)}, u32[]{:S(2)}) collective-permute-start(bf16[640,1024]{1,0:T(8,128)(2,1)S(1)} %get-tuple-element.7), channel_id=1, source_target_pairs={{0,96},{1,97},{2,98},{3,99},{4,100},{5,101},{6,102},{7,103},{8,104... | collective-permute-start | bytes 3932168 | tf_op jit(solution)/shard_map/ppermute | solution.py:334
  32.9 27.4 %collective-permute-start.6 = (bf16[4,128,1024]{2,1,0:T(8,128)(2,1)S(1)}, bf16[4,128,1024]{2,1,0:T(8,128)(2,1)}, u32[]{:S(2)}, u32[]{:S(2)}) collective-permute-start(bf16[4,128,1024]{2,1,0:T(8,128)(2,1)S(1)} %send_half.3.refs_7_.refs_8_.refs_9_.refs_14_.refs_15_.refs_16_), channel_id=1, source_target_pairs={{0,24},{64,88},{8,40},{72,104},{24,56},{88,120},{32,0},{96,64},{48... | collective-permute-start | bytes 3145736 | tf_op jit(solution)/shard_map/ppermute | solution.py:333
  38.0 46.5 %collective-permute-start.15 = (bf16[640,1024]{1,0:T(8,128)(2,1)S(1)}, bf16[640,1024]{1,0:T(8,128)(2,1)}, u32[]{:S(2)}, u32[]{:S(2)}) collective-permute-start(bf16[640,1024]{1,0:T(8,128)(2,1)S(1)} %get-tuple-element.8), channel_id=1, source_target_pairs={{0,96},{1,97},{2,98},{3,99},{4,100},{5,101},{6,102},{7,103},{8,104... | collective-permute-start | bytes 3932168 | tf_op jit(solution)/shard_map/ppermute | solution.py:334
  38.0 35.3 %collective-permute-start.5 = (bf16[4,128,1024]{2,1,0:T(8,128)(2,1)S(1)}, bf16[4,128,1024]{2,1,0:T(8,128)(2,1)S(1)}, u32[]{:S(2)}, u32[]{:S(2)}) collective-permute-start(bf16[4,128,1024]{2,1,0:T(8,128)(2,1)S(1)} %send_half.3.refs_7_.refs_8_.refs_9_.refs_14_.refs_15_.refs_16_), channel_id=1, source_target_pairs={{0,8},{64,72},{8,16},{72,80},{24,0},{88,64},{32,40},{96,104},{48,5... | collective-permute-start | bytes 3145736 | tf_op jit(solution)/shard_map/ppermute | solution.py:333
  59.6 33.3 %collective-permute-start.4 = (bf16[4,128,1024]{2,1,0:T(8,128)(2,1)S(1)}, bf16[4,128,1024]{2,1,0:T(8,128)(2,1)S(1)}, u32[]{:S(2)}, u32[]{:S(2)}) collective-permute-start(bf16[4,128,1024]{2,1,0:T(8,128)(2,1)S(1)} %collective-permute-done.refs_2_.refs_9_), channel_id=1, source_target_pairs={{32,40},{96,104},{0,24},{64,88},{16,8},{80,72},{56,48},{120,112},{... | collective-permute-start | bytes 3145736 | tf_op jit(solution)/shard_map/ppermute | solution.py:333
  60.3 34.8 %collective-permute-start.2 = (bf16[4,128,1024]{2,1,0:T(8,128)(2,1)S(1)}, bf16[4,128,1024]{2,1,0:T(8,128)(2,1)S(1)}, u32[]{:S(2)}, u32[]{:S(2)}) collective-permute-start(bf16[4,128,1024]{2,1,0:T(8,128)(2,1)S(1)} %collective-permute-done.refs_2_.refs_9_), channel_id=1, source_target_pairs={{32,56},{96,120},{0,32},{64,96},{16,48},{80,112},{56,24},{120,88},... | collective-permute-start | bytes 3145736 | tf_op jit(solution)/shard_map/ppermute | solution.py:333
  62.6 37.1 %collective-permute-start.16 = (bf16[640,1024]{1,0:T(8,128)(2,1)S(1)}, bf16[640,1024]{1,0:T(8,128)(2,1)}, u32[]{:S(2)}, u32[]{:S(2)}) collective-permute-start(bf16[640,1024]{1,0:T(8,128)(2,1)S(1)} %collective-permute-done.14.refs_0_), channel_id=1, source_target_pairs={{0,6},{1,7},{2,0},{3,1},{4,2},{5,3},{6,4},{7,5},{8,14},{9,15},{10,... | collective-permute-start | bytes 3932168 | tf_op jit(solution)/shard_map/ppermute | solution.py:335
  73.2 22.6 %collective-permute-start.9 = (bf16[4,128,1024]{2,1,0:T(8,128)(2,1)S(1)}, bf16[4,128,1024]{2,1,0:T(8,128)(2,1)S(1)}, u32[]{:S(2)}, u32[]{:S(2)}) collective-permute-start(bf16[4,128,1024]{2,1,0:T(8,128)(2,1)S(1)} %collective-permute-done.5.refs_8_.refs_9_.refs_10_.refs_15_.refs_16_.refs_17_), channel_id=1, source_target_pairs={{8,40},{72,104},{16,24},{80,88},{0,8},{64,72},{40,48},{104,112},{5... | collective-permute-start | bytes 3145736 | tf_op jit(solution)/shard_map/ppermute | solution.py:333
  84.4 36.9 %collective-permute-start.17 = (bf16[640,1024]{1,0:T(8,128)(2,1)}, bf16[640,1024]{1,0:T(8,128)(2,1)}, u32[]{:S(2)}, u32[]{:S(2)}) collective-permute-start(bf16[640,1024]{1,0:T(8,128)(2,1)} %collective-permute-done.15.refs_1_), channel_id=1, source_target_pairs={{0,2},{1,3},{2,4},{3,5},{4,6},{5,7},{6,0},{7,1},{8,10},{9,11},{10,... | collective-permute-start | bytes 3932168 | tf_op jit(solution)/shard_map/ppermute | solution.py:335
  93.8 35.9 %collective-permute-start.18 = (bf16[640,1024]{1,0:T(8,128)(2,1)S(1)}, bf16[640,1024]{1,0:T(8,128)(2,1)S(1)}, u32[]{:S(2)}, u32[]{:S(2)}) collective-permute-start(bf16[640,1024]{1,0:T(8,128)(2,1)S(1)} %collective-permute-done.14.refs_0_), channel_id=1, source_target_pairs={{0,1},{1,0},{2,3},{3,2},{4,5},{5,4},{6,7},{7,6},{8,9},{9,8},{10,11... | collective-permute-start | bytes 3932168 | tf_op jit(solution)/shard_map/ppermute | solution.py:336
  95.1 31.3 %collective-permute-start.7 = (bf16[4,128,1024]{2,1,0:T(8,128)(2,1)S(1)}, bf16[4,128,1024]{2,1,0:T(8,128)(2,1)S(1)}, u32[]{:S(2)}, u32[]{:S(2)}) collective-permute-start(bf16[4,128,1024]{2,1,0:T(8,128)(2,1)S(1)} %collective-permute-done.5.refs_8_.refs_9_.refs_10_.refs_15_.refs_16_.refs_17_), channel_id=1, source_target_pairs={{8,16},{72,80},{16,48},{80,112},{0,32},{64,96},{40,8},{104,72},{56... | collective-permute-start | bytes 3145736 | tf_op jit(solution)/shard_map/ppermute | solution.py:333
  96.8 36.6 %collective-permute-start.19 = (bf16[640,1024]{1,0:T(8,128)(2,1)}, bf16[640,1024]{1,0:T(8,128)(2,1)}, u32[]{:S(2)}, u32[]{:S(2)}) collective-permute-start(bf16[640,1024]{1,0:T(8,128)(2,1)} %collective-permute-done.15.refs_1_), channel_id=1, source_target_pairs={{0,1},{1,0},{2,3},{3,2},{4,5},{5,4},{6,7},{7,6},{8,9},{9,8},{10,11... | collective-permute-start | bytes 3932168 | tf_op jit(solution)/shard_map/ppermute | solution.py:336
  99.6 35.8 %collective-permute-start.20 = (bf16[640,1024]{1,0:T(8,128)(2,1)}, bf16[640,1024]{1,0:T(8,128)(2,1)}, u32[]{:S(2)}, u32[]{:S(2)}) collective-permute-start(bf16[640,1024]{1,0:T(8,128)(2,1)} %collective-permute-done.16.refs_2_), channel_id=1, source_target_pairs={{0,1},{1,0},{2,3},{3,2},{4,5},{5,4},{6,7},{7,6},{8,9},{9,8},{10,11... | collective-permute-start | bytes 3932168 | tf_op jit(solution)/shard_map/ppermute | solution.py:336
  127.4 32.7 %collective-permute-start.10 = (bf16[4,128,1024]{2,1,0:T(8,128)(2,1)}, bf16[4,128,1024]{2,1,0:T(8,128)(2,1)}, u32[]{:S(2)}, u32[]{:S(2)}) collective-permute-start(bf16[4,128,1024]{2,1,0:T(8,128)(2,1)} %collective-permute-done.1.refs_3_.refs_10_), channel_id=1, source_target_pairs={{24,16},{88,80},{40,48},{104,112},{56,32},{120,96},{0,8},{64,72},{... | collective-permute-start | bytes 3145736 | tf_op jit(solution)/shard_map/ppermute | solution.py:333
  130.7 29.3 %collective-permute-start.11 = (bf16[4,128,1024]{2,1,0:T(8,128)(2,1)}, bf16[4,128,1024]{2,1,0:T(8,128)(2,1)}, u32[]{:S(2)}, u32[]{:S(2)}) collective-permute-start(bf16[4,128,1024]{2,1,0:T(8,128)(2,1)} %collective-permute-done.6.refs_9_.refs_10_.refs_11_.refs_16_.refs_17_.refs_18_), channel_id=1, source_target_pairs={{24,56},{88,120},{40,32},{104,96},{56,48},{120,112},{0,24},{64,88}... | collective-permute-start | bytes 3145736 | tf_op jit(solution)/shard_map/ppermute | solution.py:333
  133.5 47.3 %collective-permute-start.12 = (bf16[4,128,1024]{2,1,0:T(8,128)(2,1)}, bf16[4,128,1024]{2,1,0:T(8,128)(2,1)S(1)}, u32[]{:S(2)}, u32[]{:S(2)}) collective-permute-start(bf16[4,128,1024]{2,1,0:T(8,128)(2,1)} %copy-done.10), channel_id=1, source_target_pairs={{56,48},{120,112},{32,56},{96,120},{48,40},{112,104},{24,16},{88,8... | collective-permute-start | bytes 3145736 | tf_op jit(solution)/shard_map/ppermute | solution.py:333
  135.4 45.4 %collective-permute-start.13 = (bf16[4,128,1024]{2,1,0:T(8,128)(2,1)}, bf16[4,128,1024]{2,1,0:T(8,128)(2,1)S(1)}, u32[]{:S(2)}, u32[]{:S(2)}) collective-permute-start(bf16[4,128,1024]{2,1,0:T(8,128)(2,1)} %copy-done.17), channel_id=1, source_target_pairs={{16,48},{80,112},{48,56},{112,120},{32,40},{96,104},{8,16},{72,80}... | collective-permute-start | bytes 3145736 | tf_op jit(solution)/shard_map/ppermute | solution.py:333
  155.3 59.0 %collective-permute-start.22 = (f32[2,640,128]{2,1,0:T(8,128)S(1)}, f32[2,640,128]{2,1,0:T(8,128)S(1)}, u32[]{:S(2)}, u32[]{:S(2)}) collective-permute-start(f32[2,640,128]{2,1,0:T(8,128)S(1)} %products.9), channel_id=1, source_target_pairs={{0,96},{1,97},{2,98},{3,99},{4,100},{5,101},{6,102},{7,103},{8,104... | collective-permute-start | bytes 1966088 | tf_op jit(solution)/shard_map/ppermute | solution.py:344
  168.7 46.5 %collective-permute-start.23 = (f32[2,640,128]{2,1,0:T(8,128)S(1)}, f32[2,640,128]{2,1,0:T(8,128)}, u32[]{:S(2)}, u32[]{:S(2)}) collective-permute-start(f32[2,640,128]{2,1,0:T(8,128)S(1)} %products.10), channel_id=1, source_target_pairs={{0,96},{1,97},{2,98},{3,99},{4,100},{5,101},{6,102},{7,103},{8,104... | collective-permute-start | bytes 1966088 | tf_op jit(solution)/shard_map/ppermute | solution.py:344
  192.3 22.0 %collective-permute-start.24 = (f32[1,640,128]{2,1,0:T(8,128)S(1)}, f32[1,640,128]{2,1,0:T(8,128)S(1)}, u32[]{:S(2)}, u32[]{:S(2)}) collective-permute-start(f32[1,640,128]{2,1,0:T(8,128)S(1)} %products.11), channel_id=1, source_target_pairs={{0,96},{1,97},{2,98},{3,99},{4,100},{5,101},{6,102},{7,103},{8,104... | collective-permute-start | bytes 983048 | tf_op jit(solution)/shard_map/ppermute | solution.py:344
  (36 other events, 461.8 us)

commit v2 on v0

v2 whole, which is shorter than its diff:
```python
import functools

import jax
import jax.numpy as jnp
from jax import lax
from jax.experimental import pallas as pl
from jax.experimental.pallas import tpu as pltpu
from jax.sharding import PartitionSpec as P

BLK = 128
NROW, NCOL = 16, 8
LOCAL = 5
ROWS = LOCAL * BLK
NAUX, OCC = 32, 256
WIDTH = NAUX * OCC
PART = BLK // NCOL
NSL = 8
SLW = WIDTH // NSL
SLOTS = LOCAL * NROW // NCOL


def source(col, j):
    return 5 * (col - j + 8) % 8


def masked(x, start, end):
    orbital = lax.broadcasted_iota(jnp.int32, x.shape, 2)
    inside = (orbital >= start) & (orbital < end)
    return jnp.where(inside, x.astype(jnp.float32), 0.0).astype(jnp.bfloat16)


def part_kernel(where, start, end, x_ref, *out_refs):
    i = pl.program_id(0)
    block = LOCAL * where[0] + i
    values = masked(x_ref[...], start[block], end[block]).reshape(PART, WIDTH)
    for j, ref in enumerate(out_refs):

        @pl.when(i == j)
        def _(ref=ref):
            ref[...] = values


def own_part(scalars, coefficients):
    return pl.pallas_call(
        part_kernel,
        grid_spec=pltpu.PrefetchScalarGridSpec(
            num_scalar_prefetch=3,
            grid=(LOCAL,),
            in_specs=[pl.BlockSpec((PART, NAUX, OCC), lambda i, w, s, e: (NCOL * i + w[1], 0, 0))],
            out_specs=[pl.BlockSpec((PART, WIDTH), lambda i, w, s, e: (0, 0))] * LOCAL,
        ),
        out_shape=[jax.ShapeDtypeStruct((PART, WIDTH), jnp.bfloat16)] * LOCAL,
        compiler_params=pltpu.CompilerParams(vmem_limit_bytes=32 << 20),
        cost_estimate=pl.CostEstimate(flops=0, bytes_accessed=5 << 19, transcendentals=0),
        name="own_part",
    )(*scalars, coefficients)


def rows_kernel(where, start, end, x_ref, out_ref):
    block = LOCAL * where[0] + pl.program_id(0)
    values = masked(x_ref[...], start[block], end[block]).reshape(BLK, 16 * OCC)
    for s in range(4):
        out_ref[s] = values[:, s * SLW : (s + 1) * SLW]


def own_rows(scalars, coefficients):
    return pl.pallas_call(
        rows_kernel,
        grid_spec=pltpu.PrefetchScalarGridSpec(
            num_scalar_prefetch=3,
            grid=(LOCAL, 2),
            in_specs=[pl.BlockSpec((BLK, 16, OCC), lambda i, g, w, s, e: (i, g, 0))],
            out_specs=pl.BlockSpec((4, BLK, SLW), lambda i, g, w, s, e: (g, i, 0)),
        ),
        out_shape=jax.ShapeDtypeStruct((NSL, ROWS, SLW), jnp.bfloat16),
        compiler_params=pltpu.CompilerParams(vmem_limit_bytes=32 << 20),
        cost_estimate=pl.CostEstimate(flops=0, bytes_accessed=20 << 20, transcendentals=0),
        name="own_rows",
    )(*scalars, coefficients)


def product_kernel(j, gathered, rows, out_ref, left, right, acc, left_sem, right_sem):
    def copies(s):
        span = pl.ds(s * SLW, SLW)
        return (
            pltpu.make_async_copy(gathered.at[:, span], left.at[s], left_sem.at[s]),
            pltpu.make_async_copy(rows.at[s], right.at[s], right_sem.at[s]),
        )

    for s in range(NSL):
        for copy in copies(s):
            copy.start()
    for s in range(NSL):
        for copy in copies(s):
            copy.wait()
        term = lax.dot_general(left[s], right[s], (((1,), (1,)), ((), ())), preferred_element_type=jnp.float32)
        if s == 0:
            acc[...] = term
        else:
            acc[...] += term
    for col in range(NCOL):
        for h in range(2):
            first = (source(col, j) + 8 * h) * PART
            out_ref[col, h * PART : (h + 1) * PART, :] = acc[first : first + PART, :]


def products(j, gathered, rows):
    anywhere = pl.BlockSpec(memory_space=pl.ANY)
    n = NROW * PART
    return pl.pallas_call(
        functools.partial(product_kernel, j),
        in_specs=[anywhere, anywhere],
        out_specs=pl.BlockSpec(memory_space=pltpu.VMEM),
        out_shape=jax.ShapeDtypeStruct((NCOL, 2 * PART, ROWS), jnp.float32),
        scratch_shapes=[
            pltpu.VMEM((NSL, n, SLW), jnp.bfloat16),
            pltpu.VMEM((NSL, ROWS, SLW), jnp.bfloat16),
            pltpu.VMEM((n, ROWS), jnp.float32),
            pltpu.SemaphoreType.DMA((NSL,)),
            pltpu.SemaphoreType.DMA((NSL,)),
        ],
        compiler_params=pltpu.CompilerParams(vmem_limit_bytes=40 << 20),
        cost_estimate=pl.CostEstimate(flops=2 * n * ROWS * WIDTH, bytes_accessed=15 << 20, transcendentals=0),
        name="products",
    )(gathered, rows)


def place_kernel(where, flags, *refs):
    *pieces, out_ref = refs
    k = pl.program_id(0)
    col = where[1]
    for j, ref in enumerate(pieces):
        first = lax.rem(5 * (col - j + 8), 8)
        for h in range(2):
            slot = lax.div(LOCAL * first + j, NCOL) + LOCAL * h
            tile = ref[:, h * PART : (h + 1) * PART, :].reshape(BLK, BLK)
            weight = flags[SLOTS * k + slot].astype(jnp.float32)
            out_ref[pl.ds(slot, BLK, stride=SLOTS), :] = tile.T * weight


def place(where, flags, pieces):
    return pl.pallas_call(
        place_kernel,
        grid_spec=pltpu.PrefetchScalarGridSpec(
            num_scalar_prefetch=2,
            grid=(LOCAL,),
            in_specs=[pl.BlockSpec((NCOL, 2 * PART, BLK), lambda i, w, f: (0, 0, i))] * LOCAL,
            out_specs=pl.BlockSpec((BLK * SLOTS, BLK), lambda i, w, f: (i, 0)),
        ),
        out_shape=jax.ShapeDtypeStruct((ROWS * SLOTS, BLK), jnp.float32),
        compiler_params=pltpu.CompilerParams(vmem_limit_bytes=32 << 20),
        cost_estimate=pl.CostEstimate(flops=0, bytes_accessed=7 << 20, transcendentals=0),
        name="place",
    )(where, flags, *pieces)


def listed_flags(pair_list, row, col):
    first = jnp.min(pair_list, axis=1)
    second = jnp.max(pair_list, axis=1)
    codes = first * 256 + second
    a = LOCAL * row + jnp.arange(LOCAL, dtype=jnp.int32)[:, None]
    b = col + NCOL * jnp.arange(SLOTS, dtype=jnp.int32)[None, :]
    wanted = (jnp.minimum(a, b) * 256 + jnp.maximum(a, b)).reshape(-1)
    return jnp.any(codes[None, :] == wanted[:, None], axis=1).astype(jnp.int32)


def per_device(coefficients, range_start, range_end, pair_list):
    row, col = lax.axis_index("row"), lax.axis_index("col")
    where = jnp.stack([row, col]).astype(jnp.int32)
    scalars = (where, range_start, range_end)
    parts = own_part(scalars, coefficients)
    gathered = [lax.all_gather(part, "row", axis=0, tiled=True) for part in parts]
    rows = own_rows(scalars, coefficients)
    flags = listed_flags(pair_list, row, col)
    pieces = [
        lax.all_to_all(products(j, g, rows), "col", 0, 0, tiled=True) for j, g in enumerate(gathered)
    ]
    return place(where, flags, pieces).reshape(ROWS, SLOTS, 1, BLK)


def solution(mesh):
    in_specs = (P("row", None, None), P(), P(), P())
    out_specs = P("row", None, "col", None)
    return jax.shard_map(per_device, mesh=mesh, in_specs=in_specs, out_specs=out_specs, check_vma=False)
```

time: 386 us -> 319 us (0.83)
  local copies, waits for them, and re-layouts: 111 us -> 25.1 us
  matrix products: 79.8 us -> 0 us
  waiting for transfers between devices: 128 us -> 203 us
  Pallas kernels: 0 us -> 51.6 us
  other arithmetic: 28.4 us -> 0.44 us
  starting transfers between devices: 0.01 us -> 25.7 us
  loops' own time: 21.8 us -> 0 us
    dot_general x10 -> x0, matrix products: 79.8 us -> none  [compute_block(): lax.dot_general(own_rows, column_block, (((1,), (1,)), ((), ())), preferr...]
    all_gather x1 -> x5, waiting for transfers between devices: 128 us -> 190 us  [per_device(): lax.all_gather(part, 'row', axis=0, tiled=True)]
    pallas_call x0 -> x8, Pallas kernels: none -> 51.6 us  [the longest x5 38.8 us: products(): pl.pallas_call(functools.partial(product_kernel, j), in_specs=[anywhere,...]
    unnamed x11 -> x26, local copies, waits for them, and re-layouts: 51.7 us -> 25 us
    all_to_all x0 -> x5, starting transfers between devices: none -> 25.5 us  [per_device(): lax.all_to_all(products(j, g, rows), 'col', 0, 0, tiled=True)]
    another operation x17 -> x0, loops' own time: 21.8 us -> none  [the longest x1 21.4 us: per_device(): columns = lax.map(single_entry, (block_piece, positions))]
    reshape x2 -> x0, local copies, waits for them, and re-layouts: 21.6 us -> none  [the longest x1 16.5 us: per_device(): coefficients.reshape(block_local, BLK, aux_count, orbital_count)]
    mul x2 -> x0, other arithmetic: 16.3 us -> none  [the longest x1 13.2 us: per_device(): coefficients.reshape(block_local, BLK, aux_count, orbital_count)]
  transfers between devices with their start and end apart: 1 -> 10, of which waited for: 1 -> 6; matrix products, arithmetic and copies ran while one was open for 19% -> 0% of each run, Pallas kernels for 0% -> 14%
where the time goes in v2:
time: 319 us
  waiting for transfers between devices  203 us (64%)
  Pallas kernels  51.6 us (16%)
  starting transfers between devices  25.7 us (8%)
  local copies, waits for them, and re-layouts  25.1 us (8%)
  between operations  13.3 us (4%)
    all_gather x5, waiting for transfers between devices, per_device(): lax.all_gather(part, 'row', axis=0, tiled=True)  190 us
    pallas_call x5, Pallas kernels, products(): pl.pallas_call(functools.partial(product_kernel, j), in_specs=[anywhere,...  38.8 us
    all_to_all x5, starting transfers between devices, per_device(): lax.all_to_all(products(j, g, rows), 'col', 0, 0, tiled=True)  25.5 us
    unnamed x26, local copies, waits for them, and re-layouts  25 us
    all_to_all x5, waiting for transfers between devices, per_device(): lax.all_to_all(products(j, g, rows), 'col', 0, 0, tiled=True)  10.4 us
    pallas_call x1, Pallas kernels, own_rows(): pl.pallas_call(rows_kernel, grid_spec=pltpu.PrefetchScalarGridSpec(num_sc...  6.39 us
  transfers between devices with their start and end apart: 10, of which 6 were waited for; matrix products, arithmetic and copies ran while one was open for 0% of the time, Pallas kernels for 14%

profile of v2, /device:TPU:1, one launch (start us, length us, event | category | flops | bytes accessed | tf_op | source)
XLA Modules:
  0.0 318.6 jit_solution(4130894275246940303)
XLA Ops:
  6.6 4.0 %copy-done.1 = bf16[640,32,256]{2,1,0:T(8,128)(2,1)S(1)} copy-done((bf16[640,32,256]{2,1,0:T(8,128)(2,1)S(1)}, bf16[640,32,256]{2,1,0:T(8,128)(2,1)}, u32[]{:S(2)}) %copy-start.1) | copy-done | bytes 10485784
  11.9 2.4 own_part.1
  17.1 4.0 %copy-done.2 = bf16[640,32,256]{2,1,0:T(8,128)(2,1)S(1)} copy-done((bf16[640,32,256]{2,1,0:T(8,128)(2,1)S(1)}, bf16[640,32,256]{2,1,0:T(8,128)(2,1)}, u32[]{:S(2)}) %copy-start.2) | copy-done | bytes 10485784
  21.0 6.4 %own_rows.1.rows = bf16[8,640,1024]{2,1,0:T(8,128)(2,1)S(1)} custom-call(s32[2]{0:T(128)S(1)} %pad_add_fusion.where, s32[80]{0:T(128)S(1)} %copy-done.10, s32[80]{0:T(128)S(1)} %copy-done.11, bf16[640,32,256]{2,1,0:T(8,128)(2,1)S(1)} %copy-done.2), custom_call_target="tpu_custom_call" | custom-call | bytes 20971520 | tf_op jit(solution)/shard_map/own_rows/pallas_call | solution.py:67
  27.4 4.0 %copy-done = bf16[8,640,1024]{2,1,0:T(8,128)(2,1)} copy-done((bf16[8,640,1024]{2,1,0:T(8,128)(2,1)}, bf16[8,640,1024]{2,1,0:T(8,128)(2,1)S(1)}, u32[]{:S(2)}) %copy-start) | copy-done | bytes 10485784
  31.4 37.7 %all-gather.6.cloned.1.call-done.gathered = bf16[256,8192]{1,0:T(8,128)(2,1)} async-done(((bf16[16,8192]{1,0:T(8,128)(2,1)}), bf16[256,8192]{1,0:T(8,128)(2,1)}) %all-gather.6.cloned.1.call-update) | async-done | bytes 4194320 | tf_op jit(solution)/shard_map/all_gather | solution.py:172
  69.1 2.2 copy-done.7
  71.3 7.9 %products.5 = f32[8,32,640]{2,1,0:T(8,128)} custom-call(bf16[256,8192]{1,0:T(8,128)(2,1)S(1)} %copy-done.7, bf16[8,640,1024]{2,1,0:T(8,128)(2,1)} %copy-done), custom_call_target="tpu_custom_call" | custom-call | flops 2684354560 | bytes 15728640 | tf_op jit(solution)/shard_map/products/pallas_call | solution.py:110
  79.3 5.1 %all-to-all-start = ((f32[8,32,640]{2,1,0:T(8,128)}), f32[8,32,640]{2,1,0:T(8,128)S(1)}, u32[]{:S(2)}, u32[]{:S(2)}) async-start(f32[8,32,640]{2,1,0:T(8,128)} %products.5), calls=%async_computation | async-start | bytes 1310720 | tf_op jit(solution)/shard_map/all_to_all | solution.py:176
  84.4 38.1 %all-gather.8.cloned.1.call-done.gathered = bf16[256,8192]{1,0:T(8,128)(2,1)} async-done(((bf16[16,8192]{1,0:T(8,128)(2,1)}), bf16[256,8192]{1,0:T(8,128)(2,1)}) %all-gather.8.cloned.1.call-update) | async-done | bytes 4194320 | tf_op jit(solution)/shard_map/all_gather | solution.py:172
  124.6 7.9 %products.6 = f32[8,32,640]{2,1,0:T(8,128)} custom-call(bf16[256,8192]{1,0:T(8,128)(2,1)S(1)} %copy-done.6, bf16[8,640,1024]{2,1,0:T(8,128)(2,1)} %copy-done), custom_call_target="tpu_custom_call" | custom-call | flops 2684354560 | bytes 15728640 | tf_op jit(solution)/shard_map/products/pallas_call | solution.py:110
  132.6 5.1 %all-to-all-start.1 = ((f32[8,32,640]{2,1,0:T(8,128)}), f32[8,32,640]{2,1,0:T(8,128)S(1)}, u32[]{:S(2)}, u32[]{:S(2)}) async-start(f32[8,32,640]{2,1,0:T(8,128)} %products.6), calls=%async_computation.1 | async-start | bytes 1310720 | tf_op jit(solution)/shard_map/all_to_all | solution.py:176
  137.7 38.1 %all-gather.10.cloned.1.call-done.gathered = bf16[256,8192]{1,0:T(8,128)(2,1)} async-done(((bf16[16,8192]{1,0:T(8,128)(2,1)}), bf16[256,8192]{1,0:T(8,128)(2,1)}) %all-gather.10.cloned.1.call-update) | async-done | bytes 4194320 | tf_op jit(solution)/shard_map/all_gather | solution.py:172
  175.7 2.2 copy-done.5
  177.9 7.9 %products.7 = f32[8,32,640]{2,1,0:T(8,128)} custom-call(bf16[256,8192]{1,0:T(8,128)(2,1)S(1)} %copy-done.5, bf16[8,640,1024]{2,1,0:T(8,128)(2,1)} %copy-done), custom_call_target="tpu_custom_call" | custom-call | flops 2684354560 | bytes 15728640 | tf_op jit(solution)/shard_map/products/pallas_call | solution.py:110
  185.8 5.1 %all-to-all-start.2 = ((f32[8,32,640]{2,1,0:T(8,128)}), f32[8,32,640]{2,1,0:T(8,128)S(1)}, u32[]{:S(2)}, u32[]{:S(2)}) async-start(f32[8,32,640]{2,1,0:T(8,128)} %products.7), calls=%async_computation.2 | async-start | bytes 1310720 | tf_op jit(solution)/shard_map/all_to_all | solution.py:176
  191.0 37.9 %all-gather.12.cloned.1.call-done.gathered = bf16[256,8192]{1,0:T(8,128)(2,1)} async-done(((bf16[16,8192]{1,0:T(8,128)(2,1)}), bf16[256,8192]{1,0:T(8,128)(2,1)}) %all-gather.12.cloned.1.call-update) | async-done | bytes 4194320 | tf_op jit(solution)/shard_map/all_gather | solution.py:172
  231.1 7.9 %products.8 = f32[8,32,640]{2,1,0:T(8,128)} custom-call(bf16[256,8192]{1,0:T(8,128)(2,1)S(1)} %copy-done.4, bf16[8,640,1024]{2,1,0:T(8,128)(2,1)} %copy-done), custom_call_target="tpu_custom_call" | custom-call | flops 2684354560 | bytes 15728640 | tf_op jit(solution)/shard_map/products/pallas_call | solution.py:110
  239.0 5.1 %all-to-all-start.3 = ((f32[8,32,640]{2,1,0:T(8,128)}), f32[8,32,640]{2,1,0:T(8,128)S(1)}, u32[]{:S(2)}, u32[]{:S(2)}) async-start(f32[8,32,640]{2,1,0:T(8,128)} %products.8), calls=%async_computation.3 | async-start | bytes 1310720 | tf_op jit(solution)/shard_map/all_to_all | solution.py:176
  244.1 37.9 %all-gather.14.cloned.1.call-done.gathered = bf16[256,8192]{1,0:T(8,128)(2,1)} async-done(((bf16[16,8192]{1,0:T(8,128)(2,1)}), bf16[256,8192]{1,0:T(8,128)(2,1)}) %all-gather.14.cloned.1.call-update) | async-done | bytes 4194320 | tf_op jit(solution)/shard_map/all_gather | solution.py:172
  284.2 7.1 %products.9 = f32[8,32,640]{2,1,0:T(8,128)S(1)} custom-call(bf16[256,8192]{1,0:T(8,128)(2,1)S(1)} %copy-done.3, bf16[8,640,1024]{2,1,0:T(8,128)(2,1)} %copy-done), custom_call_target="tpu_custom_call" | custom-call | flops 2684354560 | bytes 15728640 | tf_op jit(solution)/shard_map/products/pallas_call | solution.py:110
  292.1 5.1 %all-to-all-start.4 = ((f32[8,32,640]{2,1,0:T(8,128)}), f32[8,32,640]{2,1,0:T(8,128)S(1)}, u32[]{:S(2)}, u32[]{:S(2)}) async-start(f32[8,32,640]{2,1,0:T(8,128)} %copy-done.8), calls=%async_computation.4 | async-start | bytes 1310720 | tf_op jit(solution)/shard_map/all_to_all | solution.py:176
  297.7 10.4 %all-to-all-done.4.refs_4_ = f32[8,32,640]{2,1,0:T(8,128)S(1)} async-done(((f32[8,32,640]{2,1,0:T(8,128)}), f32[8,32,640]{2,1,0:T(8,128)S(1)}, u32[]{:S(2)}, u32[]{:S(2)}) %all-to-all-start.4) | async-done | bytes 655392 | tf_op jit(solution)/shard_map/all_to_all | solution.py:176
  308.1 4.0 %place.1 = f32[6400,128]{1,0:T(8,128)} custom-call(s32[2]{0:T(128)S(1)} %pad_add_fusion.where, s32[50]{0:T(128)S(1)} %convert_element_type.3.flags, f32[8,32,640]{2,1,0:T(8,128)S(1)} %all-to-all-done.refs_0_, f32[8,32,640]{2,1,0:T(8,128)S(1)} %all-to-all-done.1.refs_1_, f32[8,32,640]{2,1,0:T(8,128)S(1)} %all-to-all-done.2.refs_2_, ...), custom_call_target="tpu_custom_call" | custom-call | bytes 7340032 | tf_op jit(solution)/shard_map/place/pallas_call | solution.py:142
  (44 shorter events, 11.9 us)
Async XLA Ops:
  6.5 62.6 %all-gather.6.cloned.1.call-start = ((), (), s32[]{:S(2)}) async-start(), calls=%async_computation.5 | async-start | bytes 4456448 | tf_op jit(solution)/shard_map/all_gather | solution.py:172
  6.6 4.0 %copy-start.1 = (bf16[640,32,256]{2,1,0:T(8,128)(2,1)S(1)}, bf16[640,32,256]{2,1,0:T(8,128)(2,1)}, u32[]{:S(2)}) copy-start(bf16[640,32,256]{2,1,0:T(8,128)(2,1)} %x_ref.3) | copy-start | bytes 31457284
  10.6 0.7 copy-start.9
  11.2 0.7 copy-start.11
  11.9 5.1 %copy-start.10 = (s32[80]{0:T(128)S(1)}, s32[80]{0:T(128)}, u32[]{:S(2)}) copy-start(s32[80]{0:T(128)} %start.3) | copy-start | bytes 964
  14.4 108.1 %all-gather.8.cloned.1.call-start = ((), (), s32[]{:S(2)}) async-start(), calls=%async_computation.6 | async-start | bytes 4456448 | tf_op jit(solution)/shard_map/all_gather | solution.py:172
  15.1 160.6 %all-gather.10.cloned.1.call-start = ((), (), s32[]{:S(2)}) async-start(), calls=%async_computation.7 | async-start | bytes 4456448 | tf_op jit(solution)/shard_map/all_gather | solution.py:172
  15.9 213.0 %all-gather.12.cloned.1.call-start = ((), (), s32[]{:S(2)}) async-start(), calls=%async_computation.8 | async-start | bytes 4456448 | tf_op jit(solution)/shard_map/all_gather | solution.py:172
  16.4 265.6 %all-gather.14.cloned.1.call-start = ((), (), s32[]{:S(2)}) async-start(), calls=%async_computation.9 | async-start | bytes 4456448 | tf_op jit(solution)/shard_map/all_gather | solution.py:172
  17.0 4.0 %copy-start.2 = (bf16[640,32,256]{2,1,0:T(8,128)(2,1)S(1)}, bf16[640,32,256]{2,1,0:T(8,128)(2,1)}, u32[]{:S(2)}) copy-start(bf16[640,32,256]{2,1,0:T(8,128)(2,1)} %x_ref.3) | copy-start | bytes 31457284
  27.4 4.0 %copy-start = (bf16[8,640,1024]{2,1,0:T(8,128)(2,1)}, bf16[8,640,1024]{2,1,0:T(8,128)(2,1)S(1)}, u32[]{:S(2)}) copy-start(bf16[8,640,1024]{2,1,0:T(8,128)(2,1)S(1)} %own_rows.1.rows) | copy-start | bytes 31457284
  69.1 2.2 copy-start.7
  79.3 53.3 %all-to-all-start = ((f32[8,32,640]{2,1,0:T(8,128)}), f32[8,32,640]{2,1,0:T(8,128)S(1)}, u32[]{:S(2)}, u32[]{:S(2)}) async-start(f32[8,32,640]{2,1,0:T(8,128)} %products.5), calls=%async_computation | async-start | bytes 1310720 | tf_op jit(solution)/shard_map/all_to_all | solution.py:176
  122.4 2.2 copy-start.6
  132.6 53.3 %all-to-all-start.1 = ((f32[8,32,640]{2,1,0:T(8,128)}), f32[8,32,640]{2,1,0:T(8,128)S(1)}, u32[]{:S(2)}, u32[]{:S(2)}) async-start(f32[8,32,640]{2,1,0:T(8,128)} %products.6), calls=%async_computation.1 | async-start | bytes 1310720 | tf_op jit(solution)/shard_map/all_to_all | solution.py:176
  175.7 2.2 copy-start.5
  185.8 53.2 %all-to-all-start.2 = ((f32[8,32,640]{2,1,0:T(8,128)}), f32[8,32,640]{2,1,0:T(8,128)S(1)}, u32[]{:S(2)}, u32[]{:S(2)}) async-start(f32[8,32,640]{2,1,0:T(8,128)} %products.7), calls=%async_computation.2 | async-start | bytes 1310720 | tf_op jit(solution)/shard_map/all_to_all | solution.py:176
  228.9 2.2 copy-start.4
  239.0 53.1 %all-to-all-start.3 = ((f32[8,32,640]{2,1,0:T(8,128)}), f32[8,32,640]{2,1,0:T(8,128)S(1)}, u32[]{:S(2)}, u32[]{:S(2)}) async-start(f32[8,32,640]{2,1,0:T(8,128)} %products.8), calls=%async_computation.3 | async-start | bytes 1310720 | tf_op jit(solution)/shard_map/all_to_all | solution.py:176
  282.0 2.2 copy-start.3
  284.2 13.2 %copy-start.12 = (s32[1976,2]{0,1:T(2,128)S(1)}, s32[1976,2]{0,1:T(2,128)}, u32[]{:S(2)}) copy-start(s32[1976,2]{0,1:T(2,128)} %param.7) | copy-start | bytes 47428
  291.3 0.8 copy-start.8
  292.1 16.0 %all-to-all-start.4 = ((f32[8,32,640]{2,1,0:T(8,128)}), f32[8,32,640]{2,1,0:T(8,128)S(1)}, u32[]{:S(2)}, u32[]{:S(2)}) async-start(f32[8,32,640]{2,1,0:T(8,128)} %copy-done.8), calls=%async_computation.4 | async-start | bytes 1310720 | tf_op jit(solution)/shard_map/all_to_all | solution.py:176
Sparse Core Ops, SparseCore 0:
  14.5 54.6 all-gather.5
  71.3 51.1 all-gather.7
  124.6 51.1 all-gather.9
  177.7 51.0 all-gather.11
  230.9 51.0 all-gather.13

commit v3 on v2

v3 whole, which is shorter than its diff:
```python
import functools

import jax
import jax.numpy as jnp
import numpy as np
from jax import lax
from jax.experimental import pallas as pl
from jax.experimental.pallas import tpu as pltpu
from jax.sharding import PartitionSpec as P

BLK = 128
NX, NY, NZ, NCORE = 4, 4, 4, 2
NCOL = NZ * NCORE
NDEV = NX * NY * NCOL
LOCAL = 5
ROWS = LOCAL * BLK
NAUX, OCC = 32, 256
WIDTH = NAUX * OCC
PIECE = BLK // NCOL
PART = LOCAL * PIECE
NSL = 8
SLW = WIDTH // NSL
SLOTS = LOCAL * NX * NY // NCOL
AXES = ("row", "col")

UNITS = (
    ((0, 0), (0, 0), None),
    ((0, 1), (1, 0), (0, 0)),
    ((1, 0), (0, 1), (0, 0)),
    ((3, 0), (3, 0), (0, 0)),
    ((0, 3), (0, 3), (0, 0)),
    ((1, 1), (1, 1), (1, 1)),
    ((2, 0), (2, 0), (3, 3)),
    ((1, 3), (1, 3), (2, 1)),
    ((2, 1), (2, 1), (5, 5)),
    ((1, 2), (1, 2), (5, 5)),
    ((0, 2), (2, 2), (4, 8)),
    ((2, 2), (0, 2), (9, 9)),
)
BACK = (5, 7, 8, 9)
GROUPS = ((0, 1, 2, 3, 4), (5,), (6, 7), (8, 9), (10, 11))
BATCHES = (
    (("U", 0), ("U", 1), ("U", 2), ("U", 4), ("U", 5), ("V", 5)),
    (("U", 3), ("U", 6), ("U", 7), ("V", 7), ("U", 8), ("U", 9)),
    (("U", 10), ("U", 11), ("V", 8), ("V", 9)),
)
ENTRIES = tuple(entry for batch in BATCHES for entry in batch)


def dev(x, y, col):
    return (x * NY + y) * NCOL + col


def shifted(moves):
    return [
        (dev(x, y, col), dev((x + moves[col % 2][0]) % NX, (y + moves[col % 2][1]) % NY, col))
        for x in range(NX)
        for y in range(NY)
        for col in range(NCOL)
    ]


def step_to(unit):
    moves = []
    for core in range(NCORE):
        here, there = UNITS[unit][core], UNITS[UNITS[unit][2][core]][core]
        moves.append(((here[0] - there[0]) % NX, (here[1] - there[1]) % NY))
    return moves


def step_back(unit):
    return [(-UNITS[unit][core][0] % NX, -UNITS[unit][core][1] % NY) for core in range(NCORE)]


def other_row(kind, unit, core, x, y):
    m = UNITS[unit][core]
    sign = -1 if kind == "U" else 1
    return (x + sign * m[0]) % NX * NY + (y + sign * m[1]) % NY


@functools.cache
def tables():
    sizes = []
    filled = {}
    for n, batch in enumerate(BATCHES):
        for x in range(NX):
            for y in range(NY):
                for core in range(NCORE):
                    classes = {c: [] for c in range(NCOL)}
                    for kind, unit in batch:
                        row = other_row(kind, unit, core, x, y)
                        for block in range(LOCAL * row, LOCAL * row + LOCAL):
                            classes[block % NCOL].append((block, kind))
                    filled[x, y, n, core] = {c: sorted(v) for c, v in classes.items()}
                assert filled[x, y, n, 0] == filled[x, y, n, 1]
        sizes.append(max(len(v) for k, f in filled.items() if k[2] == n for v in f.values()))
    rows = []
    for x in range(NX):
        for y in range(NY):
            for col in range(NCOL):
                values = [x * NY + y, col]
                for n, batch in enumerate(BATCHES):
                    classes = filled[x, y, n, col % 2]
                    for kind, unit in batch:
                        row = other_row(kind, unit, col % 2, x, y)
                        for block in range(LOCAL * row, LOCAL * row + LOCAL):
                            target = block % NCOL
                            values.append(target * sizes[n] + classes[target].index((block, kind)))
                for n in range(len(BATCHES)):
                    held = filled[x, y, n, col % 2][col]
                    for slot in range(sizes[n]):
                        if slot < len(held):
                            values += [held[slot][0] // NCOL, int(held[slot][1] == "V")]
                        else:
                            values += [0, 2]
                rows.append(values)
    return tuple(sizes), np.asarray(rows, np.int32)


T_PIECES = 2
T_SLOTS = T_PIECES + LOCAL * len(ENTRIES)


def masked(x, start, end):
    orbital = lax.broadcasted_iota(jnp.int32, x.shape, 2)
    inside = (orbital >= start) & (orbital < end)
    return jnp.where(inside, x.astype(jnp.float32), 0.0).astype(jnp.bfloat16)


def part_kernel(tab, start, end, x_ref, out_ref, raw, sems):
    def fetch(j):
        return pltpu.make_async_copy(x_ref.at[pl.ds(j * BLK + tab[1] * PIECE, PIECE)], raw.at[j], sems.at[j])

    for j in range(LOCAL):
        fetch(j).start()
    for j in range(LOCAL):
        fetch(j).wait()
        block = LOCAL * tab[0] + j
        values = masked(raw[j], start[block], end[block])
        out_ref[j * PIECE : (j + 1) * PIECE, :] = values.reshape(PIECE, WIDTH)


def own_part(scalars, coefficients):
    return pl.pallas_call(
        part_kernel,
        grid_spec=pltpu.PrefetchScalarGridSpec(
            num_scalar_prefetch=3,
            grid=(1,),
            in_specs=[pl.BlockSpec(memory_space=pl.ANY)],
            out_specs=pl.BlockSpec((PART, WIDTH), lambda i, t, s, e: (0, 0)),
            scratch_shapes=[pltpu.VMEM((LOCAL, PIECE, NAUX, OCC), jnp.bfloat16), pltpu.SemaphoreType.DMA((LOCAL,))],
        ),
        out_shape=jax.ShapeDtypeStruct((PART, WIDTH), jnp.bfloat16),
        compiler_params=pltpu.CompilerParams(vmem_limit_bytes=56 << 20),
        cost_estimate=pl.CostEstimate(flops=0, bytes_accessed=5 << 19, transcendentals=0),
        name="own_part",
    )(*scalars, coefficients)


def rows_kernel(tab, start, end, x_ref, out_ref):
    block = LOCAL * tab[0] + pl.program_id(0)
    values = masked(x_ref[...], start[block], end[block]).reshape(BLK, 16 * OCC)
    for s in range(4):
        out_ref[s] = values[:, s * SLW : (s + 1) * SLW]


def own_rows(scalars, coefficients):
    return pl.pallas_call(
        rows_kernel,
        grid_spec=pltpu.PrefetchScalarGridSpec(
            num_scalar_prefetch=3,
            grid=(LOCAL, 2),
            in_specs=[pl.BlockSpec((BLK, 16, OCC), lambda i, g, t, s, e: (i, g, 0))],
            out_specs=pl.BlockSpec((4, BLK, SLW), lambda i, g, t, s, e: (g, i, 0)),
        ),
        out_shape=jax.ShapeDtypeStruct((NSL, ROWS, SLW), jnp.bfloat16),
        compiler_params=pltpu.CompilerParams(vmem_limit_bytes=56 << 20),
        cost_estimate=pl.CostEstimate(flops=0, bytes_accessed=20 << 20, transcendentals=0),
        name="own_rows",
    )(*scalars, coefficients)


def product_kernel(n, *refs):
    parts, rows, outs = refs[:n], refs[n], refs[n + 1 : 2 * n + 1]
    left, right, acc, left_sem, right_sem = refs[2 * n + 1 :]

    def copies(s):
        span = pl.ds(s * SLW, SLW)
        found = [pltpu.make_async_copy(rows.at[s], right.at[s], right_sem.at[s])]
        for i, part in enumerate(parts):
            target = left.at[s, pl.ds(i * PART, PART), :]
            found.append(pltpu.make_async_copy(part.at[:, span], target, left_sem.at[i, s]))
        return found

    for s in range(NSL):
        for copy in copies(s):
            copy.start()
    for s in range(NSL):
        for copy in copies(s):
            copy.wait()
        term = lax.dot_general(left[s], right[s], (((1,), (1,)), ((), ())), preferred_element_type=jnp.float32)
        if s == 0:
            acc[...] = term
        else:
            acc[...] += term
    for i, out in enumerate(outs):
        out[...] = acc[i * PART : (i + 1) * PART, :]


def products(parts, rows):
    n = len(parts)
    anywhere = pl.BlockSpec(memory_space=pl.ANY)
    return pl.pallas_call(
        functools.partial(product_kernel, n),
        grid=(1,),
        in_specs=[anywhere] * (n + 1),
        out_specs=[pl.BlockSpec((PART, ROWS), lambda i: (0, 0))] * n,
        out_shape=[jax.ShapeDtypeStruct((PART, ROWS), jnp.float32)] * n,
        scratch_shapes=[
            pltpu.VMEM((NSL, n * PART, SLW), jnp.bfloat16),
            pltpu.VMEM((NSL, ROWS, SLW), jnp.bfloat16),
            pltpu.VMEM((n * PART, ROWS), jnp.float32),
            pltpu.SemaphoreType.DMA((n, NSL)),
            pltpu.SemaphoreType.DMA((NSL,)),
        ],
        compiler_params=pltpu.CompilerParams(vmem_limit_bytes=56 << 20),
        cost_estimate=pl.CostEstimate(
            flops=2 * n * PART * ROWS * WIDTH, bytes_accessed=(10 << 20) + n * (3 << 19), transcendentals=0
        ),
        name="products",
    )(*parts, rows)


def pack_kernel(first, batch, tab, *refs):
    *parts, out_ref = refs
    for n, (kind, _) in enumerate(batch):
        part = parts[n]
        for j in range(LOCAL):
            where = tab[T_PIECES + LOCAL * (first + n) + j]
            if kind == "V":
                out_ref[where] = part[:, j * BLK : (j + 1) * BLK]
                continue
            for k in range(LOCAL):
                piece = part[j * PIECE : (j + 1) * PIECE, k * BLK : (k + 1) * BLK]
                out_ref[where, k * PIECE : (k + 1) * PIECE, :] = piece


def pack(tab, first, batch, size, parts):
    return pl.pallas_call(
        functools.partial(pack_kernel, first, batch),
        grid_spec=pltpu.PrefetchScalarGridSpec(
            num_scalar_prefetch=1,
            grid=(1,),
            in_specs=[pl.BlockSpec((PART, ROWS), lambda i, t: (0, 0))] * len(parts),
            out_specs=pl.BlockSpec((NCOL * size, PART, BLK), lambda i, t: (0, 0, 0)),
        ),
        out_shape=jax.ShapeDtypeStruct((NCOL * size, PART, BLK), jnp.float32),
        compiler_params=pltpu.CompilerParams(vmem_limit_bytes=20 << 20),
        cost_estimate=pl.CostEstimate(flops=0, bytes_accessed=3 << 20, transcendentals=0),
        name="pack",
    )(tab, *parts)


def place_kernel(sizes, tab, flags, *refs):
    *pieces, out_ref = refs
    k = pl.program_id(0)
    at = T_SLOTS
    for ref, size in zip(pieces, sizes):
        for n in range(size):
            slot, kind = tab[at], tab[at + 1]
            at += 2
            weight = flags[SLOTS * k + slot].astype(jnp.float32)

            @pl.when(kind == 0)
            def _(ref=ref, n=n, slot=slot, weight=weight):
                tile = ref[:, n].reshape(BLK, BLK)
                out_ref[pl.ds(slot, BLK, stride=SLOTS), :] = tile.T * weight

            @pl.when(kind == 1)
            def _(ref=ref, n=n, slot=slot, weight=weight):
                tile = ref[:, n].reshape(BLK, BLK)
                out_ref[pl.ds(slot, BLK, stride=SLOTS), :] = tile * weight


def place(tab, flags, sizes, pieces):
    return pl.pallas_call(
        functools.partial(place_kernel, sizes),
        grid_spec=pltpu.PrefetchScalarGridSpec(
            num_scalar_prefetch=2,
            grid=(LOCAL,),
            in_specs=[pl.BlockSpec((NCOL, size, PIECE, BLK), lambda i, t, f: (0, 0, i, 0)) for size in sizes],
            out_specs=pl.BlockSpec((BLK * SLOTS, BLK), lambda i, t, f: (i, 0)),
        ),
        out_shape=jax.ShapeDtypeStruct((ROWS * SLOTS, BLK), jnp.float32),
        compiler_params=pltpu.CompilerParams(vmem_limit_bytes=20 << 20),
        cost_estimate=pl.CostEstimate(flops=0, bytes_accessed=7 << 20, transcendentals=0),
        name="place",
    )(tab, flags, *pieces)


def listed_flags(pair_list, row, col):
    first = jnp.min(pair_list, axis=1)
    second = jnp.max(pair_list, axis=1)
    codes = first * 256 + second
    a = LOCAL * row + jnp.arange(LOCAL, dtype=jnp.int32)[:, None]
    b = col + NCOL * jnp.arange(SLOTS, dtype=jnp.int32)[None, :]
    wanted = (jnp.minimum(a, b) * 256 + jnp.maximum(a, b)).reshape(-1)
    return jnp.any(codes[None, :] == wanted[:, None], axis=1).astype(jnp.int32)


def per_device(coefficients, range_start, range_end, pair_list):
    sizes, table = tables()
    row, col = lax.axis_index("row"), lax.axis_index("col")
    tab = lax.dynamic_index_in_dim(jnp.asarray(table), row * NCOL + col, 0, keepdims=False)
    scalars = (tab, range_start, range_end)
    held = {0: own_part(scalars, coefficients)}
    rows = own_rows(scalars, coefficients)
    flags = listed_flags(pair_list, row, col)
    made = {}

    def send(unit, *first):
        a, b = UNITS[unit][2]
        source = held[a] if a == b else jnp.where(col % 2 == 0, held[a], held[b])
        if first:
            source = lax.optimization_barrier((source, *first))[0]
        held[unit] = lax.ppermute(source, AXES, shifted(step_to(unit)))

    def multiply(group):
        for unit, product in zip(group, products([held[u] for u in group], rows)):
            made["U", unit] = product
            if unit in BACK:
                made["V", unit] = lax.ppermute(product, AXES, shifted(step_back(unit)))

    for unit in (1, 2, 3, 4):
        send(unit)
    for unit in (5, 6, 7):
        send(unit, rows)
    multiply(GROUPS[0])
    send(8, made["U", 0])
    send(9, made["U", 0])
    send(11)
    send(10)
    for group in GROUPS[1:]:
        multiply(group)
    pieces = []
    first = 0
    for batch, size in zip(BATCHES, sizes):
        message = pack(tab, first, batch, size, [made[entry] for entry in batch])
        first += len(batch)
        got = lax.all_to_all(message, "col", 0, 0, tiled=True)
        pieces.append(got.reshape(NCOL, size, PART, BLK))
    return place(tab, flags, sizes, pieces).reshape(ROWS, SLOTS, 1, BLK)


def solution(mesh):
    in_specs = (P("row", None, None), P(), P(), P())
    out_specs = P("row", None, "col", None)
    return jax.shard_map(per_device, mesh=mesh, in_specs=in_specs, out_specs=out_specs, check_vma=False)
```

time: 319 us -> 175 us (0.55)
  waiting for transfers between devices: 203 us -> 43.1 us
  starting transfers between devices: 25.7 us -> 49.6 us
  Pallas kernels: 51.6 us -> 69.8 us
  local copies, waits for them, and re-layouts: 25.1 us -> 7.17 us
  between operations: 13.3 us -> 0.27 us
  other arithmetic: 0.44 us -> 4.19 us
    all_gather x5 -> x0, waiting for transfers between devices: 190 us -> none  [per_device(): lax.all_gather(part, 'row', axis=0, tiled=True)]
    ppermute x0 -> x15, starting transfers between devices: none -> 22.9 us  [the longest x11 16.4 us: send(): held[unit] = lax.ppermute(source, AXES, shifted(step_to(unit)))]
    ppermute x0 -> x15, waiting for transfers between devices: none -> 20 us  [the longest x11 16.2 us: send(): held[unit] = lax.ppermute(source, AXES, shifted(step_to(unit)))]
    unnamed x26 -> x42, local copies, waits for them, and re-layouts: 25 us -> 5.92 us
    all_to_all x5 -> x3, waiting for transfers between devices: 10.4 us -> 23.1 us  [per_device(): got = lax.all_to_all(message, 'col', 0, 0, tiled=True)]
    pallas_call x6 -> x9, Pallas kernels: 42.7 us -> 52.8 us  [the longest x5 40.5 us: products(): pl.pallas_call(functools.partial(product_kernel, n), grid=(1,), in_specs=...]
    pallas_call x1, Pallas kernels: 6.39 us -> 13.6 us  [own_rows(): pl.pallas_call(rows_kernel, grid_spec=pltpu.PrefetchScalarGridSpec(num_sc...]
    select_n x0 -> x2, other arithmetic: none -> 3.82 us  [send(): source = held[a] if a == b else jnp.where(col % 2 == 0, held[a], held[b])]
  transfers between devices with their start and end apart: 10 -> 18, of which waited for: 6 -> 8; matrix products, arithmetic and copies ran while one was open for 0% -> 2% of each run, Pallas kernels for 14% -> 34%
where the time goes in v3:
time: 175 us; the launch traced here: 174 us
  Pallas kernels  69.8 us (40%)
  starting transfers between devices  49.6 us (28%)
  waiting for transfers between devices  43.1 us (25%)
  local copies, waits for them, and re-layouts  7.17 us (4%)
  other arithmetic  4.19 us (2%)
    pallas_call x5, Pallas kernels, products(): pl.pallas_call(functools.partial(product_kernel, n), grid=(1,), in_specs=...  40.5 us
    all_to_all x3, starting transfers between devices, per_device(): got = lax.all_to_all(message, 'col', 0, 0, tiled=True)  26.7 us
    all_to_all x3, waiting for transfers between devices, per_device(): got = lax.all_to_all(message, 'col', 0, 0, tiled=True)  23.1 us
    ppermute x11, starting transfers between devices, send(): held[unit] = lax.ppermute(source, AXES, shifted(step_to(unit)))  16.4 us
    ppermute x11, waiting for transfers between devices, send(): held[unit] = lax.ppermute(source, AXES, shifted(step_to(unit)))  16.2 us
    pallas_call x1, Pallas kernels, own_rows(): pl.pallas_call(rows_kernel, grid_spec=pltpu.PrefetchScalarGridSpec(num_sc...  13.6 us
    pallas_call x1, Pallas kernels, place(): pl.pallas_call(functools.partial(place_kernel, sizes), grid_spec=pltpu.Pr...  7.22 us
    ppermute x4, starting transfers between devices, multiply(): made['V', unit] = lax.ppermute(product, AXES, shifted(step_back(unit)))  6.5 us
  transfers between devices with their start and end apart: 18, of which 8 were waited for; matrix products, arithmetic and copies ran while one was open for 2% of the time, Pallas kernels for 34%

profile of v3, /device:TPU:1, one launch (start us, length us, event | category | flops | bytes accessed | tf_op | source)
XLA Modules:
  0.0 174.1 jit_solution(4275668689269935245)
XLA Ops:
  1.2 3.3 %own_part.1.refs_0_ = bf16[80,8192]{1,0:T(8,128)(2,1)} custom-call(s32[108]{0:T(128)} %dynamic-slice_bitcast_fusion.tab, s32[80]{0:T(128)} %start.3, s32[80]{0:T(128)} %end.3, bf16[640,32,256]{2,1,0:T(8,128)(2,1)} %x_ref.3), custom_call_target="tpu_custom_call" | custom-call | bytes 2621440 | tf_op jit(solution)/shard_map/own_part/pallas_call | solution.py:144
  4.5 2.1 %collective-permute-start = (bf16[80,8192]{1,0:T(8,128)(2,1)}, bf16[80,8192]{1,0:T(8,128)(2,1)S(1)}, u32[]{:S(2)}, u32[]{:S(2)}) collective-permute-start(bf16[80,8192]{1,0:T(8,128)(2,1)} %own_part.1.refs_0_), channel_id=1, source_target_pairs={{0,8},{1,33},{2,10},{3,35},{4,12},{5,37},{6,14},{7,39},{8,16},{9,4... | collective-permute-start | bytes 3932168 | tf_op jit(solution)/shard_map/ppermute | solution.py:326
  10.8 13.6 %own_rows.1.refs_5_.refs_1_.refs_2_ = bf16[8,640,1024]{2,1,0:T(8,128)(2,1)} custom-call(s32[108]{0:T(128)} %dynamic-slice_bitcast_fusion.tab, s32[80]{0:T(128)} %start.3, s32[80]{0:T(128)} %end.3, bf16[640,32,256]{2,1,0:T(8,128)(2,1)} %x_ref.3), custom_call_target="tpu_custom_call" | custom-call | bytes 20971520 | tf_op jit(solution)/shard_map/own_rows/pallas_call | solution.py:168
  24.4 7.3 %collective-permute-done.refs_1_ = bf16[80,8192]{1,0:T(8,128)(2,1)S(1)} collective-permute-done((bf16[80,8192]{1,0:T(8,128)(2,1)}, bf16[80,8192]{1,0:T(8,128)(2,1)S(1)}, u32[]{:S(2)}, u32[]{:S(2)}) %collective-permute-start) | collective-permute-done | bytes 1310752 | tf_op jit(solution)/shard_map/ppermute | solution.py:326
  33.5 2.7 %collective-permute-done.2.refs_3_ = bf16[80,8192]{1,0:T(8,128)(2,1)} collective-permute-done((bf16[80,8192]{1,0:T(8,128)(2,1)}, bf16[80,8192]{1,0:T(8,128)(2,1)}, u32[]{:S(2)}, u32[]{:S(2)}) %collective-permute-start.2) | collective-permute-done | bytes 1310752 | tf_op jit(solution)/shard_map/ppermute | solution.py:326
  39.7 3.5 %collective-permute-start.7 = (bf16[80,8192]{1,0:T(8,128)(2,1)}, bf16[80,8192]{1,0:T(8,128)(2,1)S(1)}, u32[]{:S(2)}, u32[]{:S(2)}) collective-permute-start(bf16[80,8192]{1,0:T(8,128)(2,1)} %broadcast_select_fusion.1), channel_id=1, source_target_pairs={{0,24},{1,25},{2,26},{3,27},{4,28},{5,29},{6,30},{7,31},{8,0},{9,1... | collective-permute-start | bytes 3932168 | tf_op jit(solution)/shard_map/ppermute | solution.py:326
  44.3 12.7 %products.5 = (f32[80,640]{1,0:T(8,128)}, f32[80,640]{1,0:T(8,128)}, f32[80,640]{1,0:T(8,128)}, f32[80,640]{1,0:T(8,128)}, f32[80,640]{1,0:T(8,128)}) custom-call(bf16[80,8192]{1,0:T(8,128)(2,1)} %own_part.1.refs_0_, bf16[80,8192]{1,0:T(8,128)(2,1)} %copy-done.17, bf16[80,8192]{1,0:T(8,128)(2,1)} %collective-permute-done.1.refs_2_, ...), custom_call_target="tpu_custom_call" | custom-call | flops 4194304000 | bytes 18350080 | tf_op jit(solution)/shard_map/products/pallas_call | solution.py:213
  57.1 6.2 %products.6.refs_4_ = f32[80,640]{1,0:T(8,128)} custom-call(bf16[80,8192]{1,0:T(8,128)(2,1)} %collective-permute-done.4.refs_0_, bf16[8,640,1024]{2,1,0:T(8,128)(2,1)} %own_rows.1.refs_5_.refs_1_.refs_2_), custom_call_target="tpu_custom_call" | custom-call | flops 838860800 | bytes 12058624 | tf_op jit(solution)/shard_map/products/pallas_call | solution.py:213
  63.3 2.6 %collective-permute-start.5 = (f32[80,640]{1,0:T(8,128)}, f32[80,640]{1,0:T(8,128)S(1)}, u32[]{:S(2)}, u32[]{:S(2)}) collective-permute-start(f32[80,640]{1,0:T(8,128)} %products.6.refs_4_), channel_id=1, source_target_pairs={{0,120},{1,121},{2,122},{3,123},{4,124},{5,125},{6,126},{7,127},{8... | collective-permute-start | bytes 614408 | tf_op jit(solution)/shard_map/ppermute | solution.py:332
  67.4 5.2 %collective-permute-done.7.refs_1_ = bf16[80,8192]{1,0:T(8,128)(2,1)S(1)} collective-permute-done((bf16[80,8192]{1,0:T(8,128)(2,1)}, bf16[80,8192]{1,0:T(8,128)(2,1)S(1)}, u32[]{:S(2)}, u32[]{:S(2)}) %collective-permute-start.7) | collective-permute-done | bytes 1310752 | tf_op jit(solution)/shard_map/ppermute | solution.py:326
  73.8 7.2 %products.7 = (f32[80,640]{1,0:T(8,128)}, f32[80,640]{1,0:T(8,128)}) custom-call(bf16[80,8192]{1,0:T(8,128)(2,1)} %copy-done.18, bf16[80,8192]{1,0:T(8,128)(2,1)} %copy-done.19, bf16[8,640,1024]{2,1,0:T(8,128)(2,1)} %own_rows.1.refs_5_.refs_1_.refs_2_), custom_call_target="tpu_custom_call" | custom-call | flops 1677721600 | bytes 13631488 | tf_op jit(solution)/shard_map/products/pallas_call | solution.py:213
  82.8 11.2 %all-to-all-start = ((f32[32,80,128]{2,1,0:T(8,128)}), f32[32,80,128]{2,1,0:T(8,128)S(1)}, u32[]{:S(2)}, u32[]{:S(2)}) async-start(f32[32,80,128]{2,1,0:T(8,128)} %pack.3), calls=%async_computation | async-start | bytes 2621440 | tf_op jit(solution)/shard_map/all_to_all | solution.py:350
  94.0 2.5 %broadcast_select_fusion = bf16[80,8192]{1,0:T(8,128)(2,1)} fusion(bf16[80,8192]{1,0:T(8,128)(2,1)S(1)} %copy-done.16, bf16[80,8192]{1,0:T(8,128)(2,1)} %collective-permute-done.9.refs_0_, pred[]{:T(512)S(6)} %eq.23), kind=kLoop, calls=%fused_computation | loop fusion | flops 655360 | bytes 3932161 | tf_op jit(solution)/shard_map/jit(_where)/select_n | solution.py:323
  98.6 7.2 %products.8 = (f32[80,640]{1,0:T(8,128)}, f32[80,640]{1,0:T(8,128)}) custom-call(bf16[80,8192]{1,0:T(8,128)(2,1)} %collective-permute-done.9.refs_0_, bf16[80,8192]{1,0:T(8,128)(2,1)} %collective-permute-done.10.refs_1_, bf16[8,640,1024]{2,1,0:T(8,128)(2,1)} %own_rows.1.refs_5_.refs_1_.refs_2_), custom_call_target="tpu_custom_call" | custom-call | flops 1677721600 | bytes 13631488 | tf_op jit(solution)/shard_map/products/pallas_call | solution.py:213
  107.7 1.8 %pack.4 = f32[40,80,128]{2,1,0:T(8,128)} custom-call(s32[108]{0:T(128)S(1)} %copy-done.14, f32[80,640]{1,0:T(8,128)S(1)} %copy-done.1, f32[80,640]{1,0:T(8,128)S(1)} %copy-done.2, f32[80,640]{1,0:T(8,128)S(1)} %copy-done.3, f32[80,640]{1,0:T(8,128)S(1)} %collective-permute-done.8.refs_3_, f32[80,640]{1,0:T(8,128)S(1)} %copy-done.6, f32[80,640]{1,0:T(8,128)S(1)} %copy-done.4), custom_call_target="tpu_custom_call" | custom-call | bytes 3145728 | tf_op jit(solution)/shard_map/pack/pallas_call | solution.py:249
  109.5 2.4 %all-to-all-done = f32[32,80,128]{2,1,0:T(8,128)S(1)} async-done(((f32[32,80,128]{2,1,0:T(8,128)}), f32[32,80,128]{2,1,0:T(8,128)S(1)}, u32[]{:S(2)}, u32[]{:S(2)}) %all-to-all-start) | async-done | bytes 1310752 | tf_op jit(solution)/shard_map/all_to_all | solution.py:350
  111.9 10.5 %all-to-all-start.1 = ((f32[40,80,128]{2,1,0:T(8,128)}), f32[40,80,128]{2,1,0:T(8,128)S(1)}, u32[]{:S(2)}, u32[]{:S(2)}) async-start(f32[40,80,128]{2,1,0:T(8,128)} %pack.4), calls=%async_computation.1 | async-start | bytes 3276800 | tf_op jit(solution)/shard_map/all_to_all | solution.py:350
  123.2 3.0 %collective-permute-start.14 = (f32[80,640]{1,0:T(8,128)S(1)}, f32[80,640]{1,0:T(8,128)S(1)}, u32[]{:S(2)}, u32[]{:S(2)}) collective-permute-start(f32[80,640]{1,0:T(8,128)S(1)} %copy-done.5), channel_id=1, source_target_pairs={{0,112},{1,113},{2,114},{3,115},{4,116},{5,117},{6,118},{7,119},{8... | collective-permute-start | bytes 614408 | tf_op jit(solution)/shard_map/ppermute | solution.py:332
  126.2 7.2 %products.9 = (f32[80,640]{1,0:T(8,128)}, f32[80,640]{1,0:T(8,128)}) custom-call(bf16[80,8192]{1,0:T(8,128)(2,1)} %collective-permute-done.11.refs_0_, bf16[80,8192]{1,0:T(8,128)(2,1)} %collective-permute-done.12.refs_1_, bf16[8,640,1024]{2,1,0:T(8,128)(2,1)} %own_rows.1.refs_5_.refs_1_.refs_2_), custom_call_target="tpu_custom_call" | custom-call | flops 1677721600 | bytes 13631488 | tf_op jit(solution)/shard_map/products/pallas_call | solution.py:213
  133.4 3.8 %collective-permute-done.14.refs_3_ = f32[80,640]{1,0:T(8,128)S(1)} collective-permute-done((f32[80,640]{1,0:T(8,128)S(1)}, f32[80,640]{1,0:T(8,128)S(1)}, u32[]{:S(2)}, u32[]{:S(2)}) %collective-permute-start.14) | collective-permute-done | bytes 204832 | tf_op jit(solution)/shard_map/ppermute | solution.py:332
  140.7 3.1 %all-to-all-done.1 = f32[40,80,128]{2,1,0:T(8,128)S(1)} async-done(((f32[40,80,128]{2,1,0:T(8,128)}), f32[40,80,128]{2,1,0:T(8,128)S(1)}, u32[]{:S(2)}, u32[]{:S(2)}) %all-to-all-start.1) | async-done | bytes 1638432 | tf_op jit(solution)/shard_map/all_to_all | solution.py:350
  143.8 5.0 %all-to-all-start.2 = ((f32[32,80,128]{2,1,0:T(8,128)}), f32[32,80,128]{2,1,0:T(8,128)}, u32[]{:S(2)}, u32[]{:S(2)}) async-start(f32[32,80,128]{2,1,0:T(8,128)} %pack.5), calls=%async_computation.2 | async-start | bytes 2621440 | tf_op jit(solution)/shard_map/all_to_all | solution.py:350
  149.3 17.6 %all-to-all-done.2 = f32[32,80,128]{2,1,0:T(8,128)} async-done(((f32[32,80,128]{2,1,0:T(8,128)}), f32[32,80,128]{2,1,0:T(8,128)}, u32[]{:S(2)}, u32[]{:S(2)}) %all-to-all-start.2) | async-done | bytes 1310752 | tf_op jit(solution)/shard_map/all_to_all | solution.py:350
  166.9 7.2 %place.1 = f32[6400,128]{1,0:T(8,128)} custom-call(s32[108]{0:T(128)S(1)} %copy-done.14, s32[50]{0:T(128)S(1)} %convert_element_type.3.flags, f32[8,4,80,128]{3,2,1,0:T(8,128)S(1)} %bitcast.7, f32[8,5,80,128]{3,2,1,0:T(8,128)S(1)} %bitcast.6, f32[8,4,80,128]{3,2,1,0:T(8,128)} %bitcast.3.refs_2_), custom_call_target="tpu_custom_call" | custom-call | bytes 7340032 | tf_op jit(solution)/shard_map/place/pallas_call | solution.py:286
  (76 shorter events, 24.8 us)
Async XLA Ops:
  4.5 27.3 %collective-permute-start = (bf16[80,8192]{1,0:T(8,128)(2,1)}, bf16[80,8192]{1,0:T(8,128)(2,1)S(1)}, u32[]{:S(2)}, u32[]{:S(2)}) collective-permute-start(bf16[80,8192]{1,0:T(8,128)(2,1)} %own_part.1.refs_0_), channel_id=1, source_target_pairs={{0,8},{1,33},{2,10},{3,35},{4,12},{5,37},{6,14},{7,39},{8,16},{9,4... | collective-permute-start | bytes 3932168 | tf_op jit(solution)/shard_map/ppermute | solution.py:326
  6.6 29.5 %collective-permute-start.2 = (bf16[80,8192]{1,0:T(8,128)(2,1)}, bf16[80,8192]{1,0:T(8,128)(2,1)}, u32[]{:S(2)}, u32[]{:S(2)}) collective-permute-start(bf16[80,8192]{1,0:T(8,128)(2,1)} %own_part.1.refs_0_), channel_id=1, source_target_pairs={{0,96},{1,97},{2,98},{3,99},{4,100},{5,101},{6,102},{7,103},{8,104... | collective-permute-start | bytes 3932168 | tf_op jit(solution)/shard_map/ppermute | solution.py:326
  7.9 30.5 %collective-permute-start.1 = (bf16[80,8192]{1,0:T(8,128)(2,1)}, bf16[80,8192]{1,0:T(8,128)(2,1)}, u32[]{:S(2)}, u32[]{:S(2)}) collective-permute-start(bf16[80,8192]{1,0:T(8,128)(2,1)} %own_part.1.refs_0_), channel_id=1, source_target_pairs={{0,32},{1,9},{2,34},{3,11},{4,36},{5,13},{6,38},{7,15},{8,40},{9,1... | collective-permute-start | bytes 3932168 | tf_op jit(solution)/shard_map/ppermute | solution.py:326
  9.3 33.9 %collective-permute-start.3 = (bf16[80,8192]{1,0:T(8,128)(2,1)}, bf16[80,8192]{1,0:T(8,128)(2,1)S(1)}, u32[]{:S(2)}, u32[]{:S(2)}) collective-permute-start(bf16[80,8192]{1,0:T(8,128)(2,1)} %own_part.1.refs_0_), channel_id=1, source_target_pairs={{0,24},{1,25},{2,26},{3,27},{4,28},{5,29},{6,30},{7,31},{8,0},{9,1... | collective-permute-start | bytes 3932168 | tf_op jit(solution)/shard_map/ppermute | solution.py:326
  31.8 25.2 %collective-permute-start.4 = (bf16[80,8192]{1,0:T(8,128)(2,1)S(1)}, bf16[80,8192]{1,0:T(8,128)(2,1)}, u32[]{:S(2)}, u32[]{:S(2)}) collective-permute-start(bf16[80,8192]{1,0:T(8,128)(2,1)S(1)} %collective-permute-done.refs_1_), channel_id=1, source_target_pairs={{0,32},{1,9},{2,34},{3,11},{4,36},{5,13},{6,38},{7,15},{8,40},{9,1... | collective-permute-start | bytes 3932168 | tf_op jit(solution)/shard_map/ppermute | solution.py:326
  36.1 31.3 %collective-permute-start.6 = (bf16[80,8192]{1,0:T(8,128)(2,1)}, bf16[80,8192]{1,0:T(8,128)(2,1)S(1)}, u32[]{:S(2)}, u32[]{:S(2)}) collective-permute-start(bf16[80,8192]{1,0:T(8,128)(2,1)} %collective-permute-done.2.refs_3_), channel_id=1, source_target_pairs={{0,96},{1,97},{2,98},{3,99},{4,100},{5,101},{6,102},{7,103},{8,104... | collective-permute-start | bytes 3932168 | tf_op jit(solution)/shard_map/ppermute | solution.py:326
  39.7 32.9 %collective-permute-start.7 = (bf16[80,8192]{1,0:T(8,128)(2,1)}, bf16[80,8192]{1,0:T(8,128)(2,1)S(1)}, u32[]{:S(2)}, u32[]{:S(2)}) collective-permute-start(bf16[80,8192]{1,0:T(8,128)(2,1)} %broadcast_select_fusion.1), channel_id=1, source_target_pairs={{0,24},{1,25},{2,26},{3,27},{4,28},{5,29},{6,30},{7,31},{8,0},{9,1... | collective-permute-start | bytes 3932168 | tf_op jit(solution)/shard_map/ppermute | solution.py:326
  57.0 37.0 %collective-permute-start.9 = (bf16[80,8192]{1,0:T(8,128)(2,1)}, bf16[80,8192]{1,0:T(8,128)(2,1)}, u32[]{:S(2)}, u32[]{:S(2)}) collective-permute-start(bf16[80,8192]{1,0:T(8,128)(2,1)} %collective-permute-done.4.refs_0_), channel_id=1, source_target_pairs={{0,32},{1,33},{2,34},{3,35},{4,36},{5,37},{6,38},{7,39},{8,40},{9,... | collective-permute-start | bytes 3932168 | tf_op jit(solution)/shard_map/ppermute | solution.py:326
  63.3 17.8 %copy-start = (f32[80,640]{1,0:T(8,128)S(1)}, f32[80,640]{1,0:T(8,128)}, u32[]{:S(2)}) copy-start(f32[80,640]{1,0:T(8,128)} %products.6.refs_4_) | copy-start | bytes 614404
  63.3 17.8 %copy-start.10 = (f32[80,640]{1,0:T(8,128)S(1)}, f32[80,640]{1,0:T(8,128)}, u32[]{:S(2)}) copy-start(f32[80,640]{1,0:T(8,128)} %get-tuple-element.20.refs_0_) | copy-start | bytes 614404
  63.3 17.8 %copy-start.11 = (f32[80,640]{1,0:T(8,128)S(1)}, f32[80,640]{1,0:T(8,128)}, u32[]{:S(2)}) copy-start(f32[80,640]{1,0:T(8,128)} %get-tuple-element.21.refs_1_) | copy-start | bytes 614404
  63.3 17.8 %copy-start.12 = (f32[80,640]{1,0:T(8,128)S(1)}, f32[80,640]{1,0:T(8,128)}, u32[]{:S(2)}) copy-start(f32[80,640]{1,0:T(8,128)} %get-tuple-element.22.refs_2_) | copy-start | bytes 614404
  63.3 17.8 %copy-start.13 = (f32[80,640]{1,0:T(8,128)S(1)}, f32[80,640]{1,0:T(8,128)}, u32[]{:S(2)}) copy-start(f32[80,640]{1,0:T(8,128)} %get-tuple-element.23.refs_3_) | copy-start | bytes 614404
  63.3 17.8 %copy-start.14 = (s32[108]{0:T(128)S(1)}, s32[108]{0:T(128)}, u32[]{:S(2)}) copy-start(s32[108]{0:T(128)} %dynamic-slice_bitcast_fusion.tab) | copy-start | bytes 1300
  63.3 17.7 %collective-permute-start.5 = (f32[80,640]{1,0:T(8,128)}, f32[80,640]{1,0:T(8,128)S(1)}, u32[]{:S(2)}, u32[]{:S(2)}) collective-permute-start(f32[80,640]{1,0:T(8,128)} %products.6.refs_4_), channel_id=1, source_target_pairs={{0,120},{1,121},{2,122},{3,123},{4,124},{5,125},{6,126},{7,127},{8... | collective-permute-start | bytes 614408 | tf_op jit(solution)/shard_map/ppermute | solution.py:332
  66.0 31.9 %collective-permute-start.10 = (bf16[80,8192]{1,0:T(8,128)(2,1)}, bf16[80,8192]{1,0:T(8,128)(2,1)}, u32[]{:S(2)}, u32[]{:S(2)}) collective-permute-start(bf16[80,8192]{1,0:T(8,128)(2,1)} %collective-permute-done.4.refs_0_), channel_id=1, source_target_pairs={{0,8},{1,9},{2,10},{3,11},{4,12},{5,13},{6,14},{7,15},{8,16},{9,17... | collective-permute-start | bytes 3932168 | tf_op jit(solution)/shard_map/ppermute | solution.py:326
  81.0 24.8 %collective-permute-start.8 = (f32[80,640]{1,0:T(8,128)}, f32[80,640]{1,0:T(8,128)S(1)}, u32[]{:S(2)}, u32[]{:S(2)}) collective-permute-start(f32[80,640]{1,0:T(8,128)} %get-tuple-element.29.refs_2_), channel_id=1, source_target_pairs={{0,104},{1,105},{2,106},{3,107},{4,108},{5,109},{6,110},{7,111},{8... | collective-permute-start | bytes 614408 | tf_op jit(solution)/shard_map/ppermute | solution.py:332
  82.8 29.1 %all-to-all-start = ((f32[32,80,128]{2,1,0:T(8,128)}), f32[32,80,128]{2,1,0:T(8,128)S(1)}, u32[]{:S(2)}, u32[]{:S(2)}) async-start(f32[32,80,128]{2,1,0:T(8,128)} %pack.3), calls=%async_computation | async-start | bytes 2621440 | tf_op jit(solution)/shard_map/all_to_all | solution.py:350
  96.6 29.6 %collective-permute-start.11 = (bf16[80,8192]{1,0:T(8,128)(2,1)}, bf16[80,8192]{1,0:T(8,128)(2,1)}, u32[]{:S(2)}, u32[]{:S(2)}) collective-permute-start(bf16[80,8192]{1,0:T(8,128)(2,1)} %broadcast_select_fusion), channel_id=1, source_target_pairs={{0,24},{1,9},{2,26},{3,11},{4,28},{5,13},{6,30},{7,15},{8,0},{9,17... | collective-permute-start | bytes 3932168 | tf_op jit(solution)/shard_map/ppermute | solution.py:326
  97.9 28.3 %collective-permute-start.12 = (bf16[80,8192]{1,0:T(8,128)(2,1)}, bf16[80,8192]{1,0:T(8,128)(2,1)}, u32[]{:S(2)}, u32[]{:S(2)}) collective-permute-start(bf16[80,8192]{1,0:T(8,128)(2,1)} %collective-permute-done.10.refs_1_), channel_id=1, source_target_pairs={{0,32},{1,97},{2,34},{3,99},{4,36},{5,101},{6,38},{7,103},{8,40},{... | collective-permute-start | bytes 3932168 | tf_op jit(solution)/shard_map/ppermute | solution.py:326
  111.9 31.9 %all-to-all-start.1 = ((f32[40,80,128]{2,1,0:T(8,128)}), f32[40,80,128]{2,1,0:T(8,128)S(1)}, u32[]{:S(2)}, u32[]{:S(2)}) async-start(f32[40,80,128]{2,1,0:T(8,128)} %pack.4), calls=%async_computation.1 | async-start | bytes 3276800 | tf_op jit(solution)/shard_map/all_to_all | solution.py:350
  122.4 11.0 %collective-permute-start.13 = (f32[80,640]{1,0:T(8,128)S(1)}, f32[80,640]{1,0:T(8,128)S(1)}, u32[]{:S(2)}, u32[]{:S(2)}) collective-permute-start(f32[80,640]{1,0:T(8,128)S(1)} %copy-done.7), channel_id=1, source_target_pairs={{0,88},{1,89},{2,90},{3,91},{4,92},{5,93},{6,94},{7,95},{8,64},{9,... | collective-permute-start | bytes 614408 | tf_op jit(solution)/shard_map/ppermute | solution.py:332
  123.2 14.1 %collective-permute-start.14 = (f32[80,640]{1,0:T(8,128)S(1)}, f32[80,640]{1,0:T(8,128)S(1)}, u32[]{:S(2)}, u32[]{:S(2)}) collective-permute-start(f32[80,640]{1,0:T(8,128)S(1)} %copy-done.5), channel_id=1, source_target_pairs={{0,112},{1,113},{2,114},{3,115},{4,116},{5,117},{6,118},{7,119},{8... | collective-permute-start | bytes 614408 | tf_op jit(solution)/shard_map/ppermute | solution.py:332
  143.8 23.0 %all-to-all-start.2 = ((f32[32,80,128]{2,1,0:T(8,128)}), f32[32,80,128]{2,1,0:T(8,128)}, u32[]{:S(2)}, u32[]{:S(2)}) async-start(f32[32,80,128]{2,1,0:T(8,128)} %pack.5), calls=%async_computation.2 | async-start | bytes 2621440 | tf_op jit(solution)/shard_map/all_to_all | solution.py:350
  (15 other events, 92.9 us)

commit v4 on v3

v4 whole, which is shorter than its diff:
```python
import functools

import jax
import jax.numpy as jnp
import numpy as np
from jax import lax
from jax.experimental import pallas as pl
from jax.experimental.pallas import tpu as pltpu
from jax.sharding import PartitionSpec as P

BLK = 128
NX, NY, NZ, NCORE = 4, 4, 4, 2
NCOL = NZ * NCORE
NDEV = NX * NY * NCOL
LOCAL = 5
ROWS = LOCAL * BLK
NAUX, OCC = 32, 256
WIDTH = NAUX * OCC
PIECE = BLK // NCOL
PART = LOCAL * PIECE
NSL = 8
SLW = WIDTH // NSL
SLOTS = LOCAL * NX * NY // NCOL
AXES = ("row", "col")

UNITS = (
    ((0, 0), (0, 0), None),
    ((0, 1), (1, 0), (0, 0)),
    ((1, 0), (0, 1), (0, 0)),
    ((3, 0), (3, 0), (0, 0)),
    ((0, 3), (0, 3), (0, 0)),
    ((1, 1), (1, 1), (1, 1)),
    ((2, 0), (2, 0), (3, 3)),
    ((1, 3), (1, 3), (2, 1)),
    ((2, 1), (2, 1), (5, 5)),
    ((1, 2), (1, 2), (5, 5)),
    ((0, 2), (2, 2), (4, 8)),
    ((2, 2), (0, 2), (9, 9)),
)
BACK = (5, 7, 8, 9)
GROUPS = ((0, 1, 2, 3, 4), (5,), (6, 7), (8, 9), (10, 11))
BATCHES = (
    (("U", 0), ("U", 1), ("U", 2), ("U", 3), ("U", 4), ("U", 5), ("V", 5), ("U", 6), ("U", 7)),
    (("V", 7), ("U", 8), ("U", 9), ("U", 10), ("U", 11), ("V", 8), ("V", 9)),
)
ENTRIES = tuple(entry for batch in BATCHES for entry in batch)


def dev(x, y, col):
    return (x * NY + y) * NCOL + col


def shifted(moves):
    return [
        (dev(x, y, col), dev((x + moves[col % 2][0]) % NX, (y + moves[col % 2][1]) % NY, col))
        for x in range(NX)
        for y in range(NY)
        for col in range(NCOL)
    ]


def step_to(unit):
    moves = []
    for core in range(NCORE):
        here, there = UNITS[unit][core], UNITS[UNITS[unit][2][core]][core]
        moves.append(((here[0] - there[0]) % NX, (here[1] - there[1]) % NY))
    return moves


def step_back(unit):
    return [(-UNITS[unit][core][0] % NX, -UNITS[unit][core][1] % NY) for core in range(NCORE)]


def other_row(kind, unit, core, x, y):
    m = UNITS[unit][core]
    sign = -1 if kind == "U" else 1
    return (x + sign * m[0]) % NX * NY + (y + sign * m[1]) % NY


@functools.cache
def tables():
    sizes = []
    filled = {}
    for n, batch in enumerate(BATCHES):
        for x in range(NX):
            for y in range(NY):
                for core in range(NCORE):
                    classes = {c: [] for c in range(NCOL)}
                    for kind, unit in batch:
                        row = other_row(kind, unit, core, x, y)
                        for block in range(LOCAL * row, LOCAL * row + LOCAL):
                            classes[block % NCOL].append((block, kind))
                    filled[x, y, n, core] = {c: sorted(v) for c, v in classes.items()}
                assert filled[x, y, n, 0] == filled[x, y, n, 1]
        sizes.append(max(len(v) for k, f in filled.items() if k[2] == n for v in f.values()))
    rows = []
    for x in range(NX):
        for y in range(NY):
            for col in range(NCOL):
                values = [x * NY + y, col]
                for n, batch in enumerate(BATCHES):
                    classes = filled[x, y, n, col % 2]
                    for kind, unit in batch:
                        row = other_row(kind, unit, col % 2, x, y)
                        for block in range(LOCAL * row, LOCAL * row + LOCAL):
                            target = block % NCOL
                            values.append(target * sizes[n] + classes[target].index((block, kind)))
                for n in range(len(BATCHES)):
                    held = filled[x, y, n, col % 2][col]
                    for slot in range(sizes[n]):
                        if slot < len(held):
                            values += [held[slot][0] // NCOL, int(held[slot][1] == "V")]
                        else:
                            values += [0, 2]
                rows.append(values)
    return tuple(sizes), np.asarray(rows, np.int32)


T_PIECES = 2
T_SLOTS = T_PIECES + LOCAL * len(ENTRIES)


def masked(x, start, end):
    orbital = lax.broadcasted_iota(jnp.int32, x.shape, 2)
    inside = (orbital >= start) & (orbital < end)
    return jnp.where(inside, x.astype(jnp.float32), 0.0).astype(jnp.bfloat16)


def in_vmem(value):
    return pltpu.with_memory_space_constraint(value, pltpu.VMEM)


def in_hbm(value):
    return pltpu.with_memory_space_constraint(value, pltpu.HBM)


VMEM_SPEC = pl.BlockSpec(memory_space=pltpu.VMEM)
HBM_SPEC = pl.BlockSpec(memory_space=pltpu.HBM)
SMEM_SPEC = pl.BlockSpec(memory_space=pltpu.SMEM)
MARK = jax.ShapeDtypeStruct((8, 128), jnp.float32)


def part_kernel(tab, start, end, x_ref, out_ref, raw, sems):
    def fetch(j):
        return pltpu.make_async_copy(x_ref.at[pl.ds(j * BLK + tab[1] * PIECE, PIECE)], raw.at[j], sems.at[j])

    for j in range(LOCAL):
        fetch(j).start()
    for j in range(LOCAL):
        fetch(j).wait()
        block = LOCAL * tab[0] + j
        values = masked(raw[j], start[block], end[block])
        out_ref[j * PIECE : (j + 1) * PIECE, :] = values.reshape(PIECE, WIDTH)


def own_part(scalars, coefficients):
    return pl.pallas_call(
        part_kernel,
        in_specs=[SMEM_SPEC] * 3 + [HBM_SPEC],
        out_specs=VMEM_SPEC,
        out_shape=pltpu.VMEM((PART, WIDTH), jnp.bfloat16),
        scratch_shapes=[pltpu.VMEM((LOCAL, PIECE, NAUX, OCC), jnp.bfloat16), pltpu.SemaphoreType.DMA((LOCAL,))],
        compiler_params=pltpu.CompilerParams(vmem_limit_bytes=6 << 20),
        cost_estimate=pl.CostEstimate(flops=0, bytes_accessed=5 << 19, transcendentals=0),
        name="own_part",
    )(*scalars, in_hbm(coefficients))


CHUNK = 64


def rows_kernel(tab, start, end, x_ref, out_ref, mark_ref, raw, sems):
    steps = ROWS // CHUNK
    mark_ref[...] = jnp.zeros_like(mark_ref)

    def fetch(n):
        return pltpu.make_async_copy(x_ref.at[pl.ds(n * CHUNK, CHUNK)], raw.at[lax.rem(n, 4)], sems.at[lax.rem(n, 4)])

    for n in range(3):
        fetch(n).start()

    def step(n, carry):
        @pl.when(n + 3 < steps)
        def _():
            fetch(n + 3).start()

        fetch(n).wait()
        block = LOCAL * tab[0] + lax.div(n, BLK // CHUNK)
        values = masked(raw[lax.rem(n, 4)], start[block], end[block]).reshape(CHUNK, WIDTH)
        at = pl.ds(pl.multiple_of(n * CHUNK, CHUNK), CHUNK)
        for s in range(NSL):
            out_ref[s, at, :] = values[:, s * SLW : (s + 1) * SLW]
        return carry

    lax.fori_loop(0, steps, step, 0)


def own_rows(scalars, coefficients):
    return pl.pallas_call(
        rows_kernel,
        in_specs=[SMEM_SPEC] * 3 + [HBM_SPEC],
        out_specs=[VMEM_SPEC] * 2,
        out_shape=[pltpu.VMEM((NSL, ROWS, SLW), jnp.bfloat16), MARK],
        scratch_shapes=[pltpu.VMEM((4, CHUNK, NAUX, OCC), jnp.bfloat16), pltpu.SemaphoreType.DMA((4,))],
        compiler_params=pltpu.CompilerParams(vmem_limit_bytes=12 << 20),
        cost_estimate=pl.CostEstimate(flops=0, bytes_accessed=20 << 20, transcendentals=0),
        name="own_rows",
    )(*scalars, in_hbm(coefficients))


def product_kernel(n, *refs):
    parts, rows, outs, mark_ref, acc = refs[:n], refs[n], refs[n + 2 : 2 * n + 2], refs[2 * n + 2], refs[2 * n + 3]
    mark_ref[...] = jnp.zeros_like(mark_ref)
    for s in range(NSL):
        left = jnp.concatenate([part[:, s * SLW : (s + 1) * SLW] for part in parts], axis=0)
        term = lax.dot_general(left, rows[s], (((1,), (1,)), ((), ())), preferred_element_type=jnp.float32)
        if s == 0:
            acc[...] = term
        else:
            acc[...] += term
    for i, out in enumerate(outs):
        out[...] = acc[i * PART : (i + 1) * PART, :]


def products(parts, rows, token):
    n = len(parts)
    return pl.pallas_call(
        functools.partial(product_kernel, n),
        in_specs=[VMEM_SPEC] * (n + 1) + [pl.BlockSpec(memory_space=pl.ANY)],
        out_specs=[VMEM_SPEC] * (n + 1),
        out_shape=[pltpu.VMEM((PART, ROWS), jnp.float32)] * n + [MARK],
        scratch_shapes=[pltpu.VMEM((n * PART, ROWS), jnp.float32)],
        compiler_params=pltpu.CompilerParams(vmem_limit_bytes=12 << 20),
        cost_estimate=pl.CostEstimate(
            flops=2 * n * PART * ROWS * WIDTH, bytes_accessed=(10 << 20) + n * (3 << 19), transcendentals=0
        ),
        name="products",
    )(*[in_vmem(part) for part in parts], in_vmem(rows), token)


def pack_kernel(first, batch, tab, *refs):
    *parts, _, out_ref, mark_ref = refs
    mark_ref[...] = jnp.zeros_like(mark_ref)
    for n, (kind, _) in enumerate(batch):
        part = parts[n]
        for j in range(LOCAL):
            where = tab[T_PIECES + LOCAL * (first + n) + j]
            if kind == "V":
                out_ref[where] = part[:, j * BLK : (j + 1) * BLK]
                continue
            for k in range(LOCAL):
                piece = part[j * PIECE : (j + 1) * PIECE, k * BLK : (k + 1) * BLK]
                out_ref[where, k * PIECE : (k + 1) * PIECE, :] = piece


def pack(tab, first, batch, size, parts, token):
    return pl.pallas_call(
        functools.partial(pack_kernel, first, batch),
        in_specs=[SMEM_SPEC] + [VMEM_SPEC] * len(parts) + [pl.BlockSpec(memory_space=pl.ANY)],
        out_specs=[VMEM_SPEC] * 2,
        out_shape=[pltpu.VMEM((NCOL * size, PART, BLK), jnp.float32), MARK],
        compiler_params=pltpu.CompilerParams(vmem_limit_bytes=4 << 20),
        cost_estimate=pl.CostEstimate(flops=0, bytes_accessed=3 << 20, transcendentals=0),
        name="pack",
    )(tab, *[in_vmem(part) for part in parts], token)


def place_kernel(sizes, tab, flags, *refs):
    n_in = len(sizes)
    pieces, out_ref, made, sems = refs[:n_in], refs[n_in], refs[n_in + 1], refs[n_in + 2]

    def send(k):
        return pltpu.make_async_copy(made.at[k], out_ref.at[pl.ds(k * BLK * SLOTS, BLK * SLOTS), :], sems.at[k])

    for k in range(LOCAL):
        at = T_SLOTS
        for ref, size in zip(pieces, sizes):
            for n in range(size):
                slot, kind = tab[at], tab[at + 1]
                at += 2
                weight = flags[SLOTS * k + slot].astype(jnp.float32)

                def tile(ref=ref, n=n, size=size, weight=weight):
                    found = [ref[c * size + n, k * PIECE : (k + 1) * PIECE, :] for c in range(NCOL)]
                    return jnp.concatenate(found, axis=0) * weight

                @pl.when(kind == 0)
                def _(slot=slot, tile=tile):
                    made[k, pl.ds(slot, BLK, stride=SLOTS), :] = tile().T

                @pl.when(kind == 1)
                def _(slot=slot, tile=tile):
                    made[k, pl.ds(slot, BLK, stride=SLOTS), :] = tile()

        send(k).start()
    for k in range(LOCAL):
        send(k).wait()


def place(tab, flags, sizes, pieces):
    return pl.pallas_call(
        functools.partial(place_kernel, sizes),
        in_specs=[SMEM_SPEC] * 2 + [VMEM_SPEC] * len(sizes),
        out_specs=HBM_SPEC,
        out_shape=jax.ShapeDtypeStruct((ROWS * SLOTS, BLK), jnp.float32),
        scratch_shapes=[pltpu.VMEM((LOCAL, BLK * SLOTS, BLK), jnp.float32), pltpu.SemaphoreType.DMA((LOCAL,))],
        compiler_params=pltpu.CompilerParams(vmem_limit_bytes=8 << 20),
        cost_estimate=pl.CostEstimate(flops=0, bytes_accessed=7 << 20, transcendentals=0),
        name="place",
    )(tab, flags, *[in_vmem(piece) for piece in pieces])


def flags_kernel(tab, pairs_ref, out_ref):
    first = jnp.minimum(pairs_ref[0:1, :], pairs_ref[1:2, :])
    second = jnp.maximum(pairs_ref[0:1, :], pairs_ref[1:2, :])
    codes = first * 256 + second
    for i in range(LOCAL):
        a = LOCAL * tab[0] + i
        for slot in range(SLOTS):
            b = tab[1] + NCOL * slot
            wanted = jnp.minimum(a, b) * 256 + jnp.maximum(a, b)
            out_ref[SLOTS * i + slot] = jnp.max((codes == wanted).astype(jnp.int32))


def listed_flags(tab, pair_list):
    return pl.pallas_call(
        flags_kernel,
        in_specs=[SMEM_SPEC, VMEM_SPEC],
        out_specs=SMEM_SPEC,
        out_shape=jax.ShapeDtypeStruct((LOCAL * SLOTS,), jnp.int32),
        compiler_params=pltpu.CompilerParams(vmem_limit_bytes=1 << 20),
        cost_estimate=pl.CostEstimate(flops=1 << 20, bytes_accessed=1 << 14, transcendentals=0),
        name="listed_flags",
    )(tab, pair_list.T)


def choose_kernel(tab, even_ref, odd_ref, out_ref, sem):
    core = lax.rem(tab[1], NCORE)
    for which, ref in enumerate((even_ref, odd_ref)):

        @pl.when(core == which)
        def _(ref=ref):
            pltpu.make_async_copy(ref, out_ref, sem).start()

    pltpu.make_async_copy(even_ref, out_ref, sem).wait()


def choose(tab, even, odd):
    return pl.pallas_call(
        choose_kernel,
        in_specs=[SMEM_SPEC] + [pl.BlockSpec(memory_space=pl.ANY)] * 2,
        out_specs=VMEM_SPEC,
        out_shape=pltpu.VMEM((PART, WIDTH), jnp.bfloat16),
        scratch_shapes=[pltpu.SemaphoreType.DMA],
        compiler_params=pltpu.CompilerParams(vmem_limit_bytes=4 << 20),
        cost_estimate=pl.CostEstimate(flops=0, bytes_accessed=5 << 19, transcendentals=0),
        name="choose",
    )(tab, even, odd)


def per_device(coefficients, range_start, range_end, pair_list):
    sizes, table = tables()
    row, col = lax.axis_index("row"), lax.axis_index("col")
    tab = lax.dynamic_index_in_dim(jnp.asarray(table), row * NCOL + col, 0, keepdims=False)
    scalars = (in_hbm(tab), in_hbm(range_start), in_hbm(range_end))
    held = {0: own_part(scalars, coefficients)}
    rows, token = own_rows(scalars, coefficients)
    flags = listed_flags(tab, pair_list)
    made = {}

    def send(unit):
        a, b = UNITS[unit][2]
        source = held[a] if a == b else choose(tab, held[a], held[b])
        held[unit] = lax.ppermute(source, AXES, shifted(step_to(unit)))

    def multiply(group, token):
        *results, token = products([held[u] for u in group], rows, token)
        for unit, product in zip(group, results):
            made["U", unit] = product
            if unit in BACK:
                made["V", unit] = lax.ppermute(product, AXES, shifted(step_back(unit)))
        return token

    def gate(units, token):
        *values, token = lax.optimization_barrier((*[held[u] for u in units], token))
        held.update(zip(units, values))
        return token

    for unit in (1, 2, 3, 4):
        send(unit)
    token = gate((1, 2, 3, 4), token)
    for unit in (5, 6, 7):
        send(unit)
    token = multiply(GROUPS[0], token)
    token = gate((5,), token)
    send(8)
    send(9)
    token = multiply(GROUPS[1], token)
    token = multiply(GROUPS[2], token)
    message, token = pack(tab, 0, BATCHES[0], sizes[0], [made[entry] for entry in BATCHES[0]], token)
    pieces = [lax.all_to_all(message, "col", 0, 0, tiled=True)]
    token = gate((8, 9), token)
    send(11)
    send(10)
    token = multiply(GROUPS[3], token)
    token = multiply(GROUPS[4], token)
    message, _ = pack(tab, len(BATCHES[0]), BATCHES[1], sizes[1], [made[entry] for entry in BATCHES[1]], token)
    pieces.append(lax.all_to_all(message, "col", 0, 0, tiled=True))
    return place(tab, flags, sizes, pieces).reshape(ROWS, SLOTS, 1, BLK)


def solution(mesh):
    in_specs = (P("row", None, None), P(), P(), P())
    out_specs = P("row", None, "col", None)
    return jax.shard_map(per_device, mesh=mesh, in_specs=in_specs, out_specs=out_specs, check_vma=False)
```

time: 175 us -> 165 us (0.943)
  waiting for transfers between devices: 43.1 us -> 75.2 us
  Pallas kernels: 69.8 us -> 42.6 us
  starting transfers between devices: 49.6 us -> 36.4 us
  other arithmetic: 4.19 us -> 0 us
  local copies, waits for them, and re-layouts: 7.17 us -> 10.2 us
    pallas_call x11 -> x13, Pallas kernels: 69.8 us -> 42.6 us  [the longest x5 21.4 us: products(): pl.pallas_call(functools.partial(product_kernel, n), in_specs=[VMEM_SPEC]...]
    ppermute x11, waiting for transfers between devices: 16.2 us -> 42.2 us  [send(): held[unit] = lax.ppermute(source, AXES, shifted(step_to(unit)))]
    all_to_all x3 -> x2, starting transfers between devices: 26.7 us -> 13.1 us  [the longest x1 7.56 us: per_device(): pieces = [lax.all_to_all(message, 'col', 0, 0, tiled=True)]]
    ppermute x4, starting transfers between devices: 6.5 us -> 12.4 us  [multiply(): made['V', unit] = lax.ppermute(product, AXES, shifted(step_back(unit)))]
    ppermute x4, waiting for transfers between devices: 3.8 us -> 9.74 us  [multiply(): made['V', unit] = lax.ppermute(product, AXES, shifted(step_back(unit)))]
    ppermute x11, starting transfers between devices: 16.4 us -> 10.8 us  [send(): held[unit] = lax.ppermute(source, AXES, shifted(step_to(unit)))]
    select_n x2 -> x0, other arithmetic: 3.82 us -> none  [send(): source = held[a] if a == b else jnp.where(col % 2 == 0, held[a], held[b])]
    unnamed x42 -> x16, local copies, waits for them, and re-layouts: 5.92 us -> 9.04 us
  transfers between devices with their start and end apart: 18 -> 17, of which waited for: 8 -> 11; matrix products, arithmetic and copies ran while one was open for 2% -> 0% of each run, Pallas kernels for 34% -> 21%
where the time goes in v4:
time: 165 us
  waiting for transfers between devices  75.2 us (46%)
  Pallas kernels  42.6 us (26%)
  starting transfers between devices  36.4 us (22%)
  local copies, waits for them, and re-layouts  10.2 us (6%)
    ppermute x11, waiting for transfers between devices, send(): held[unit] = lax.ppermute(source, AXES, shifted(step_to(unit)))  42.2 us
    all_to_all x1, waiting for transfers between devices, per_device(): pieces.append(lax.all_to_all(message, 'col', 0, 0, tiled=True))  23.2 us
    pallas_call x5, Pallas kernels, products(): pl.pallas_call(functools.partial(product_kernel, n), in_specs=[VMEM_SPEC]...  21.4 us
    ppermute x4, starting transfers between devices, multiply(): made['V', unit] = lax.ppermute(product, AXES, shifted(step_back(unit)))  12.4 us
    ppermute x11, starting transfers between devices, send(): held[unit] = lax.ppermute(source, AXES, shifted(step_to(unit)))  10.8 us
    ppermute x4, waiting for transfers between devices, multiply(): made['V', unit] = lax.ppermute(product, AXES, shifted(step_back(unit)))  9.74 us
    unnamed x16, local copies, waits for them, and re-layouts  9.04 us
    all_to_all x1, starting transfers between devices, per_device(): pieces = [lax.all_to_all(message, 'col', 0, 0, tiled=True)]  7.56 us
  transfers between devices with their start and end apart: 17, of which 11 were waited for; matrix products, arithmetic and copies ran while one was open for 0% of the time, Pallas kernels for 21%

profile of v4, /device:TPU:1, one launch (start us, length us, event | category | flops | bytes accessed | tf_op | source)
XLA Modules:
  0.0 164.7 jit_solution(12775046544879063680)
XLA Ops:
  1.2 2.2 %own_part.1.refs_0_ = bf16[80,8192]{1,0:T(8,128)(2,1)S(1)} custom-call(s32[108]{0:T(128)} %dynamic-slice_bitcast_fusion.tab, s32[80]{0:T(128)} %start.3, s32[80]{0:T(128)} %end.3, bf16[640,32,256]{2,1,0:T(8,128)(2,1)} %x_ref.3), custom_call_target="tpu_custom_call" | custom-call | bytes 2621440 | tf_op jit(solution)/shard_map/own_part/pallas_call | solution.py:157
  3.5 3.6 %collective-permute-start.3 = (bf16[80,8192]{1,0:T(8,128)(2,1)S(1)}, bf16[80,8192]{1,0:T(8,128)(2,1)S(1)}, u32[]{:S(2)}, u32[]{:S(2)}) collective-permute-start(bf16[80,8192]{1,0:T(8,128)(2,1)S(1)} %own_part.1.refs_0_), channel_id=1, source_target_pairs={{0,24},{1,25},{2,26},{3,27},{4,28},{5,29},{6,30},{7,31},{8,0},{9,1... | collective-permute-start | bytes 3932168 | tf_op jit(solution)/shard_map/ppermute | solution.py:374
  7.1 2.5 %collective-permute-start.2 = (bf16[80,8192]{1,0:T(8,128)(2,1)S(1)}, bf16[80,8192]{1,0:T(8,128)(2,1)S(1)}, u32[]{:S(2)}, u32[]{:S(2)}) collective-permute-start(bf16[80,8192]{1,0:T(8,128)(2,1)S(1)} %own_part.1.refs_0_), channel_id=1, source_target_pairs={{0,96},{1,97},{2,98},{3,99},{4,100},{5,101},{6,102},{7,103},{8,104... | collective-permute-start | bytes 3932168 | tf_op jit(solution)/shard_map/ppermute | solution.py:374
  9.6 6.4 %own_rows.1 = (bf16[8,640,1024]{2,1,0:T(8,128)(2,1)S(1)}, f32[8,128]{1,0:T(8,128)S(1)}) custom-call(s32[108]{0:T(128)} %dynamic-slice_bitcast_fusion.tab, s32[80]{0:T(128)} %start.3, s32[80]{0:T(128)} %end.3, bf16[640,32,256]{2,1,0:T(8,128)(2,1)} %x_ref.3), custom_call_target="tpu_custom_call" | custom-call | bytes 20971520 | tf_op jit(solution)/shard_map/own_rows/pallas_call | solution.py:199
  16.0 18.6 %collective-permute-done.3.refs_4_.even_ref = bf16[80,8192]{1,0:T(8,128)(2,1)S(1)} collective-permute-done((bf16[80,8192]{1,0:T(8,128)(2,1)S(1)}, bf16[80,8192]{1,0:T(8,128)(2,1)S(1)}, u32[]{:S(2)}, u32[]{:S(2)}) %collective-permute-start.3) | collective-permute-done | bytes 1310752 | tf_op jit(solution)/shard_map/ppermute | solution.py:374
  36.7 3.1 %collective-permute-done.1.refs_2_.even_ref = bf16[80,8192]{1,0:T(8,128)(2,1)S(1)} collective-permute-done((bf16[80,8192]{1,0:T(8,128)(2,1)S(1)}, bf16[80,8192]{1,0:T(8,128)(2,1)S(1)}, u32[]{:S(2)}, u32[]{:S(2)}) %collective-permute-start.1) | collective-permute-done | bytes 1310752 | tf_op jit(solution)/shard_map/ppermute | solution.py:374
  44.2 5.2 %products.5 = (f32[80,640]{1,0:T(8,128)S(1)}, f32[80,640]{1,0:T(8,128)S(1)}, f32[80,640]{1,0:T(8,128)S(1)}, f32[80,640]{1,0:T(8,128)S(1)}, f32[80,640]{1,0:T(8,128)S(1)}, /*index=5*/f32[8,128]{1,0:T(8,128)S(1)}) custom-call(bf16[80,8192]{1,0:T(8,128)(2,1)S(1)} %own_part.1.refs_0_, bf16[80,8192]{1,0:T(8,128)(2,1)S(1)} %collective-permute-done.refs_1_.odd_ref, ...), custom_call_target="tpu_custom_call" | custom-call | flops 4194304000 | bytes 18350080 | tf_op jit(solution)/shard_map/products/pallas_call | solution.py:227
  50.5 8.3 %collective-permute-done.4.refs_0_ = bf16[80,8192]{1,0:T(8,128)(2,1)} collective-permute-done((bf16[80,8192]{1,0:T(8,128)(2,1)S(1)}, bf16[80,8192]{1,0:T(8,128)(2,1)}, u32[]{:S(2)}, u32[]{:S(2)}) %collective-permute-start.4) | collective-permute-done | bytes 1310752 | tf_op jit(solution)/shard_map/ppermute | solution.py:374
  58.8 4.6 %products.6 = (f32[80,640]{1,0:T(8,128)S(1)}, f32[8,128]{1,0:T(8,128)S(1)}) custom-call(bf16[80,8192]{1,0:T(8,128)(2,1)} %collective-permute-done.4.refs_0_, bf16[8,640,1024]{2,1,0:T(8,128)(2,1)S(1)} %get-tuple-element.42.refs_5_.refs_1_.refs_2_, f32[8,128]{1,0:T(8,128)S(1)} %get-tuple-element.51.refs_2_), custom_call_target="tpu_custom_call" | custom-call | flops 838860800 | bytes 12058624 | tf_op jit(solution)/shard_map/products/pallas_call | solution.py:227
  63.5 5.3 %collective-permute-start.5 = (f32[80,640]{1,0:T(8,128)S(1)}, f32[80,640]{1,0:T(8,128)S(1)}, u32[]{:S(2)}, u32[]{:S(2)}) collective-permute-start(f32[80,640]{1,0:T(8,128)S(1)} %get-tuple-element.52.refs_5_), channel_id=1, source_target_pairs={{0,120},{1,121},{2,122},{3,123},{4,124},{5,125},{6,126},{7,127},{8... | collective-permute-start | bytes 614408 | tf_op jit(solution)/shard_map/ppermute | solution.py:381
  68.8 3.4 %collective-permute-done.7.refs_1_ = bf16[80,8192]{1,0:T(8,128)(2,1)S(1)} collective-permute-done((bf16[80,8192]{1,0:T(8,128)(2,1)S(1)}, bf16[80,8192]{1,0:T(8,128)(2,1)S(1)}, u32[]{:S(2)}, u32[]{:S(2)}) %collective-permute-start.7) | collective-permute-done | bytes 1310752 | tf_op jit(solution)/shard_map/ppermute | solution.py:374
  74.1 3.2 %products.7 = (f32[80,640]{1,0:T(8,128)S(1)}, f32[80,640]{1,0:T(8,128)S(1)}, f32[8,128]{1,0:T(8,128)S(1)}) custom-call(bf16[80,8192]{1,0:T(8,128)(2,1)S(1)} %collective-permute-done.6.refs_0_, bf16[80,8192]{1,0:T(8,128)(2,1)S(1)} %collective-permute-done.7.refs_1_, bf16[8,640,1024]{2,1,0:T(8,128)(2,1)S(1)} %get-tuple-element.42.refs_5_.refs_1_.refs_2_, ...), custom_call_target="tpu_custom_call" | custom-call | flops 1677721600 | bytes 13631488 | tf_op jit(solution)/shard_map/products/pallas_call | solution.py:227
  79.4 7.6 %all-to-all-start = ((f32[56,80,128]{2,1,0:T(8,128)}), f32[56,80,128]{2,1,0:T(8,128)S(1)}, u32[]{:S(2)}, u32[]{:S(2)}) async-start(f32[56,80,128]{2,1,0:T(8,128)} %copy-done.4), calls=%async_computation | async-start | bytes 4587520 | tf_op jit(solution)/shard_map/all_to_all | solution.py:401
  93.4 4.0 %copy-done.1 = bf16[8,640,1024]{2,1,0:T(8,128)(2,1)S(1)} copy-done((bf16[8,640,1024]{2,1,0:T(8,128)(2,1)S(1)}, bf16[8,640,1024]{2,1,0:T(8,128)(2,1)}, u32[]{:S(2)}) %copy-start.1) | copy-done | bytes 10485784
  97.4 5.0 %products.8 = (f32[80,640]{1,0:T(8,128)S(1)}, f32[80,640]{1,0:T(8,128)S(1)}, f32[8,128]{1,0:T(8,128)S(1)}) custom-call(bf16[80,8192]{1,0:T(8,128)(2,1)} %collective-permute-done.9.refs_0_.odd_ref, bf16[80,8192]{1,0:T(8,128)(2,1)} %collective-permute-done.10.refs_1_, bf16[8,640,1024]{2,1,0:T(8,128)(2,1)S(1)} %copy-done.1, f32[8,128]{1,0:T(8,128)S(1)} %get-tuple-element.61.refs_3_), custom_call_target="tpu_custom_call" | custom-call | flops 1677721600 | bytes 13631488 | tf_op jit(solution)/shard_map/products/pallas_call | solution.py:227
  102.3 4.0 %collective-permute-start.13 = (f32[80,640]{1,0:T(8,128)S(1)}, f32[80,640]{1,0:T(8,128)S(1)}, u32[]{:S(2)}, u32[]{:S(2)}) collective-permute-start(f32[80,640]{1,0:T(8,128)S(1)} %get-tuple-element.62.refs_1_), channel_id=1, source_target_pairs={{0,88},{1,89},{2,90},{3,91},{4,92},{5,93},{6,94},{7,95},{8,64},{9,... | collective-permute-start | bytes 614408 | tf_op jit(solution)/shard_map/ppermute | solution.py:381
  106.3 2.6 %collective-permute-start.14 = (f32[80,640]{1,0:T(8,128)S(1)}, f32[80,640]{1,0:T(8,128)S(1)}, u32[]{:S(2)}, u32[]{:S(2)}) collective-permute-start(f32[80,640]{1,0:T(8,128)S(1)} %get-tuple-element.63.refs_2_), channel_id=1, source_target_pairs={{0,112},{1,113},{2,114},{3,115},{4,116},{5,117},{6,118},{7,119},{8... | collective-permute-start | bytes 614408 | tf_op jit(solution)/shard_map/ppermute | solution.py:381
  108.9 3.1 %collective-permute-done.11.refs_0_ = bf16[80,8192]{1,0:T(8,128)(2,1)S(1)} collective-permute-done((bf16[80,8192]{1,0:T(8,128)(2,1)S(1)}, bf16[80,8192]{1,0:T(8,128)(2,1)S(1)}, u32[]{:S(2)}, u32[]{:S(2)}) %collective-permute-start.11) | collective-permute-done | bytes 1310752 | tf_op jit(solution)/shard_map/ppermute | solution.py:374
  112.0 3.3 %products.9 = (f32[80,640]{1,0:T(8,128)S(1)}, f32[80,640]{1,0:T(8,128)S(1)}, f32[8,128]{1,0:T(8,128)S(1)}) custom-call(bf16[80,8192]{1,0:T(8,128)(2,1)S(1)} %collective-permute-done.11.refs_0_, bf16[80,8192]{1,0:T(8,128)(2,1)S(1)} %collective-permute-done.12.refs_1_, bf16[8,640,1024]{2,1,0:T(8,128)(2,1)S(1)} %copy-done.1, f32[8,128]{1,0:T(8,128)S(1)} %get-tuple-element.64.refs_3_), custom_call_target="tpu_custom_call" | custom-call | flops 1677721600 | bytes 13631488 | tf_op jit(solution)/shard_map/products/pallas_call | solution.py:227
  115.3 4.5 %collective-permute-done.8.refs_0_ = f32[80,640]{1,0:T(8,128)S(1)} collective-permute-done((f32[80,640]{1,0:T(8,128)S(1)}, f32[80,640]{1,0:T(8,128)S(1)}, u32[]{:S(2)}, u32[]{:S(2)}) %collective-permute-start.8) | collective-permute-done | bytes 204832 | tf_op jit(solution)/shard_map/ppermute | solution.py:381
  119.7 5.3 %collective-permute-done.14.refs_6_ = f32[80,640]{1,0:T(8,128)S(1)} collective-permute-done((f32[80,640]{1,0:T(8,128)S(1)}, f32[80,640]{1,0:T(8,128)S(1)}, u32[]{:S(2)}, u32[]{:S(2)}) %collective-permute-start.14) | collective-permute-done | bytes 204832 | tf_op jit(solution)/shard_map/ppermute | solution.py:381
  127.5 5.6 %all-to-all-start.1 = ((f32[48,80,128]{2,1,0:T(8,128)}), f32[48,80,128]{2,1,0:T(8,128)}, u32[]{:S(2)}, u32[]{:S(2)}) async-start(f32[48,80,128]{2,1,0:T(8,128)} %copy-done.5), calls=%async_computation.1 | async-start | bytes 3932160 | tf_op jit(solution)/shard_map/all_to_all | solution.py:408
  134.9 23.2 %all-to-all-done.1.refs_1_ = f32[48,80,128]{2,1,0:T(8,128)} async-done(((f32[48,80,128]{2,1,0:T(8,128)}), f32[48,80,128]{2,1,0:T(8,128)}, u32[]{:S(2)}, u32[]{:S(2)}) %all-to-all-start.1) | async-done | bytes 1966112 | tf_op jit(solution)/shard_map/all_to_all | solution.py:408
  158.1 6.5 %place.1 = f32[6400,128]{1,0:T(8,128)} custom-call(s32[108]{0:T(128)S(1)} %copy-done.6, s32[50]{0:T(128)S(1)} %listed_flags.1.flags, f32[56,80,128]{2,1,0:T(8,128)S(1)} %all-to-all-done.refs_0_, f32[48,80,128]{2,1,0:T(8,128)} %all-to-all-done.1.refs_1_), custom_call_target="tpu_custom_call" | custom-call | bytes 7340032 | tf_op jit(solution)/shard_map/place/pallas_call | solution.py:301
  (40 shorter events, 23.5 us)
Async XLA Ops:
  3.4 37.9 %copy-start.6 = (s32[108]{0:T(128)S(1)}, s32[108]{0:T(128)}, u32[]{:S(2)}) copy-start(s32[108]{0:T(128)} %dynamic-slice_bitcast_fusion.tab) | copy-start | bytes 1300
  3.5 31.1 %collective-permute-start.3 = (bf16[80,8192]{1,0:T(8,128)(2,1)S(1)}, bf16[80,8192]{1,0:T(8,128)(2,1)S(1)}, u32[]{:S(2)}, u32[]{:S(2)}) collective-permute-start(bf16[80,8192]{1,0:T(8,128)(2,1)S(1)} %own_part.1.refs_0_), channel_id=1, source_target_pairs={{0,24},{1,25},{2,26},{3,27},{4,28},{5,29},{6,30},{7,31},{8,0},{9,1... | collective-permute-start | bytes 3932168 | tf_op jit(solution)/shard_map/ppermute | solution.py:374
  7.1 29.6 %collective-permute-start.2 = (bf16[80,8192]{1,0:T(8,128)(2,1)S(1)}, bf16[80,8192]{1,0:T(8,128)(2,1)S(1)}, u32[]{:S(2)}, u32[]{:S(2)}) collective-permute-start(bf16[80,8192]{1,0:T(8,128)(2,1)S(1)} %own_part.1.refs_0_), channel_id=1, source_target_pairs={{0,96},{1,97},{2,98},{3,99},{4,100},{5,101},{6,102},{7,103},{8,104... | collective-permute-start | bytes 3932168 | tf_op jit(solution)/shard_map/ppermute | solution.py:374
  9.6 30.2 %collective-permute-start.1 = (bf16[80,8192]{1,0:T(8,128)(2,1)S(1)}, bf16[80,8192]{1,0:T(8,128)(2,1)S(1)}, u32[]{:S(2)}, u32[]{:S(2)}) collective-permute-start(bf16[80,8192]{1,0:T(8,128)(2,1)S(1)} %own_part.1.refs_0_), channel_id=1, source_target_pairs={{0,32},{1,9},{2,34},{3,11},{4,36},{5,13},{6,38},{7,15},{8,40},{9,1... | collective-permute-start | bytes 3932168 | tf_op jit(solution)/shard_map/ppermute | solution.py:374
  9.6 30.2 %collective-permute-start = (bf16[80,8192]{1,0:T(8,128)(2,1)S(1)}, bf16[80,8192]{1,0:T(8,128)(2,1)S(1)}, u32[]{:S(2)}, u32[]{:S(2)}) collective-permute-start(bf16[80,8192]{1,0:T(8,128)(2,1)S(1)} %own_part.1.refs_0_), channel_id=1, source_target_pairs={{0,8},{1,33},{2,10},{3,35},{4,12},{5,37},{6,14},{7,39},{8,16},{9,4... | collective-permute-start | bytes 3932168 | tf_op jit(solution)/shard_map/ppermute | solution.py:374
  15.9 58.2 %copy-start = (bf16[8,640,1024]{2,1,0:T(8,128)(2,1)}, bf16[8,640,1024]{2,1,0:T(8,128)(2,1)S(1)}, u32[]{:S(2)}) copy-start(bf16[8,640,1024]{2,1,0:T(8,128)(2,1)S(1)} %get-tuple-element.42.refs_5_.refs_1_.refs_2_) | copy-start | bytes 31457284
  39.8 19.0 %collective-permute-start.4 = (bf16[80,8192]{1,0:T(8,128)(2,1)S(1)}, bf16[80,8192]{1,0:T(8,128)(2,1)}, u32[]{:S(2)}, u32[]{:S(2)}) collective-permute-start(bf16[80,8192]{1,0:T(8,128)(2,1)S(1)} %collective-permute-done.refs_1_.odd_ref), channel_id=1, source_target_pairs={{0,32},{1,9},{2,34},{3,11},{4,36},{5,13},{6,38},{7,15},{8,40},{9,1... | collective-permute-start | bytes 3932168 | tf_op jit(solution)/shard_map/ppermute | solution.py:374
  42.0 30.2 %collective-permute-start.7 = (bf16[80,8192]{1,0:T(8,128)(2,1)S(1)}, bf16[80,8192]{1,0:T(8,128)(2,1)S(1)}, u32[]{:S(2)}, u32[]{:S(2)}) collective-permute-start(bf16[80,8192]{1,0:T(8,128)(2,1)S(1)} %choose.2), channel_id=1, source_target_pairs={{0,24},{1,25},{2,26},{3,27},{4,28},{5,29},{6,30},{7,31},{8,0},{9,1... | collective-permute-start | bytes 3932168 | tf_op jit(solution)/shard_map/ppermute | solution.py:374
  44.2 29.9 %collective-permute-start.6 = (bf16[80,8192]{1,0:T(8,128)(2,1)S(1)}, bf16[80,8192]{1,0:T(8,128)(2,1)S(1)}, u32[]{:S(2)}, u32[]{:S(2)}) collective-permute-start(bf16[80,8192]{1,0:T(8,128)(2,1)S(1)} %collective-permute-done.2.refs_3_), channel_id=1, source_target_pairs={{0,96},{1,97},{2,98},{3,99},{4,100},{5,101},{6,102},{7,103},{8,104... | collective-permute-start | bytes 3932168 | tf_op jit(solution)/shard_map/ppermute | solution.py:374
  58.8 29.7 %collective-permute-start.10 = (bf16[80,8192]{1,0:T(8,128)(2,1)}, bf16[80,8192]{1,0:T(8,128)(2,1)}, u32[]{:S(2)}, u32[]{:S(2)}) collective-permute-start(bf16[80,8192]{1,0:T(8,128)(2,1)} %collective-permute-done.4.refs_0_), channel_id=1, source_target_pairs={{0,8},{1,9},{2,10},{3,11},{4,12},{5,13},{6,14},{7,15},{8,16},{9,17... | collective-permute-start | bytes 3932168 | tf_op jit(solution)/shard_map/ppermute | solution.py:374
  58.8 29.7 %collective-permute-start.9 = (bf16[80,8192]{1,0:T(8,128)(2,1)}, bf16[80,8192]{1,0:T(8,128)(2,1)}, u32[]{:S(2)}, u32[]{:S(2)}) collective-permute-start(bf16[80,8192]{1,0:T(8,128)(2,1)} %collective-permute-done.4.refs_0_), channel_id=1, source_target_pairs={{0,32},{1,33},{2,34},{3,35},{4,36},{5,37},{6,38},{7,39},{8,40},{9,... | collective-permute-start | bytes 3932168 | tf_op jit(solution)/shard_map/ppermute | solution.py:374
  63.5 13.9 %collective-permute-start.5 = (f32[80,640]{1,0:T(8,128)S(1)}, f32[80,640]{1,0:T(8,128)S(1)}, u32[]{:S(2)}, u32[]{:S(2)}) collective-permute-start(f32[80,640]{1,0:T(8,128)S(1)} %get-tuple-element.52.refs_5_), channel_id=1, source_target_pairs={{0,120},{1,121},{2,122},{3,123},{4,124},{5,125},{6,126},{7,127},{8... | collective-permute-start | bytes 614408 | tf_op jit(solution)/shard_map/ppermute | solution.py:381
  78.0 1.4 copy-start.4
  79.4 48.0 %all-to-all-start = ((f32[56,80,128]{2,1,0:T(8,128)}), f32[56,80,128]{2,1,0:T(8,128)S(1)}, u32[]{:S(2)}, u32[]{:S(2)}) async-start(f32[56,80,128]{2,1,0:T(8,128)} %copy-done.4), calls=%async_computation | async-start | bytes 4587520 | tf_op jit(solution)/shard_map/all_to_all | solution.py:401
  88.6 1.3 copy-start.3
  91.8 20.2 %collective-permute-start.11 = (bf16[80,8192]{1,0:T(8,128)(2,1)S(1)}, bf16[80,8192]{1,0:T(8,128)(2,1)S(1)}, u32[]{:S(2)}, u32[]{:S(2)}) collective-permute-start(bf16[80,8192]{1,0:T(8,128)(2,1)S(1)} %choose.3), channel_id=1, source_target_pairs={{0,24},{1,9},{2,26},{3,11},{4,28},{5,13},{6,30},{7,15},{8,0},{9,17... | collective-permute-start | bytes 3932168 | tf_op jit(solution)/shard_map/ppermute | solution.py:374
  91.9 20.1 %collective-permute-start.12 = (bf16[80,8192]{1,0:T(8,128)(2,1)}, bf16[80,8192]{1,0:T(8,128)(2,1)S(1)}, u32[]{:S(2)}, u32[]{:S(2)}) collective-permute-start(bf16[80,8192]{1,0:T(8,128)(2,1)} %collective-permute-done.10.refs_1_), channel_id=1, source_target_pairs={{0,32},{1,97},{2,34},{3,99},{4,36},{5,101},{6,38},{7,103},{8,40},{... | collective-permute-start | bytes 3932168 | tf_op jit(solution)/shard_map/ppermute | solution.py:374
  92.8 26.9 %collective-permute-start.8 = (f32[80,640]{1,0:T(8,128)S(1)}, f32[80,640]{1,0:T(8,128)S(1)}, u32[]{:S(2)}, u32[]{:S(2)}) collective-permute-start(f32[80,640]{1,0:T(8,128)S(1)} %get-tuple-element.55.refs_8_), channel_id=1, source_target_pairs={{0,104},{1,105},{2,106},{3,107},{4,108},{5,109},{6,110},{7,111},{8... | collective-permute-start | bytes 614408 | tf_op jit(solution)/shard_map/ppermute | solution.py:381
  93.4 4.0 %copy-start.1 = (bf16[8,640,1024]{2,1,0:T(8,128)(2,1)S(1)}, bf16[8,640,1024]{2,1,0:T(8,128)(2,1)}, u32[]{:S(2)}) copy-start(bf16[8,640,1024]{2,1,0:T(8,128)(2,1)} %copy-done) | copy-start | bytes 31457284
  102.3 17.4 %collective-permute-start.13 = (f32[80,640]{1,0:T(8,128)S(1)}, f32[80,640]{1,0:T(8,128)S(1)}, u32[]{:S(2)}, u32[]{:S(2)}) collective-permute-start(f32[80,640]{1,0:T(8,128)S(1)} %get-tuple-element.62.refs_1_), channel_id=1, source_target_pairs={{0,88},{1,89},{2,90},{3,91},{4,92},{5,93},{6,94},{7,95},{8,64},{9,... | collective-permute-start | bytes 614408 | tf_op jit(solution)/shard_map/ppermute | solution.py:381
  106.3 18.7 %collective-permute-start.14 = (f32[80,640]{1,0:T(8,128)S(1)}, f32[80,640]{1,0:T(8,128)S(1)}, u32[]{:S(2)}, u32[]{:S(2)}) collective-permute-start(f32[80,640]{1,0:T(8,128)S(1)} %get-tuple-element.63.refs_2_), channel_id=1, source_target_pairs={{0,112},{1,113},{2,114},{3,115},{4,116},{5,117},{6,118},{7,119},{8... | collective-permute-start | bytes 614408 | tf_op jit(solution)/shard_map/ppermute | solution.py:381
  126.2 1.3 copy-start.5
  127.5 5.6 %copy-start.7 = (s32[1976,2]{0,1:T(2,128)S(1)}, s32[1976,2]{0,1:T(2,128)}, u32[]{:S(2)}) copy-start(s32[1976,2]{0,1:T(2,128)} %param.8) | copy-start | bytes 47428
  127.5 30.6 %all-to-all-start.1 = ((f32[48,80,128]{2,1,0:T(8,128)}), f32[48,80,128]{2,1,0:T(8,128)}, u32[]{:S(2)}, u32[]{:S(2)}) async-start(f32[48,80,128]{2,1,0:T(8,128)} %copy-done.5), calls=%async_computation.1 | async-start | bytes 3932160 | tf_op jit(solution)/shard_map/all_to_all | solution.py:408
  (1 other events, 1.1 us)

commit v5 on v4

--- a/solution.py
+++ b/solution.py
@@ -140,30 +140,32 @@
 MARK = jax.ShapeDtypeStruct((8, 128), jnp.float32)
 
 
-def part_kernel(tab, start, end, x_ref, out_ref, raw, sems):
+def part_kernel(start, end, x_ref, out_ref, raw, sems):
+    row, col = lax.axis_index("row"), lax.axis_index("col")
+
     def fetch(j):
-        return pltpu.make_async_copy(x_ref.at[pl.ds(j * BLK + tab[1] * PIECE, PIECE)], raw.at[j], sems.at[j])
+        return pltpu.make_async_copy(x_ref.at[pl.ds(j * BLK + col * PIECE, PIECE)], raw.at[j], sems.at[j])
 
     for j in range(LOCAL):
         fetch(j).start()
     for j in range(LOCAL):
         fetch(j).wait()
-        block = LOCAL * tab[0] + j
+        block = LOCAL * row + j
         values = masked(raw[j], start[block], end[block])
         out_ref[j * PIECE : (j + 1) * PIECE, :] = values.reshape(PIECE, WIDTH)
 
 
-def own_part(scalars, coefficients):
+def own_part(start, end, coefficients):
     return pl.pallas_call(
         part_kernel,
-        in_specs=[SMEM_SPEC] * 3 + [HBM_SPEC],
+        in_specs=[SMEM_SPEC] * 2 + [HBM_SPEC],
         out_specs=VMEM_SPEC,
         out_shape=pltpu.VMEM((PART, WIDTH), jnp.bfloat16),
         scratch_shapes=[pltpu.VMEM((LOCAL, PIECE, NAUX, OCC), jnp.bfloat16), pltpu.SemaphoreType.DMA((LOCAL,))],
         compiler_params=pltpu.CompilerParams(vmem_limit_bytes=6 << 20),
         cost_estimate=pl.CostEstimate(flops=0, bytes_accessed=5 << 19, transcendentals=0),
         name="own_part",
-    )(*scalars, in_hbm(coefficients))
+    )(start, end, in_hbm(coefficients))
 
 
 CHUNK = 64
@@ -238,76 +240,179 @@
     )(*[in_vmem(part) for part in parts], in_vmem(rows), token)
 
 
+def stream_kernel(n, *refs):
+    parts, rows, outs = refs[:n], refs[n], refs[n + 2 : 2 * n + 2]
+    mark_ref, left, right, acc, left_sem, right_sem = refs[2 * n + 2 :]
+    mark_ref[...] = jnp.zeros_like(mark_ref)
+
+    def copies(s):
+        span = pl.ds(s * SLW, SLW)
+        found = [pltpu.make_async_copy(rows.at[s], right.at[s], right_sem.at[s])]
+        for i, part in enumerate(parts):
+            target = left.at[s, pl.ds(i * PART, PART), :]
+            found.append(pltpu.make_async_copy(part.at[:, span], target, left_sem.at[i, s]))
+        return found
+
+    for s in range(NSL):
+        for copy in copies(s):
+            copy.start()
+    for s in range(NSL):
+        for copy in copies(s):
+            copy.wait()
+        term = lax.dot_general(left[s], right[s], (((1,), (1,)), ((), ())), preferred_element_type=jnp.float32)
+        if s == 0:
+            acc[...] = term
+        else:
+            acc[...] += term
+    for i, out in enumerate(outs):
+        out[...] = acc[i * PART : (i + 1) * PART, :]
+
+
+def stream_products(parts, rows, token):
+    n = len(parts)
+    return pl.pallas_call(
+        functools.partial(stream_kernel, n),
+        in_specs=[HBM_SPEC] * (n + 1) + [pl.BlockSpec(memory_space=pl.ANY)],
+        out_specs=[VMEM_SPEC] * (n + 1),
+        out_shape=[pltpu.VMEM((PART, ROWS), jnp.float32)] * n + [MARK],
+        scratch_shapes=[
+            pltpu.VMEM((NSL, n * PART, SLW), jnp.bfloat16),
+            pltpu.VMEM((NSL, ROWS, SLW), jnp.bfloat16),
+            pltpu.VMEM((n * PART, ROWS), jnp.float32),
+            pltpu.SemaphoreType.DMA((n, NSL)),
+            pltpu.SemaphoreType.DMA((NSL,)),
+        ],
+        compiler_params=pltpu.CompilerParams(vmem_limit_bytes=20 << 20),
+        cost_estimate=pl.CostEstimate(
+            flops=2 * n * PART * ROWS * WIDTH, bytes_accessed=(10 << 20) + n * (3 << 19), transcendentals=0
+        ),
+        name="stream_products",
+    )(*[in_hbm(part) for part in parts], in_hbm(rows), token)
+
+
+def touch_kernel(rows_ref, token_ref, mark_ref):
+    mark_ref[...] = jnp.zeros_like(mark_ref)
+
+
+def touch(rows, token):
+    return pl.pallas_call(
+        touch_kernel,
+        in_specs=[VMEM_SPEC, pl.BlockSpec(memory_space=pl.ANY)],
+        out_specs=VMEM_SPEC,
+        out_shape=MARK,
+        compiler_params=pltpu.CompilerParams(vmem_limit_bytes=1 << 20),
+        cost_estimate=pl.CostEstimate(flops=0, bytes_accessed=1 << 12, transcendentals=0),
+        name="touch",
+    )(in_vmem(rows), token)
+
+
 def pack_kernel(first, batch, tab, *refs):
-    *parts, _, out_ref, mark_ref = refs
+    *parts, _, out_ref, mark_ref, made, sem = refs
     mark_ref[...] = jnp.zeros_like(mark_ref)
     for n, (kind, _) in enumerate(batch):
         part = parts[n]
         for j in range(LOCAL):
             where = tab[T_PIECES + LOCAL * (first + n) + j]
             if kind == "V":
-                out_ref[where] = part[:, j * BLK : (j + 1) * BLK]
+                made[where] = part[:, j * BLK : (j + 1) * BLK]
                 continue
             for k in range(LOCAL):
                 piece = part[j * PIECE : (j + 1) * PIECE, k * BLK : (k + 1) * BLK]
-                out_ref[where, k * PIECE : (k + 1) * PIECE, :] = piece
+                made[where, k * PIECE : (k + 1) * PIECE, :] = piece
+    copy = pltpu.make_async_copy(made, out_ref, sem)
+    copy.start()
+    copy.wait()
 
 
 def pack(tab, first, batch, size, parts, token):
     return pl.pallas_call(
         functools.partial(pack_kernel, first, batch),
         in_specs=[SMEM_SPEC] + [VMEM_SPEC] * len(parts) + [pl.BlockSpec(memory_space=pl.ANY)],
-        out_specs=[VMEM_SPEC] * 2,
-        out_shape=[pltpu.VMEM((NCOL * size, PART, BLK), jnp.float32), MARK],
-        compiler_params=pltpu.CompilerParams(vmem_limit_bytes=4 << 20),
+        out_specs=[HBM_SPEC, VMEM_SPEC],
+        out_shape=[pltpu.HBM((NCOL * size, PART, BLK), jnp.float32), MARK],
+        scratch_shapes=[pltpu.VMEM((NCOL * size, PART, BLK), jnp.float32), pltpu.SemaphoreType.DMA],
+        compiler_params=pltpu.CompilerParams(vmem_limit_bytes=6 << 20),
         cost_estimate=pl.CostEstimate(flops=0, bytes_accessed=3 << 20, transcendentals=0),
         name="pack",
     )(tab, *[in_vmem(part) for part in parts], token)
 
 
-def place_kernel(sizes, tab, flags, *refs):
-    n_in = len(sizes)
-    pieces, out_ref, made, sems = refs[:n_in], refs[n_in], refs[n_in + 1], refs[n_in + 2]
-
+def place_tiles(tab, flags, number, sizes, ref, made, k):
+    size = sizes[number]
+    for n in range(size):
+        at = T_SLOTS + 2 * (sum(sizes[:number]) + n)
+        slot, kind = tab[at], tab[at + 1]
+        weight = flags[SLOTS * k + slot].astype(jnp.float32)
+
+        def tile(n=n, weight=weight):
+            found = [ref[c * size + n, k * PIECE : (k + 1) * PIECE, :] for c in range(NCOL)]
+            return jnp.concatenate(found, axis=0) * weight
+
+        @pl.when(kind == 0)
+        def _(slot=slot, tile=tile):
+            made[k, pl.ds(slot, BLK, stride=SLOTS), :] = tile().T
+
+        @pl.when(kind == 1)
+        def _(slot=slot, tile=tile):
+            made[k, pl.ds(slot, BLK, stride=SLOTS), :] = tile()
+
+
+def early_kernel(sizes, tab, flags, *refs):
+    count = len(refs) // 2 - 1
+    given, made, pieces, sems = refs[:count], refs[count], refs[count + 1 : -1], refs[-1]
+    copies = [pltpu.make_async_copy(ref, piece, sems.at[n]) for n, (ref, piece) in enumerate(zip(given, pieces))]
+    for copy in copies:
+        copy.start()
+    for copy in copies:
+        copy.wait()
+    for k in range(LOCAL):
+        for number, ref in enumerate(pieces):
+            place_tiles(tab, flags, number, sizes, ref, made, k)
+
+
+def place_early(tab, flags, sizes, pieces):
+    return pl.pallas_call(
+        functools.partial(early_kernel, sizes),
+        in_specs=[SMEM_SPEC] * 2 + [HBM_SPEC] * len(pieces),
+        out_specs=VMEM_SPEC,
+        out_shape=pltpu.VMEM((LOCAL, BLK * SLOTS, BLK), jnp.float32),
+        scratch_shapes=[pltpu.VMEM(piece.shape, jnp.float32) for piece in pieces]
+        + [pltpu.SemaphoreType.DMA((len(pieces),))],
+        compiler_params=pltpu.CompilerParams(vmem_limit_bytes=10 << 20),
+        cost_estimate=pl.CostEstimate(flops=0, bytes_accessed=6 << 20, transcendentals=0),
+        name="place_early",
+    )(tab, flags, *[in_hbm(piece) for piece in pieces])
+
+
+def late_kernel(sizes, tab, flags, early, piece, out_ref, made, sems, early_sem):
     def send(k):
         return pltpu.make_async_copy(made.at[k], out_ref.at[pl.ds(k * BLK * SLOTS, BLK * SLOTS), :], sems.at[k])
 
+    copy = pltpu.make_async_copy(early, made, early_sem)
+    copy.start()
+    copy.wait()
     for k in range(LOCAL):
-        at = T_SLOTS
-        for ref, size in zip(pieces, sizes):
-            for n in range(size):
-                slot, kind = tab[at], tab[at + 1]
-                at += 2
-                weight = flags[SLOTS * k + slot].astype(jnp.float32)
-
-                def tile(ref=ref, n=n, size=size, weight=weight):
-                    found = [ref[c * size + n, k * PIECE : (k + 1) * PIECE, :] for c in range(NCOL)]
-                    return jnp.concatenate(found, axis=0) * weight
-
-                @pl.when(kind == 0)
-                def _(slot=slot, tile=tile):
-                    made[k, pl.ds(slot, BLK, stride=SLOTS), :] = tile().T
-
-                @pl.when(kind == 1)
-                def _(slot=slot, tile=tile):
-                    made[k, pl.ds(slot, BLK, stride=SLOTS), :] = tile()
-
+        place_tiles(tab, flags, len(sizes) - 1, sizes, piece, made, k)
         send(k).start()
     for k in range(LOCAL):
         send(k).wait()
 
 
-def place(tab, flags, sizes, pieces):
-    return pl.pallas_call(
-        functools.partial(place_kernel, sizes),
-        in_specs=[SMEM_SPEC] * 2 + [VMEM_SPEC] * len(sizes),
+def place_late(tab, flags, sizes, early, piece):
+    return pl.pallas_call(
+        functools.partial(late_kernel, sizes),
+        in_specs=[SMEM_SPEC] * 2 + [VMEM_SPEC] * 2,
         out_specs=HBM_SPEC,
         out_shape=jax.ShapeDtypeStruct((ROWS * SLOTS, BLK), jnp.float32),
-        scratch_shapes=[pltpu.VMEM((LOCAL, BLK * SLOTS, BLK), jnp.float32), pltpu.SemaphoreType.DMA((LOCAL,))],
+        scratch_shapes=[
+            pltpu.VMEM((LOCAL, BLK * SLOTS, BLK), jnp.float32),
+            pltpu.SemaphoreType.DMA((LOCAL,)),
+            pltpu.SemaphoreType.DMA,
+        ],
         compiler_params=pltpu.CompilerParams(vmem_limit_bytes=8 << 20),
         cost_estimate=pl.CostEstimate(flops=0, bytes_accessed=7 << 20, transcendentals=0),
-        name="place",
-    )(tab, flags, *[in_vmem(piece) for piece in pieces])
+        name="place_late",
+    )(tab, flags, in_vmem(early), in_vmem(piece))
 
 
 def flags_kernel(tab, pairs_ref, out_ref):
@@ -345,7 +450,7 @@
     pltpu.make_async_copy(even_ref, out_ref, sem).wait()
 
 
-def choose(tab, even, odd):
+def choose(tab, even, odd, late):
     return pl.pallas_call(
         choose_kernel,
         in_specs=[SMEM_SPEC] + [pl.BlockSpec(memory_space=pl.ANY)] * 2,
@@ -355,7 +460,7 @@
         compiler_params=pltpu.CompilerParams(vmem_limit_bytes=4 << 20),
         cost_estimate=pl.CostEstimate(flops=0, bytes_accessed=5 << 19, transcendentals=0),
         name="choose",
-    )(tab, even, odd)
+    )(tab, in_hbm(even) if late else even, in_hbm(odd) if late else odd)
 
 
 def per_device(coefficients, range_start, range_end, pair_list):
@@ -363,27 +468,30 @@
     row, col = lax.axis_index("row"), lax.axis_index("col")
     tab = lax.dynamic_index_in_dim(jnp.asarray(table), row * NCOL + col, 0, keepdims=False)
     scalars = (in_hbm(tab), in_hbm(range_start), in_hbm(range_end))
-    held = {0: own_part(scalars, coefficients)}
+    held = {0: own_part(*scalars[1:], coefficients)}
     rows, token = own_rows(scalars, coefficients)
     flags = listed_flags(tab, pair_list)
     made = {}
 
     def send(unit):
         a, b = UNITS[unit][2]
-        source = held[a] if a == b else choose(tab, held[a], held[b])
+        source = held[a] if a == b else choose(tab, held[a], held[b], unit > 8)
         held[unit] = lax.ppermute(source, AXES, shifted(step_to(unit)))
 
-    def multiply(group, token):
-        *results, token = products([held[u] for u in group], rows, token)
+    def multiply(group, token, how=products):
+        *results, token = how([held[u] for u in group], rows, token)
         for unit, product in zip(group, results):
             made["U", unit] = product
-            if unit in BACK:
-                made["V", unit] = lax.ppermute(product, AXES, shifted(step_back(unit)))
         return token
 
-    def gate(units, token):
-        *values, token = lax.optimization_barrier((*[held[u] for u in units], token))
+    def send_back(unit):
+        made["V", unit] = lax.ppermute(made["U", unit], AXES, shifted(step_back(unit)))
+
+    def gate(units, token, back=()):
+        found = [held[u] for u in units] + [made["V", u] for u in back]
+        *values, token = lax.optimization_barrier((*found, token))
         held.update(zip(units, values))
+        made.update({("V", u): value for u, value in zip(back, values[len(units) :])})
         return token
 
     for unit in (1, 2, 3, 4):
@@ -395,18 +503,30 @@
     token = gate((5,), token)
     send(8)
     send(9)
+
+    def ship(number, token):
+        first = sum(len(earlier) for earlier in BATCHES[:number])
+        batch = BATCHES[number]
+        message, token = pack(tab, first, batch, sizes[number], [made[entry] for entry in batch], token)
+        return lax.all_to_all(message, "col", 0, 0, tiled=True), token
+
     token = multiply(GROUPS[1], token)
+    send_back(5)
     token = multiply(GROUPS[2], token)
-    message, token = pack(tab, 0, BATCHES[0], sizes[0], [made[entry] for entry in BATCHES[0]], token)
-    pieces = [lax.all_to_all(message, "col", 0, 0, tiled=True)]
+    piece_a, token = ship(0, token)
     token = gate((8, 9), token)
     send(11)
     send(10)
-    token = multiply(GROUPS[3], token)
+    token = multiply(GROUPS[3], token, stream_products)
+    send_back(8)
+    send_back(9)
+    made["U", 7], token = lax.optimization_barrier((made["U", 7], token))
+    send_back(7)
+    token = touch(rows, token)
     token = multiply(GROUPS[4], token)
-    message, _ = pack(tab, len(BATCHES[0]), BATCHES[1], sizes[1], [made[entry] for entry in BATCHES[1]], token)
-    pieces.append(lax.all_to_all(message, "col", 0, 0, tiled=True))
-    return place(tab, flags, sizes, pieces).reshape(ROWS, SLOTS, 1, BLK)
+    piece_b, token = ship(1, token)
+    early = place_early(tab, flags, sizes, [piece_a])
+    return place_late(tab, flags, sizes, early, piece_b).reshape(ROWS, SLOTS, 1, BLK)
 
 
 def solution(mesh):

time: 165 us -> 161 us (0.976)
  Pallas kernels: 42.6 us -> 53.2 us
  waiting for transfers between devices: 75.2 us -> 66.9 us
  local copies, waits for them, and re-layouts: 10.2 us -> 2.29 us
    pallas_call x2 -> x5, Pallas kernels: 8.72 us -> 17.8 us  [the longest x1 6.46 us: stream_products(): pl.pallas_call(functools.partial(stream_kernel, n), in_specs=[HBM_SPEC] *...]
    unnamed x16 -> x14, local copies, waits for them, and re-layouts: 9.04 us -> 1.09 us
    all_to_all x2, waiting for transfers between devices: 23.2 us -> 18.3 us  [ship(): return (lax.all_to_all(message, 'col', 0, 0, tiled=True), token)]
    ppermute x11, waiting for transfers between devices: 42.2 us -> 38.8 us  [send(): held[unit] = lax.ppermute(source, AXES, shifted(step_to(unit)))]
    pallas_call x5 -> x4, Pallas kernels: 21.4 us -> 18.5 us  [products(): pl.pallas_call(functools.partial(product_kernel, n), in_specs=[VMEM_SPEC]...]
    pallas_call x2, Pallas kernels: 1.84 us -> 4.6 us  [pack(): pl.pallas_call(functools.partial(pack_kernel, first, batch), in_specs=[SM...]
  transfers between devices with their start and end apart: 17 -> 17, of which waited for: 11 -> 12; matrix products, arithmetic and copies ran while one was open for 0% -> 1% of each run, Pallas kernels for 21% -> 29%
where the time goes in v5:
time: 161 us; the launch traced here: 160 us
  waiting for transfers between devices  66.9 us (42%)
  Pallas kernels  53.2 us (33%)
  starting transfers between devices  37.8 us (23%)
  local copies, waits for them, and re-layouts  2.29 us (1%)
    ppermute x11, waiting for transfers between devices, send(): held[unit] = lax.ppermute(source, AXES, shifted(step_to(unit)))  38.8 us
    pallas_call x4, Pallas kernels, products(): pl.pallas_call(functools.partial(product_kernel, n), in_specs=[VMEM_SPEC]...  18.5 us
    all_to_all x2, waiting for transfers between devices, ship(): return (lax.all_to_all(message, 'col', 0, 0, tiled=True), token)  18.3 us
    all_to_all x2, starting transfers between devices, ship(): return (lax.all_to_all(message, 'col', 0, 0, tiled=True), token)  13.1 us
    ppermute x4, starting transfers between devices, send_back(): lax.ppermute(made['U', unit], AXES, shifted(step_back(unit)))  12.4 us
    ppermute x11, starting transfers between devices, send(): held[unit] = lax.ppermute(source, AXES, shifted(step_to(unit)))  12.2 us
    ppermute x4, waiting for transfers between devices, send_back(): lax.ppermute(made['U', unit], AXES, shifted(step_back(unit)))  9.74 us
    pallas_call x1, Pallas kernels, own_rows(): pl.pallas_call(rows_kernel, in_specs=[SMEM_SPEC] * 3 + [HBM_SPEC], out_sp...  6.49 us
  transfers between devices with their start and end apart: 17, of which 12 were waited for; matrix products, arithmetic and copies ran while one was open for 1% of the time, Pallas kernels for 29%

profile of v5, /device:TPU:1, one launch (start us, length us, event | category | flops | bytes accessed | tf_op | source)
XLA Modules:
  0.0 160.4 jit_solution(16866000300406667639)
XLA Ops:
  2.2 3.6 %collective-permute-start.3 = (bf16[80,8192]{1,0:T(8,128)(2,1)S(1)}, bf16[80,8192]{1,0:T(8,128)(2,1)S(1)}, u32[]{:S(2)}, u32[]{:S(2)}) collective-permute-start(bf16[80,8192]{1,0:T(8,128)(2,1)S(1)} %own_part.1.refs_0_), channel_id=1, source_target_pairs={{0,24},{1,25},{2,26},{3,27},{4,28},{5,29},{6,30},{7,31},{8,0},{9,1... | collective-permute-start | bytes 3932168 | tf_op jit(solution)/shard_map/ppermute | solution.py:479
  5.9 2.5 %collective-permute-start.2 = (bf16[80,8192]{1,0:T(8,128)(2,1)S(1)}, bf16[80,8192]{1,0:T(8,128)(2,1)}, u32[]{:S(2)}, u32[]{:S(2)}) collective-permute-start(bf16[80,8192]{1,0:T(8,128)(2,1)S(1)} %own_part.1.refs_0_), channel_id=1, source_target_pairs={{0,96},{1,97},{2,98},{3,99},{4,100},{5,101},{6,102},{7,103},{8,104... | collective-permute-start | bytes 3932168 | tf_op jit(solution)/shard_map/ppermute | solution.py:479
  9.6 6.5 %own_rows.1 = (bf16[8,640,1024]{2,1,0:T(8,128)(2,1)S(1)}, f32[8,128]{1,0:T(8,128)S(1)}) custom-call(s32[108]{0:T(128)} %dynamic-slice_bitcast_fusion.tab, s32[80]{0:T(128)} %start.3, s32[80]{0:T(128)} %end.3, bf16[640,32,256]{2,1,0:T(8,128)(2,1)} %x_ref.3), custom_call_target="tpu_custom_call" | custom-call | bytes 20971520 | tf_op jit(solution)/shard_map/own_rows/pallas_call | solution.py:201
  16.1 17.3 %collective-permute-done.3.refs_4_.even_ref = bf16[80,8192]{1,0:T(8,128)(2,1)S(1)} collective-permute-done((bf16[80,8192]{1,0:T(8,128)(2,1)S(1)}, bf16[80,8192]{1,0:T(8,128)(2,1)S(1)}, u32[]{:S(2)}, u32[]{:S(2)}) %collective-permute-start.3) | collective-permute-done | bytes 1310752 | tf_op jit(solution)/shard_map/ppermute | solution.py:479
  35.5 3.2 %collective-permute-done.1.refs_2_.even_ref = bf16[80,8192]{1,0:T(8,128)(2,1)} collective-permute-done((bf16[80,8192]{1,0:T(8,128)(2,1)S(1)}, bf16[80,8192]{1,0:T(8,128)(2,1)}, u32[]{:S(2)}, u32[]{:S(2)}) %collective-permute-start.1) | collective-permute-done | bytes 1310752 | tf_op jit(solution)/shard_map/ppermute | solution.py:479
  44.3 7.3 %products.4 = (f32[80,640]{1,0:T(8,128)S(1)}, f32[80,640]{1,0:T(8,128)S(1)}, f32[80,640]{1,0:T(8,128)S(1)}, f32[80,640]{1,0:T(8,128)S(1)}, f32[80,640]{1,0:T(8,128)S(1)}, /*index=5*/f32[8,128]{1,0:T(8,128)S(1)}) custom-call(bf16[80,8192]{1,0:T(8,128)(2,1)S(1)} %own_part.1.refs_0_, bf16[80,8192]{1,0:T(8,128)(2,1)} %collective-permute-done.refs_1_.odd_ref, ...), custom_call_target="tpu_custom_call" | custom-call | flops 4194304000 | bytes 18350080 | tf_op jit(solution)/shard_map/products/pallas_call | solution.py:229
  52.7 5.2 %collective-permute-done.4.refs_0_ = bf16[80,8192]{1,0:T(8,128)(2,1)} collective-permute-done((bf16[80,8192]{1,0:T(8,128)(2,1)}, bf16[80,8192]{1,0:T(8,128)(2,1)}, u32[]{:S(2)}, u32[]{:S(2)}) %collective-permute-start.4) | collective-permute-done | bytes 1310752 | tf_op jit(solution)/shard_map/ppermute | solution.py:479
  57.9 4.6 %products.5 = (f32[80,640]{1,0:T(8,128)S(1)}, f32[8,128]{1,0:T(8,128)S(1)}) custom-call(bf16[80,8192]{1,0:T(8,128)(2,1)} %collective-permute-done.4.refs_0_, bf16[8,640,1024]{2,1,0:T(8,128)(2,1)S(1)} %get-tuple-element.44.refs_5_.refs_1_.refs_2_.rows_ref, f32[8,128]{1,0:T(8,128)S(1)} %get-tuple-element.53.refs_2_), custom_call_target="tpu_custom_call" | custom-call | flops 838860800 | bytes 12058624 | tf_op jit(solution)/shard_map/products/pallas_call | solution.py:229
  62.6 5.3 %collective-permute-start.5 = (f32[80,640]{1,0:T(8,128)S(1)}, f32[80,640]{1,0:T(8,128)S(1)}, u32[]{:S(2)}, u32[]{:S(2)}) collective-permute-start(f32[80,640]{1,0:T(8,128)S(1)} %get-tuple-element.54.refs_5_), channel_id=1, source_target_pairs={{0,120},{1,121},{2,122},{3,123},{4,124},{5,125},{6,126},{7,127},{8... | collective-permute-start | bytes 614408 | tf_op jit(solution)/shard_map/ppermute | solution.py:488
  67.9 4.4 %collective-permute-done.7.refs_1_ = bf16[80,8192]{1,0:T(8,128)(2,1)S(1)} collective-permute-done((bf16[80,8192]{1,0:T(8,128)(2,1)S(1)}, bf16[80,8192]{1,0:T(8,128)(2,1)S(1)}, u32[]{:S(2)}, u32[]{:S(2)}) %collective-permute-start.7) | collective-permute-done | bytes 1310752 | tf_op jit(solution)/shard_map/ppermute | solution.py:479
  74.4 3.3 %products.6 = (f32[80,640]{1,0:T(8,128)S(1)}, f32[80,640]{1,0:T(8,128)S(1)}, f32[8,128]{1,0:T(8,128)S(1)}) custom-call(bf16[80,8192]{1,0:T(8,128)(2,1)S(1)} %collective-permute-done.6.refs_0_, bf16[80,8192]{1,0:T(8,128)(2,1)S(1)} %collective-permute-done.7.refs_1_, bf16[8,640,1024]{2,1,0:T(8,128)(2,1)S(1)} %get-tuple-element.44.refs_5_.refs_1_.refs_2_.rows_ref, ...), custom_call_target="tpu_custom_call" | custom-call | flops 1677721600 | bytes 13631488 | tf_op jit(solution)/shard_map/products/pallas_call | solution.py:229
  79.8 7.7 %all-to-all-start = ((f32[56,80,128]{2,1,0:T(8,128)}), f32[56,80,128]{2,1,0:T(8,128)}, u32[]{:S(2)}, u32[]{:S(2)}) async-start(f32[56,80,128]{2,1,0:T(8,128)} %get-tuple-element.59), calls=%async_computation | async-start | bytes 4587520 | tf_op jit(solution)/shard_map/all_to_all | solution.py:511
  92.2 6.5 %stream_products.1 = (f32[80,640]{1,0:T(8,128)S(1)}, f32[80,640]{1,0:T(8,128)S(1)}, f32[8,128]{1,0:T(8,128)S(1)}) custom-call(bf16[80,8192]{1,0:T(8,128)(2,1)} %collective-permute-done.8.refs_0_.odd_ref, bf16[80,8192]{1,0:T(8,128)(2,1)} %collective-permute-done.9.refs_1_, bf16[8,640,1024]{2,1,0:T(8,128)(2,1)} %copy-done, f32[8,128]{1,0:T(8,128)S(1)} %get-tuple-element.63.refs_3_), custom_call_target="tpu_custom_call" | custom-call | flops 1677721600 | bytes 13631488 | tf_op jit(solution)/shard_map/stream_products/pallas_call | solution.py:273
  99.7 2.4 %collective-permute-start.13 = (f32[80,640]{1,0:T(8,128)S(1)}, f32[80,640]{1,0:T(8,128)S(1)}, u32[]{:S(2)}, u32[]{:S(2)}) collective-permute-start(f32[80,640]{1,0:T(8,128)S(1)} %get-tuple-element.66.refs_1_), channel_id=1, source_target_pairs={{0,88},{1,89},{2,90},{3,91},{4,92},{5,93},{6,94},{7,95},{8,64},{9,... | collective-permute-start | bytes 614408 | tf_op jit(solution)/shard_map/ppermute | solution.py:488
  102.1 3.7 %collective-permute-start.14 = (f32[80,640]{1,0:T(8,128)S(1)}, f32[80,640]{1,0:T(8,128)S(1)}, u32[]{:S(2)}, u32[]{:S(2)}) collective-permute-start(f32[80,640]{1,0:T(8,128)S(1)} %get-tuple-element.67.refs_2_), channel_id=1, source_target_pairs={{0,112},{1,113},{2,114},{3,115},{4,116},{5,117},{6,118},{7,119},{8... | collective-permute-start | bytes 614408 | tf_op jit(solution)/shard_map/ppermute | solution.py:488
  105.8 2.3 %collective-permute-done.11.refs_0_ = bf16[80,8192]{1,0:T(8,128)(2,1)S(1)} collective-permute-done((bf16[80,8192]{1,0:T(8,128)(2,1)S(1)}, bf16[80,8192]{1,0:T(8,128)(2,1)S(1)}, u32[]{:S(2)}, u32[]{:S(2)}) %collective-permute-start.11) | collective-permute-done | bytes 1310752 | tf_op jit(solution)/shard_map/ppermute | solution.py:479
  110.0 3.3 %products.7 = (f32[80,640]{1,0:T(8,128)S(1)}, f32[80,640]{1,0:T(8,128)S(1)}, f32[8,128]{1,0:T(8,128)S(1)}) custom-call(bf16[80,8192]{1,0:T(8,128)(2,1)S(1)} %collective-permute-done.11.refs_0_, bf16[80,8192]{1,0:T(8,128)(2,1)S(1)} %collective-permute-done.12.refs_1_, bf16[8,640,1024]{2,1,0:T(8,128)(2,1)S(1)} %bitcast.5, f32[8,128]{1,0:T(8,128)S(1)} %touch.1.refs_3_), custom_call_target="tpu_custom_call" | custom-call | flops 1677721600 | bytes 13631488 | tf_op jit(solution)/shard_map/products/pallas_call | solution.py:229
  113.3 4.4 %collective-permute-done.10.refs_0_ = f32[80,640]{1,0:T(8,128)S(1)} collective-permute-done((f32[80,640]{1,0:T(8,128)S(1)}, f32[80,640]{1,0:T(8,128)S(1)}, u32[]{:S(2)}, u32[]{:S(2)}) %collective-permute-start.10) | collective-permute-done | bytes 204832 | tf_op jit(solution)/shard_map/ppermute | solution.py:488
  117.8 5.3 %collective-permute-done.14.refs_6_ = f32[80,640]{1,0:T(8,128)S(1)} collective-permute-done((f32[80,640]{1,0:T(8,128)S(1)}, f32[80,640]{1,0:T(8,128)S(1)}, u32[]{:S(2)}, u32[]{:S(2)}) %collective-permute-start.14) | collective-permute-done | bytes 204832 | tf_op jit(solution)/shard_map/ppermute | solution.py:488
  123.1 2.5 %pack.3 = (f32[48,80,128]{2,1,0:T(8,128)}, f32[8,128]{1,0:T(8,128)}) custom-call(s32[108]{0:T(128)S(1)} %copy-done.2, f32[80,640]{1,0:T(8,128)S(1)} %collective-permute-done.10.refs_0_, f32[80,640]{1,0:T(8,128)S(1)} %get-tuple-element.66.refs_1_, f32[80,640]{1,0:T(8,128)S(1)} %get-tuple-element.67.refs_2_, f32[80,640]{1,0:T(8,128)S(1)} %get-tuple-element.69.refs_3_, ...), custom_call_target="tpu_custom_call" | custom-call | bytes 3145728 | tf_op jit(solution)/shard_map/pack/pallas_call | solution.py:328
  125.6 5.4 %all-to-all-start.1 = ((f32[48,80,128]{2,1,0:T(8,128)}), f32[48,80,128]{2,1,0:T(8,128)}, u32[]{:S(2)}, u32[]{:S(2)}) async-start(f32[48,80,128]{2,1,0:T(8,128)} %get-tuple-element.72), calls=%async_computation.1 | async-start | bytes 3932160 | tf_op jit(solution)/shard_map/all_to_all | solution.py:511
  132.9 4.9 %place_early.1.early = f32[5,1280,128]{2,1,0:T(8,128)S(1)} custom-call(s32[108]{0:T(128)S(1)} %copy-done.2, s32[50]{0:T(128)S(1)} %listed_flags.1.flags, f32[56,80,128]{2,1,0:T(8,128)} %all-to-all-done.refs_0_), custom_call_target="tpu_custom_call" | custom-call | bytes 6291456 | tf_op jit(solution)/shard_map/place_early/pallas_call | solution.py:374
  137.8 18.3 %all-to-all-done.1.piece = f32[48,80,128]{2,1,0:T(8,128)} async-done(((f32[48,80,128]{2,1,0:T(8,128)}), f32[48,80,128]{2,1,0:T(8,128)}, u32[]{:S(2)}, u32[]{:S(2)}) %all-to-all-start.1) | async-done | bytes 1966112 | tf_op jit(solution)/shard_map/all_to_all | solution.py:511
  156.1 4.2 %place_late.1 = f32[6400,128]{1,0:T(8,128)} custom-call(s32[108]{0:T(128)S(1)} %copy-done.2, s32[50]{0:T(128)S(1)} %listed_flags.1.flags, f32[5,1280,128]{2,1,0:T(8,128)S(1)} %place_early.1.early, f32[48,80,128]{2,1,0:T(8,128)} %all-to-all-done.1.piece), custom_call_target="tpu_custom_call" | custom-call | bytes 7340032 | tf_op jit(solution)/shard_map/place_late/pallas_call | solution.py:402
  (41 shorter events, 26.0 us)
Async XLA Ops:
  2.2 31.1 %collective-permute-start.3 = (bf16[80,8192]{1,0:T(8,128)(2,1)S(1)}, bf16[80,8192]{1,0:T(8,128)(2,1)S(1)}, u32[]{:S(2)}, u32[]{:S(2)}) collective-permute-start(bf16[80,8192]{1,0:T(8,128)(2,1)S(1)} %own_part.1.refs_0_), channel_id=1, source_target_pairs={{0,24},{1,25},{2,26},{3,27},{4,28},{5,29},{6,30},{7,31},{8,0},{9,1... | collective-permute-start | bytes 3932168 | tf_op jit(solution)/shard_map/ppermute | solution.py:479
  5.9 29.6 %collective-permute-start.2 = (bf16[80,8192]{1,0:T(8,128)(2,1)S(1)}, bf16[80,8192]{1,0:T(8,128)(2,1)}, u32[]{:S(2)}, u32[]{:S(2)}) collective-permute-start(bf16[80,8192]{1,0:T(8,128)(2,1)S(1)} %own_part.1.refs_0_), channel_id=1, source_target_pairs={{0,96},{1,97},{2,98},{3,99},{4,100},{5,101},{6,102},{7,103},{8,104... | collective-permute-start | bytes 3932168 | tf_op jit(solution)/shard_map/ppermute | solution.py:479
  8.3 30.3 %collective-permute-start.1 = (bf16[80,8192]{1,0:T(8,128)(2,1)S(1)}, bf16[80,8192]{1,0:T(8,128)(2,1)}, u32[]{:S(2)}, u32[]{:S(2)}) collective-permute-start(bf16[80,8192]{1,0:T(8,128)(2,1)S(1)} %own_part.1.refs_0_), channel_id=1, source_target_pairs={{0,32},{1,9},{2,34},{3,11},{4,36},{5,13},{6,38},{7,15},{8,40},{9,1... | collective-permute-start | bytes 3932168 | tf_op jit(solution)/shard_map/ppermute | solution.py:479
  8.3 30.4 %collective-permute-start = (bf16[80,8192]{1,0:T(8,128)(2,1)S(1)}, bf16[80,8192]{1,0:T(8,128)(2,1)}, u32[]{:S(2)}, u32[]{:S(2)}) collective-permute-start(bf16[80,8192]{1,0:T(8,128)(2,1)S(1)} %own_part.1.refs_0_), channel_id=1, source_target_pairs={{0,8},{1,33},{2,10},{3,35},{4,12},{5,37},{6,14},{7,39},{8,16},{9,4... | collective-permute-start | bytes 3932168 | tf_op jit(solution)/shard_map/ppermute | solution.py:479
  9.6 30.6 %copy-start.2 = (s32[108]{0:T(128)S(1)}, s32[108]{0:T(128)}, u32[]{:S(2)}) copy-start(s32[108]{0:T(128)} %dynamic-slice_bitcast_fusion.tab) | copy-start | bytes 1300
  16.0 58.4 %copy-start = (bf16[8,640,1024]{2,1,0:T(8,128)(2,1)}, bf16[8,640,1024]{2,1,0:T(8,128)(2,1)S(1)}, u32[]{:S(2)}) copy-start(bf16[8,640,1024]{2,1,0:T(8,128)(2,1)S(1)} %get-tuple-element.44.refs_5_.refs_1_.refs_2_.rows_ref) | copy-start | bytes 31457284
  38.7 19.2 %collective-permute-start.4 = (bf16[80,8192]{1,0:T(8,128)(2,1)}, bf16[80,8192]{1,0:T(8,128)(2,1)}, u32[]{:S(2)}, u32[]{:S(2)}) collective-permute-start(bf16[80,8192]{1,0:T(8,128)(2,1)} %collective-permute-done.refs_1_.odd_ref), channel_id=1, source_target_pairs={{0,32},{1,9},{2,34},{3,11},{4,36},{5,13},{6,38},{7,15},{8,40},{9,1... | collective-permute-start | bytes 3932168 | tf_op jit(solution)/shard_map/ppermute | solution.py:479
  42.1 30.2 %collective-permute-start.7 = (bf16[80,8192]{1,0:T(8,128)(2,1)S(1)}, bf16[80,8192]{1,0:T(8,128)(2,1)S(1)}, u32[]{:S(2)}, u32[]{:S(2)}) collective-permute-start(bf16[80,8192]{1,0:T(8,128)(2,1)S(1)} %choose.2), channel_id=1, source_target_pairs={{0,24},{1,25},{2,26},{3,27},{4,28},{5,29},{6,30},{7,31},{8,0},{9,1... | collective-permute-start | bytes 3932168 | tf_op jit(solution)/shard_map/ppermute | solution.py:479
  44.3 30.1 %collective-permute-start.6 = (bf16[80,8192]{1,0:T(8,128)(2,1)}, bf16[80,8192]{1,0:T(8,128)(2,1)S(1)}, u32[]{:S(2)}, u32[]{:S(2)}) collective-permute-start(bf16[80,8192]{1,0:T(8,128)(2,1)} %collective-permute-done.2.refs_3_), channel_id=1, source_target_pairs={{0,96},{1,97},{2,98},{3,99},{4,100},{5,101},{6,102},{7,103},{8,104... | collective-permute-start | bytes 3932168 | tf_op jit(solution)/shard_map/ppermute | solution.py:479
  51.6 1.1 copy-start.1
  57.9 29.7 %collective-permute-start.9 = (bf16[80,8192]{1,0:T(8,128)(2,1)}, bf16[80,8192]{1,0:T(8,128)(2,1)}, u32[]{:S(2)}, u32[]{:S(2)}) collective-permute-start(bf16[80,8192]{1,0:T(8,128)(2,1)} %collective-permute-done.4.refs_0_), channel_id=1, source_target_pairs={{0,8},{1,9},{2,10},{3,11},{4,12},{5,13},{6,14},{7,15},{8,16},{9,17... | collective-permute-start | bytes 3932168 | tf_op jit(solution)/shard_map/ppermute | solution.py:479
  57.9 29.7 %collective-permute-start.8 = (bf16[80,8192]{1,0:T(8,128)(2,1)}, bf16[80,8192]{1,0:T(8,128)(2,1)}, u32[]{:S(2)}, u32[]{:S(2)}) collective-permute-start(bf16[80,8192]{1,0:T(8,128)(2,1)} %collective-permute-done.4.refs_0_), channel_id=1, source_target_pairs={{0,32},{1,33},{2,34},{3,35},{4,36},{5,37},{6,38},{7,39},{8,40},{9,... | collective-permute-start | bytes 3932168 | tf_op jit(solution)/shard_map/ppermute | solution.py:479
  62.6 15.1 %collective-permute-start.5 = (f32[80,640]{1,0:T(8,128)S(1)}, f32[80,640]{1,0:T(8,128)S(1)}, u32[]{:S(2)}, u32[]{:S(2)}) collective-permute-start(f32[80,640]{1,0:T(8,128)S(1)} %get-tuple-element.54.refs_5_), channel_id=1, source_target_pairs={{0,120},{1,121},{2,122},{3,123},{4,124},{5,125},{6,126},{7,127},{8... | collective-permute-start | bytes 614408 | tf_op jit(solution)/shard_map/ppermute | solution.py:488
  79.8 26.1 %slice-start = ((s8[10485760]{0:T(1024)(128)(4,1)}), s8[2097152]{0:T(1024)(128)(4,1)S(1)}, s32[]{:S(2)}) async-start(s8[10485760]{0:T(1024)(128)(4,1)} %bitcast.4), calls=%async_computation.2 | async-start | bytes 4194304
  79.8 45.8 %all-to-all-start = ((f32[56,80,128]{2,1,0:T(8,128)}), f32[56,80,128]{2,1,0:T(8,128)}, u32[]{:S(2)}, u32[]{:S(2)}) async-start(f32[56,80,128]{2,1,0:T(8,128)} %get-tuple-element.59), calls=%async_computation | async-start | bytes 4587520 | tf_op jit(solution)/shard_map/all_to_all | solution.py:511
  87.7 18.2 %slice-start.1 = ((s8[10485760]{0:T(1024)(128)(4,1)}), s8[4194304]{0:T(1024)(128)(4,1)S(1)}, s32[]{:S(2)}) async-start(s8[10485760]{0:T(1024)(128)(4,1)} %bitcast.4), calls=%async_computation.3 | async-start | bytes 8388608
  89.8 16.0 %slice-start.2 = ((s8[10485760]{0:T(1024)(128)(4,1)}), s8[4194304]{0:T(1024)(128)(4,1)S(1)}, s32[]{:S(2)}) async-start(s8[10485760]{0:T(1024)(128)(4,1)} %bitcast.4), calls=%async_computation.4 | async-start | bytes 8388608
  89.8 18.3 %collective-permute-start.11 = (bf16[80,8192]{1,0:T(8,128)(2,1)S(1)}, bf16[80,8192]{1,0:T(8,128)(2,1)S(1)}, u32[]{:S(2)}, u32[]{:S(2)}) collective-permute-start(bf16[80,8192]{1,0:T(8,128)(2,1)S(1)} %choose.3), channel_id=1, source_target_pairs={{0,24},{1,9},{2,26},{3,11},{4,28},{5,13},{6,30},{7,15},{8,0},{9,17... | collective-permute-start | bytes 3932168 | tf_op jit(solution)/shard_map/ppermute | solution.py:479
  90.2 19.8 %collective-permute-start.12 = (bf16[80,8192]{1,0:T(8,128)(2,1)}, bf16[80,8192]{1,0:T(8,128)(2,1)S(1)}, u32[]{:S(2)}, u32[]{:S(2)}) collective-permute-start(bf16[80,8192]{1,0:T(8,128)(2,1)} %collective-permute-done.9.refs_1_), channel_id=1, source_target_pairs={{0,32},{1,97},{2,34},{3,99},{4,36},{5,101},{6,38},{7,103},{8,40},{... | collective-permute-start | bytes 3932168 | tf_op jit(solution)/shard_map/ppermute | solution.py:479
  98.7 19.1 %collective-permute-start.10 = (f32[80,640]{1,0:T(8,128)S(1)}, f32[80,640]{1,0:T(8,128)S(1)}, u32[]{:S(2)}, u32[]{:S(2)}) collective-permute-start(f32[80,640]{1,0:T(8,128)S(1)} %get-tuple-element.65.refs_8_), channel_id=1, source_target_pairs={{0,104},{1,105},{2,106},{3,107},{4,108},{5,109},{6,110},{7,111},{8... | collective-permute-start | bytes 614408 | tf_op jit(solution)/shard_map/ppermute | solution.py:488
  99.7 18.1 %collective-permute-start.13 = (f32[80,640]{1,0:T(8,128)S(1)}, f32[80,640]{1,0:T(8,128)S(1)}, u32[]{:S(2)}, u32[]{:S(2)}) collective-permute-start(f32[80,640]{1,0:T(8,128)S(1)} %get-tuple-element.66.refs_1_), channel_id=1, source_target_pairs={{0,88},{1,89},{2,90},{3,91},{4,92},{5,93},{6,94},{7,95},{8,64},{9,... | collective-permute-start | bytes 614408 | tf_op jit(solution)/shard_map/ppermute | solution.py:488
  102.1 21.0 %collective-permute-start.14 = (f32[80,640]{1,0:T(8,128)S(1)}, f32[80,640]{1,0:T(8,128)S(1)}, u32[]{:S(2)}, u32[]{:S(2)}) collective-permute-start(f32[80,640]{1,0:T(8,128)S(1)} %get-tuple-element.67.refs_2_), channel_id=1, source_target_pairs={{0,112},{1,113},{2,114},{3,115},{4,116},{5,117},{6,118},{7,119},{8... | collective-permute-start | bytes 614408 | tf_op jit(solution)/shard_map/ppermute | solution.py:488
  125.6 5.4 %copy-start.3 = (s32[1976,2]{0,1:T(2,128)S(1)}, s32[1976,2]{0,1:T(2,128)}, u32[]{:S(2)}) copy-start(s32[1976,2]{0,1:T(2,128)} %param.8) | copy-start | bytes 47428
  125.6 30.5 %all-to-all-start.1 = ((f32[48,80,128]{2,1,0:T(8,128)}), f32[48,80,128]{2,1,0:T(8,128)}, u32[]{:S(2)}, u32[]{:S(2)}) async-start(f32[48,80,128]{2,1,0:T(8,128)} %get-tuple-element.72), calls=%async_computation.1 | async-start | bytes 3932160 | tf_op jit(solution)/shard_map/all_to_all | solution.py:511

commit v6 on v5

--- a/solution.py
+++ b/solution.py
@@ -210,11 +210,14 @@
     )(*scalars, in_hbm(coefficients))
 
 
-def product_kernel(n, *refs):
-    parts, rows, outs, mark_ref, acc = refs[:n], refs[n], refs[n + 2 : 2 * n + 2], refs[2 * n + 2], refs[2 * n + 3]
+def product_kernel(widths, *refs):
+    n, m = len(widths), sum(widths)
+    given, rows, outs, mark_ref, acc = refs[:m], refs[m], refs[m + 2 : m + n + 2], refs[m + n + 2], refs[m + n + 3]
+    parts = [given[sum(widths[:i]) : sum(widths[: i + 1])] for i in range(n)]
     mark_ref[...] = jnp.zeros_like(mark_ref)
     for s in range(NSL):
-        left = jnp.concatenate([part[:, s * SLW : (s + 1) * SLW] for part in parts], axis=0)
+        span = slice(s * SLW, (s + 1) * SLW)
+        left = jnp.concatenate([sum([ref[:, span] for ref in part[1:]], part[0][:, span]) for part in parts], axis=0)
         term = lax.dot_general(left, rows[s], (((1,), (1,)), ((), ())), preferred_element_type=jnp.float32)
         if s == 0:
             acc[...] = term
@@ -225,10 +228,12 @@
 
 
 def products(parts, rows, token):
-    n = len(parts)
-    return pl.pallas_call(
-        functools.partial(product_kernel, n),
-        in_specs=[VMEM_SPEC] * (n + 1) + [pl.BlockSpec(memory_space=pl.ANY)],
+    parts = [part if isinstance(part, tuple) else (part,) for part in parts]
+    widths = [len(part) for part in parts]
+    n, given = len(parts), [array for part in parts for array in part]
+    return pl.pallas_call(
+        functools.partial(product_kernel, widths),
+        in_specs=[VMEM_SPEC] * (len(given) + 1) + [pl.BlockSpec(memory_space=pl.ANY)],
         out_specs=[VMEM_SPEC] * (n + 1),
         out_shape=[pltpu.VMEM((PART, ROWS), jnp.float32)] * n + [MARK],
         scratch_shapes=[pltpu.VMEM((n * PART, ROWS), jnp.float32)],
@@ -237,7 +242,7 @@
             flops=2 * n * PART * ROWS * WIDTH, bytes_accessed=(10 << 20) + n * (3 << 19), transcendentals=0
         ),
         name="products",
-    )(*[in_vmem(part) for part in parts], in_vmem(rows), token)
+    )(*[in_vmem(array) for array in given], in_vmem(rows), token)
 
 
 def stream_kernel(n, *refs):
@@ -514,9 +519,9 @@
     send_back(5)
     token = multiply(GROUPS[2], token)
     piece_a, token = ship(0, token)
-    token = gate((8, 9), token)
+    token = gate((4, 8, 9), token)
     send(11)
-    send(10)
+    held[10] = tuple(lax.ppermute(held[u], AXES, shifted(step_to(10))[c::2]) for c, u in enumerate(UNITS[10][2]))
     token = multiply(GROUPS[3], token, stream_products)
     send_back(8)
     send_back(9)

time: 161 us -> 158 us (0.981)
  waiting for transfers between devices: 66.9 us -> 60.9 us
  starting transfers between devices: 37.8 us -> 43.4 us
  Pallas kernels: 53.2 us -> 50 us
    ppermute x11 -> x10, waiting for transfers between devices: 38.8 us -> 28.5 us  [send(): held[unit] = lax.ppermute(source, AXES, shifted(step_to(unit)))]
    ppermute x0 -> x2, waiting for transfers between devices: none -> 4.44 us  [per_device(): lax.ppermute(held[u], AXES, shifted(step_to(10))[c::2])]
    pallas_call x2 -> x1, Pallas kernels: 4.01 us -> 0.65 us  [choose(): pl.pallas_call(choose_kernel, in_specs=[SMEM_SPEC] + [pl.BlockSpec(memory...]
    all_to_all x2, starting transfers between devices: 13.1 us -> 16.2 us  [ship(): return (lax.all_to_all(message, 'col', 0, 0, tiled=True), token)]
    ppermute x0 -> x2, starting transfers between devices: none -> 2.65 us  [per_device(): lax.ppermute(held[u], AXES, shifted(step_to(10))[c::2])]
    ppermute x11 -> x10, starting transfers between devices: 12.2 us -> 13.3 us  [send(): held[unit] = lax.ppermute(source, AXES, shifted(step_to(unit)))]
  transfers between devices with their start and end apart: 17 -> 18, of which waited for: 12 -> 11; matrix products, arithmetic and copies ran while one was open for 1% -> 1% of each run, Pallas kernels for 29% -> 28%
where the time goes in v6:
time: 158 us; the launch traced here: 157 us
  waiting for transfers between devices  60.9 us (39%)
  Pallas kernels  50 us (32%)
  starting transfers between devices  43.4 us (27%)
  local copies, waits for them, and re-layouts  2.58 us (2%)
    ppermute x10, waiting for transfers between devices, send(): held[unit] = lax.ppermute(source, AXES, shifted(step_to(unit)))  28.5 us
    pallas_call x4, Pallas kernels, products(): pl.pallas_call(functools.partial(product_kernel, widths), in_specs=[VMEM_...  18.5 us
    all_to_all x2, waiting for transfers between devices, ship(): return (lax.all_to_all(message, 'col', 0, 0, tiled=True), token)  18.3 us
    all_to_all x2, starting transfers between devices, ship(): return (lax.all_to_all(message, 'col', 0, 0, tiled=True), token)  16.2 us
    ppermute x10, starting transfers between devices, send(): held[unit] = lax.ppermute(source, AXES, shifted(step_to(unit)))  13.3 us
    ppermute x4, starting transfers between devices, send_back(): lax.ppermute(made['U', unit], AXES, shifted(step_back(unit)))  11.2 us
    ppermute x4, waiting for transfers between devices, send_back(): lax.ppermute(made['U', unit], AXES, shifted(step_back(unit)))  9.65 us
    pallas_call x1, Pallas kernels, stream_products(): pl.pallas_call(functools.partial(stream_kernel, n), in_specs=[HBM_SPEC] *...  6.59 us
  transfers between devices with their start and end apart: 18, of which 11 were waited for; matrix products, arithmetic and copies ran while one was open for 1% of the time, Pallas kernels for 28%

profile of v6, /device:TPU:1, one launch (start us, length us, event | category | flops | bytes accessed | tf_op | source)
XLA Modules:
  0.0 157.1 jit_solution(8291623644260493135)
XLA Ops:
  0.0 2.2 %own_part.1.refs_0_ = bf16[80,8192]{1,0:T(8,128)(2,1)S(1)} custom-call(s32[80]{0:T(128)} %start.3, s32[80]{0:T(128)} %end.3, bf16[640,32,256]{2,1,0:T(8,128)(2,1)} %x_ref.3), custom_call_target="tpu_custom_call" | custom-call | bytes 2621440 | tf_op jit(solution)/shard_map/own_part/pallas_call | solution.py:159
  2.2 2.1 %collective-permute-start = (bf16[80,8192]{1,0:T(8,128)(2,1)S(1)}, bf16[80,8192]{1,0:T(8,128)(2,1)S(1)}, u32[]{:S(2)}, u32[]{:S(2)}) collective-permute-start(bf16[80,8192]{1,0:T(8,128)(2,1)S(1)} %own_part.1.refs_0_), channel_id=1, source_target_pairs={{0,8},{1,33},{2,10},{3,35},{4,12},{5,37},{6,14},{7,39},{8,16},{9,4... | collective-permute-start | bytes 3932168 | tf_op jit(solution)/shard_map/ppermute | solution.py:484
  9.8 6.5 %own_rows.1 = (bf16[8,640,1024]{2,1,0:T(8,128)(2,1)S(1)}, f32[8,128]{1,0:T(8,128)S(1)}) custom-call(s32[108]{0:T(128)} %dynamic-slice_bitcast_fusion.tab, s32[80]{0:T(128)} %start.3, s32[80]{0:T(128)} %end.3, bf16[640,32,256]{2,1,0:T(8,128)(2,1)} %x_ref.3), custom_call_target="tpu_custom_call" | custom-call | bytes 20971520 | tf_op jit(solution)/shard_map/own_rows/pallas_call | solution.py:201
  16.3 15.8 %collective-permute-done.refs_1_.odd_ref = bf16[80,8192]{1,0:T(8,128)(2,1)S(1)} collective-permute-done((bf16[80,8192]{1,0:T(8,128)(2,1)S(1)}, bf16[80,8192]{1,0:T(8,128)(2,1)S(1)}, u32[]{:S(2)}, u32[]{:S(2)}) %collective-permute-start) | collective-permute-done | bytes 1310752 | tf_op jit(solution)/shard_map/ppermute | solution.py:484
  32.1 3.9 %collective-permute-done.1.refs_2_.even_ref = bf16[80,8192]{1,0:T(8,128)(2,1)} collective-permute-done((bf16[80,8192]{1,0:T(8,128)(2,1)S(1)}, bf16[80,8192]{1,0:T(8,128)(2,1)}, u32[]{:S(2)}, u32[]{:S(2)}) %collective-permute-start.1) | collective-permute-done | bytes 1310752 | tf_op jit(solution)/shard_map/ppermute | solution.py:484
  40.9 7.4 %products.4 = (f32[80,640]{1,0:T(8,128)S(1)}, f32[80,640]{1,0:T(8,128)S(1)}, f32[80,640]{1,0:T(8,128)S(1)}, f32[80,640]{1,0:T(8,128)S(1)}, f32[80,640]{1,0:T(8,128)S(1)}, /*index=5*/f32[8,128]{1,0:T(8,128)S(1)}) custom-call(bf16[80,8192]{1,0:T(8,128)(2,1)S(1)} %own_part.1.refs_0_, bf16[80,8192]{1,0:T(8,128)(2,1)S(1)} %collective-permute-done.refs_1_.odd_ref, ...), custom_call_target="tpu_custom_call" | custom-call | flops 4194304000 | bytes 18350080 | tf_op jit(solution)/shard_map/products/pallas_call | solution.py:234
  48.2 5.9 %collective-permute-done.4.refs_0_ = bf16[80,8192]{1,0:T(8,128)(2,1)} collective-permute-done((bf16[80,8192]{1,0:T(8,128)(2,1)S(1)}, bf16[80,8192]{1,0:T(8,128)(2,1)}, u32[]{:S(2)}, u32[]{:S(2)}) %collective-permute-start.4) | collective-permute-done | bytes 1310752 | tf_op jit(solution)/shard_map/ppermute | solution.py:484
  55.1 4.7 %products.5 = (f32[80,640]{1,0:T(8,128)S(1)}, f32[8,128]{1,0:T(8,128)S(1)}) custom-call(bf16[80,8192]{1,0:T(8,128)(2,1)} %collective-permute-done.4.refs_0_, bf16[8,640,1024]{2,1,0:T(8,128)(2,1)S(1)} %get-tuple-element.45.refs_5_.refs_1_.refs_2_.rows_ref.refs_3_, f32[8,128]{1,0:T(8,128)S(1)} %get-tuple-element.54.refs_2_), custom_call_target="tpu_custom_call" | custom-call | flops 838860800 | bytes 12058624 | tf_op jit(solution)/shard_map/products/pallas_call | solution.py:234
  59.8 4.3 %collective-permute-start.5 = (f32[80,640]{1,0:T(8,128)S(1)}, f32[80,640]{1,0:T(8,128)S(1)}, u32[]{:S(2)}, u32[]{:S(2)}) collective-permute-start(f32[80,640]{1,0:T(8,128)S(1)} %get-tuple-element.55.refs_5_), channel_id=1, source_target_pairs={{0,120},{1,121},{2,122},{3,123},{4,124},{5,125},{6,126},{7,127},{8... | collective-permute-start | bytes 614408 | tf_op jit(solution)/shard_map/ppermute | solution.py:493
  66.0 3.3 %products.6 = (f32[80,640]{1,0:T(8,128)S(1)}, f32[80,640]{1,0:T(8,128)S(1)}, f32[8,128]{1,0:T(8,128)S(1)}) custom-call(bf16[80,8192]{1,0:T(8,128)(2,1)S(1)} %collective-permute-done.6.refs_0_, bf16[80,8192]{1,0:T(8,128)(2,1)S(1)} %collective-permute-done.7.refs_1_, bf16[8,640,1024]{2,1,0:T(8,128)(2,1)S(1)} %get-tuple-element.45.refs_5_.refs_1_.refs_2_.rows_ref.refs_3_, ...), custom_call_target="tpu_custom_call" | custom-call | flops 1677721600 | bytes 13631488 | tf_op jit(solution)/shard_map/products/pallas_call | solution.py:234
  71.2 2.1 %pack.2 = (f32[56,80,128]{2,1,0:T(8,128)}, f32[8,128]{1,0:T(8,128)S(1)}) custom-call(s32[108]{0:T(128)S(1)} %copy-done.2, f32[80,640]{1,0:T(8,128)S(1)} %get-tuple-element.47.refs_0_, f32[80,640]{1,0:T(8,128)S(1)} %get-tuple-element.48.refs_1_, f32[80,640]{1,0:T(8,128)S(1)} %get-tuple-element.49.refs_2_, f32[80,640]{1,0:T(8,128)S(1)} %get-tuple-element.50.refs_3_, ...), custom_call_target="tpu_custom_call" | custom-call | bytes 3145728 | tf_op jit(solution)/shard_map/pack/pallas_call | solution.py:333
  73.3 10.6 %all-to-all-start = ((f32[56,80,128]{2,1,0:T(8,128)}), f32[56,80,128]{2,1,0:T(8,128)S(1)}, u32[]{:S(2)}, u32[]{:S(2)}) async-start(f32[56,80,128]{2,1,0:T(8,128)} %get-tuple-element.60), calls=%async_computation | async-start | bytes 4587520 | tf_op jit(solution)/shard_map/all_to_all | solution.py:516
  89.2 6.6 %stream_products.1 = (f32[80,640]{1,0:T(8,128)S(1)}, f32[80,640]{1,0:T(8,128)S(1)}, f32[8,128]{1,0:T(8,128)S(1)}) custom-call(bf16[80,8192]{1,0:T(8,128)(2,1)} %collective-permute-done.8.refs_0_, bf16[80,8192]{1,0:T(8,128)(2,1)} %collective-permute-done.9.refs_1_, bf16[8,640,1024]{2,1,0:T(8,128)(2,1)} %copy-done, f32[8,128]{1,0:T(8,128)S(1)} %get-tuple-element.64.refs_3_), custom_call_target="tpu_custom_call" | custom-call | flops 1677721600 | bytes 13631488 | tf_op jit(solution)/shard_map/stream_products/pallas_call | solution.py:278
  96.6 3.6 %collective-permute-start.14 = (f32[80,640]{1,0:T(8,128)S(1)}, f32[80,640]{1,0:T(8,128)S(1)}, u32[]{:S(2)}, u32[]{:S(2)}) collective-permute-start(f32[80,640]{1,0:T(8,128)S(1)} %get-tuple-element.67.refs_1_), channel_id=1, source_target_pairs={{0,88},{1,89},{2,90},{3,91},{4,92},{5,93},{6,94},{7,95},{8,64},{9,... | collective-permute-start | bytes 614408 | tf_op jit(solution)/shard_map/ppermute | solution.py:493
  100.2 2.5 %collective-permute-start.15 = (f32[80,640]{1,0:T(8,128)S(1)}, f32[80,640]{1,0:T(8,128)S(1)}, u32[]{:S(2)}, u32[]{:S(2)}) collective-permute-start(f32[80,640]{1,0:T(8,128)S(1)} %get-tuple-element.68.refs_2_), channel_id=1, source_target_pairs={{0,112},{1,113},{2,114},{3,115},{4,116},{5,117},{6,118},{7,119},{8... | collective-permute-start | bytes 614408 | tf_op jit(solution)/shard_map/ppermute | solution.py:493
  102.7 4.4 %collective-permute-done.12.refs_1_ = bf16[80,8192]{1,0:T(8,128)(2,1)S(1)} collective-permute-done((bf16[80,8192]{1,0:T(8,128)(2,1)}, bf16[80,8192]{1,0:T(8,128)(2,1)S(1)}, u32[]{:S(2)}, u32[]{:S(2)}) %collective-permute-start.12) | collective-permute-done | bytes 1310752 | tf_op jit(solution)/shard_map/ppermute | solution.py:524
  107.2 3.3 %products.7 = (f32[80,640]{1,0:T(8,128)S(1)}, f32[80,640]{1,0:T(8,128)S(1)}, f32[8,128]{1,0:T(8,128)S(1)}) custom-call(bf16[80,8192]{1,0:T(8,128)(2,1)S(1)} %collective-permute-done.11.refs_0_, bf16[80,8192]{1,0:T(8,128)(2,1)S(1)} %collective-permute-done.12.refs_1_, bf16[80,8192]{1,0:T(8,128)(2,1)S(1)} %collective-permute-done.13.refs_2_, ...), custom_call_target="tpu_custom_call" | custom-call | flops 1677721600 | bytes 13631488 | tf_op jit(solution)/shard_map/products/pallas_call | solution.py:234
  110.4 3.3 %collective-permute-done.10.refs_0_ = f32[80,640]{1,0:T(8,128)S(1)} collective-permute-done((f32[80,640]{1,0:T(8,128)S(1)}, f32[80,640]{1,0:T(8,128)S(1)}, u32[]{:S(2)}, u32[]{:S(2)}) %collective-permute-start.10) | collective-permute-done | bytes 204832 | tf_op jit(solution)/shard_map/ppermute | solution.py:493
  113.7 4.4 %collective-permute-done.15.refs_6_ = f32[80,640]{1,0:T(8,128)S(1)} collective-permute-done((f32[80,640]{1,0:T(8,128)S(1)}, f32[80,640]{1,0:T(8,128)S(1)}, u32[]{:S(2)}, u32[]{:S(2)}) %collective-permute-start.15) | collective-permute-done | bytes 204832 | tf_op jit(solution)/shard_map/ppermute | solution.py:493
  118.2 2.5 %pack.3 = (f32[48,80,128]{2,1,0:T(8,128)}, f32[8,128]{1,0:T(8,128)}) custom-call(s32[108]{0:T(128)S(1)} %copy-done.2, f32[80,640]{1,0:T(8,128)S(1)} %collective-permute-done.10.refs_0_, f32[80,640]{1,0:T(8,128)S(1)} %get-tuple-element.67.refs_1_, f32[80,640]{1,0:T(8,128)S(1)} %get-tuple-element.68.refs_2_, f32[80,640]{1,0:T(8,128)S(1)} %get-tuple-element.71.refs_3_, ...), custom_call_target="tpu_custom_call" | custom-call | bytes 3145728 | tf_op jit(solution)/shard_map/pack/pallas_call | solution.py:333
  122.1 5.7 %all-to-all-start.1 = ((f32[48,80,128]{2,1,0:T(8,128)}), f32[48,80,128]{2,1,0:T(8,128)}, u32[]{:S(2)}, u32[]{:S(2)}) async-start(f32[48,80,128]{2,1,0:T(8,128)} %get-tuple-element.74), calls=%async_computation.1 | async-start | bytes 3932160 | tf_op jit(solution)/shard_map/all_to_all | solution.py:516
  129.6 4.9 %place_early.1.early = f32[5,1280,128]{2,1,0:T(8,128)S(1)} custom-call(s32[108]{0:T(128)S(1)} %copy-done.2, s32[50]{0:T(128)S(1)} %listed_flags.1.flags, f32[56,80,128]{2,1,0:T(8,128)} %copy-done.4), custom_call_target="tpu_custom_call" | custom-call | bytes 6291456 | tf_op jit(solution)/shard_map/place_early/pallas_call | solution.py:379
  134.5 18.3 %all-to-all-done.1.piece = f32[48,80,128]{2,1,0:T(8,128)} async-done(((f32[48,80,128]{2,1,0:T(8,128)}), f32[48,80,128]{2,1,0:T(8,128)}, u32[]{:S(2)}, u32[]{:S(2)}) %all-to-all-start.1) | async-done | bytes 1966112 | tf_op jit(solution)/shard_map/all_to_all | solution.py:516
  152.8 4.2 %place_late.1 = f32[6400,128]{1,0:T(8,128)} custom-call(s32[108]{0:T(128)S(1)} %copy-done.2, s32[50]{0:T(128)S(1)} %listed_flags.1.flags, f32[5,1280,128]{2,1,0:T(8,128)S(1)} %place_early.1.early, f32[48,80,128]{2,1,0:T(8,128)} %all-to-all-done.1.piece), custom_call_target="tpu_custom_call" | custom-call | bytes 7340032 | tf_op jit(solution)/shard_map/place_late/pallas_call | solution.py:407
  (37 shorter events, 24.4 us)
Async XLA Ops:
  2.2 29.8 %collective-permute-start = (bf16[80,8192]{1,0:T(8,128)(2,1)S(1)}, bf16[80,8192]{1,0:T(8,128)(2,1)S(1)}, u32[]{:S(2)}, u32[]{:S(2)}) collective-permute-start(bf16[80,8192]{1,0:T(8,128)(2,1)S(1)} %own_part.1.refs_0_), channel_id=1, source_target_pairs={{0,8},{1,33},{2,10},{3,35},{4,12},{5,37},{6,14},{7,39},{8,16},{9,4... | collective-permute-start | bytes 3932168 | tf_op jit(solution)/shard_map/ppermute | solution.py:484
  4.3 31.7 %collective-permute-start.1 = (bf16[80,8192]{1,0:T(8,128)(2,1)S(1)}, bf16[80,8192]{1,0:T(8,128)(2,1)}, u32[]{:S(2)}, u32[]{:S(2)}) collective-permute-start(bf16[80,8192]{1,0:T(8,128)(2,1)S(1)} %own_part.1.refs_0_), channel_id=1, source_target_pairs={{0,32},{1,9},{2,34},{3,11},{4,36},{5,13},{6,38},{7,15},{8,40},{9,1... | collective-permute-start | bytes 3932168 | tf_op jit(solution)/shard_map/ppermute | solution.py:484
  5.6 30.4 %collective-permute-start.2 = (bf16[80,8192]{1,0:T(8,128)(2,1)S(1)}, bf16[80,8192]{1,0:T(8,128)(2,1)}, u32[]{:S(2)}, u32[]{:S(2)}) collective-permute-start(bf16[80,8192]{1,0:T(8,128)(2,1)S(1)} %own_part.1.refs_0_), channel_id=1, source_target_pairs={{0,96},{1,97},{2,98},{3,99},{4,100},{5,101},{6,102},{7,103},{8,104... | collective-permute-start | bytes 3932168 | tf_op jit(solution)/shard_map/ppermute | solution.py:484
  7.1 28.9 %collective-permute-start.3 = (bf16[80,8192]{1,0:T(8,128)(2,1)S(1)}, bf16[80,8192]{1,0:T(8,128)(2,1)}, u32[]{:S(2)}, u32[]{:S(2)}) collective-permute-start(bf16[80,8192]{1,0:T(8,128)(2,1)S(1)} %own_part.1.refs_0_), channel_id=1, source_target_pairs={{0,24},{1,25},{2,26},{3,27},{4,28},{5,29},{6,30},{7,31},{8,0},{9,1... | collective-permute-start | bytes 3932168 | tf_op jit(solution)/shard_map/ppermute | solution.py:484
  9.7 27.5 %copy-start.2 = (s32[108]{0:T(128)S(1)}, s32[108]{0:T(128)}, u32[]{:S(2)}) copy-start(s32[108]{0:T(128)} %dynamic-slice_bitcast_fusion.tab) | copy-start | bytes 1300
  16.2 49.8 %copy-start = (bf16[8,640,1024]{2,1,0:T(8,128)(2,1)}, bf16[8,640,1024]{2,1,0:T(8,128)(2,1)S(1)}, u32[]{:S(2)}) copy-start(bf16[8,640,1024]{2,1,0:T(8,128)(2,1)S(1)} %get-tuple-element.45.refs_5_.refs_1_.refs_2_.rows_ref.refs_3_) | copy-start | bytes 31457284
  36.0 18.1 %collective-permute-start.4 = (bf16[80,8192]{1,0:T(8,128)(2,1)S(1)}, bf16[80,8192]{1,0:T(8,128)(2,1)}, u32[]{:S(2)}, u32[]{:S(2)}) collective-permute-start(bf16[80,8192]{1,0:T(8,128)(2,1)S(1)} %collective-permute-done.refs_1_.odd_ref), channel_id=1, source_target_pairs={{0,32},{1,9},{2,34},{3,11},{4,36},{5,13},{6,38},{7,15},{8,40},{9,1... | collective-permute-start | bytes 3932168 | tf_op jit(solution)/shard_map/ppermute | solution.py:484
  37.9 27.8 %collective-permute-start.7 = (bf16[80,8192]{1,0:T(8,128)(2,1)S(1)}, bf16[80,8192]{1,0:T(8,128)(2,1)S(1)}, u32[]{:S(2)}, u32[]{:S(2)}) collective-permute-start(bf16[80,8192]{1,0:T(8,128)(2,1)S(1)} %choose.1), channel_id=1, source_target_pairs={{0,24},{1,25},{2,26},{3,27},{4,28},{5,29},{6,30},{7,31},{8,0},{9,1... | collective-permute-start | bytes 3932168 | tf_op jit(solution)/shard_map/ppermute | solution.py:484
  39.5 26.5 %collective-permute-start.6 = (bf16[80,8192]{1,0:T(8,128)(2,1)}, bf16[80,8192]{1,0:T(8,128)(2,1)S(1)}, u32[]{:S(2)}, u32[]{:S(2)}) collective-permute-start(bf16[80,8192]{1,0:T(8,128)(2,1)} %collective-permute-done.2.refs_3_), channel_id=1, source_target_pairs={{0,96},{1,97},{2,98},{3,99},{4,100},{5,101},{6,102},{7,103},{8,104... | collective-permute-start | bytes 3932168 | tf_op jit(solution)/shard_map/ppermute | solution.py:484
  54.2 29.7 %collective-permute-start.8 = (bf16[80,8192]{1,0:T(8,128)(2,1)}, bf16[80,8192]{1,0:T(8,128)(2,1)}, u32[]{:S(2)}, u32[]{:S(2)}) collective-permute-start(bf16[80,8192]{1,0:T(8,128)(2,1)} %collective-permute-done.4.refs_0_), channel_id=1, source_target_pairs={{0,32},{1,33},{2,34},{3,35},{4,36},{5,37},{6,38},{7,39},{8,40},{9,... | collective-permute-start | bytes 3932168 | tf_op jit(solution)/shard_map/ppermute | solution.py:484
  55.1 29.6 %collective-permute-start.9 = (bf16[80,8192]{1,0:T(8,128)(2,1)}, bf16[80,8192]{1,0:T(8,128)(2,1)}, u32[]{:S(2)}, u32[]{:S(2)}) collective-permute-start(bf16[80,8192]{1,0:T(8,128)(2,1)} %collective-permute-done.4.refs_0_), channel_id=1, source_target_pairs={{0,8},{1,9},{2,10},{3,11},{4,12},{5,13},{6,14},{7,15},{8,16},{9,17... | collective-permute-start | bytes 3932168 | tf_op jit(solution)/shard_map/ppermute | solution.py:484
  59.8 11.4 %collective-permute-start.5 = (f32[80,640]{1,0:T(8,128)S(1)}, f32[80,640]{1,0:T(8,128)S(1)}, u32[]{:S(2)}, u32[]{:S(2)}) collective-permute-start(f32[80,640]{1,0:T(8,128)S(1)} %get-tuple-element.55.refs_5_), channel_id=1, source_target_pairs={{0,120},{1,121},{2,122},{3,123},{4,124},{5,125},{6,126},{7,127},{8... | collective-permute-start | bytes 614408 | tf_op jit(solution)/shard_map/ppermute | solution.py:493
  73.3 47.4 %all-to-all-start = ((f32[56,80,128]{2,1,0:T(8,128)}), f32[56,80,128]{2,1,0:T(8,128)S(1)}, u32[]{:S(2)}, u32[]{:S(2)}) async-start(f32[56,80,128]{2,1,0:T(8,128)} %get-tuple-element.60), calls=%async_computation | async-start | bytes 4587520 | tf_op jit(solution)/shard_map/all_to_all | solution.py:516
  84.7 15.4 %collective-permute-start.11 = (bf16[80,8192]{1,0:T(8,128)(2,1)}, bf16[80,8192]{1,0:T(8,128)(2,1)S(1)}, u32[]{:S(2)}, u32[]{:S(2)}) collective-permute-start(bf16[80,8192]{1,0:T(8,128)(2,1)} %collective-permute-done.3.refs_4_), channel_id=1, source_target_pairs={{0,24},{2,26},{4,28},{6,30},{8,0},{10,2},{12,4},{14,6},{16,8},{18,... | collective-permute-start | bytes 3932168 | tf_op jit(solution)/shard_map/ppermute | solution.py:524
  85.5 21.7 %collective-permute-start.12 = (bf16[80,8192]{1,0:T(8,128)(2,1)}, bf16[80,8192]{1,0:T(8,128)(2,1)S(1)}, u32[]{:S(2)}, u32[]{:S(2)}) collective-permute-start(bf16[80,8192]{1,0:T(8,128)(2,1)} %collective-permute-done.8.refs_0_), channel_id=1, source_target_pairs={{1,9},{3,11},{5,13},{7,15},{9,17},{11,19},{13,21},{15,23},{17,25},... | collective-permute-start | bytes 3932168 | tf_op jit(solution)/shard_map/ppermute | solution.py:524
  87.4 19.8 %collective-permute-start.13 = (bf16[80,8192]{1,0:T(8,128)(2,1)}, bf16[80,8192]{1,0:T(8,128)(2,1)S(1)}, u32[]{:S(2)}, u32[]{:S(2)}) collective-permute-start(bf16[80,8192]{1,0:T(8,128)(2,1)} %collective-permute-done.9.refs_1_), channel_id=1, source_target_pairs={{0,32},{1,97},{2,34},{3,99},{4,36},{5,101},{6,38},{7,103},{8,40},{... | collective-permute-start | bytes 3932168 | tf_op jit(solution)/shard_map/ppermute | solution.py:484
  89.2 13.5 %copy-start.1 = (bf16[8,640,1024]{2,1,0:T(8,128)(2,1)S(1)}, bf16[8,640,1024]{2,1,0:T(8,128)(2,1)}, u32[]{:S(2)}) copy-start(bf16[8,640,1024]{2,1,0:T(8,128)(2,1)} %copy-done) | copy-start | bytes 31457284
  95.8 17.9 %collective-permute-start.10 = (f32[80,640]{1,0:T(8,128)S(1)}, f32[80,640]{1,0:T(8,128)S(1)}, u32[]{:S(2)}, u32[]{:S(2)}) collective-permute-start(f32[80,640]{1,0:T(8,128)S(1)} %get-tuple-element.66.refs_8_), channel_id=1, source_target_pairs={{0,104},{1,105},{2,106},{3,107},{4,108},{5,109},{6,110},{7,111},{8... | collective-permute-start | bytes 614408 | tf_op jit(solution)/shard_map/ppermute | solution.py:493
  96.6 17.1 %collective-permute-start.14 = (f32[80,640]{1,0:T(8,128)S(1)}, f32[80,640]{1,0:T(8,128)S(1)}, u32[]{:S(2)}, u32[]{:S(2)}) collective-permute-start(f32[80,640]{1,0:T(8,128)S(1)} %get-tuple-element.67.refs_1_), channel_id=1, source_target_pairs={{0,88},{1,89},{2,90},{3,91},{4,92},{5,93},{6,94},{7,95},{8,64},{9,... | collective-permute-start | bytes 614408 | tf_op jit(solution)/shard_map/ppermute | solution.py:493
  100.2 18.0 %collective-permute-start.15 = (f32[80,640]{1,0:T(8,128)S(1)}, f32[80,640]{1,0:T(8,128)S(1)}, u32[]{:S(2)}, u32[]{:S(2)}) collective-permute-start(f32[80,640]{1,0:T(8,128)S(1)} %get-tuple-element.68.refs_2_), channel_id=1, source_target_pairs={{0,112},{1,113},{2,114},{3,115},{4,116},{5,117},{6,118},{7,119},{8... | collective-permute-start | bytes 614408 | tf_op jit(solution)/shard_map/ppermute | solution.py:493
  120.7 1.4 copy-start.4
  120.7 7.0 %copy-start.3 = (s32[1976,2]{0,1:T(2,128)S(1)}, s32[1976,2]{0,1:T(2,128)}, u32[]{:S(2)}) copy-start(s32[1976,2]{0,1:T(2,128)} %param.8) | copy-start | bytes 47428
  122.1 30.7 %all-to-all-start.1 = ((f32[48,80,128]{2,1,0:T(8,128)}), f32[48,80,128]{2,1,0:T(8,128)}, u32[]{:S(2)}, u32[]{:S(2)}) async-start(f32[48,80,128]{2,1,0:T(8,128)} %get-tuple-element.74), calls=%async_computation.1 | async-start | bytes 3932160 | tf_op jit(solution)/shard_map/all_to_all | solution.py:516

commit v7 on v6

--- a/solution.py
+++ b/solution.py
@@ -519,7 +519,7 @@
     send_back(5)
     token = multiply(GROUPS[2], token)
     piece_a, token = ship(0, token)
-    token = gate((4, 8, 9), token)
+    token = gate((8, 9), token)
     send(11)
     held[10] = tuple(lax.ppermute(held[u], AXES, shifted(step_to(10))[c::2]) for c, u in enumerate(UNITS[10][2]))
     token = multiply(GROUPS[3], token, stream_products)

time: 158 us -> 158 us (level)
  transfers between devices with their start and end apart: 18 -> 18, of which waited for: 11 -> 12; matrix products, arithmetic and copies ran while one was open for 1% -> 1% of each run, Pallas kernels for 28% -> 28%
where the time goes in v7:
time: 158 us; the launch traced here: 157 us
  waiting for transfers between devices  60.6 us (38%)
  Pallas kernels  50 us (32%)
  starting transfers between devices  43 us (27%)
  local copies, waits for them, and re-layouts  2.58 us (2%)
    ppermute x10, waiting for transfers between devices, send(): held[unit] = lax.ppermute(source, AXES, shifted(step_to(unit)))  29.3 us
    pallas_call x4, Pallas kernels, products(): pl.pallas_call(functools.partial(product_kernel, widths), in_specs=[VMEM_...  18.5 us
    all_to_all x2, waiting for transfers between devices, ship(): return (lax.all_to_all(message, 'col', 0, 0, tiled=True), token)  18.3 us
    all_to_all x2, starting transfers between devices, ship(): return (lax.all_to_all(message, 'col', 0, 0, tiled=True), token)  15.1 us
    ppermute x10, starting transfers between devices, send(): held[unit] = lax.ppermute(source, AXES, shifted(step_to(unit)))  14 us
    ppermute x4, starting transfers between devices, send_back(): lax.ppermute(made['U', unit], AXES, shifted(step_back(unit)))  11.2 us
    ppermute x4, waiting for transfers between devices, send_back(): lax.ppermute(made['U', unit], AXES, shifted(step_back(unit)))  8.77 us
    pallas_call x1, Pallas kernels, stream_products(): pl.pallas_call(functools.partial(stream_kernel, n), in_specs=[HBM_SPEC] *...  6.59 us
  transfers between devices with their start and end apart: 18, of which 12 were waited for; matrix products, arithmetic and copies ran while one was open for 1% of the time, Pallas kernels for 28%

profile of v7, /device:TPU:1, one launch (start us, length us, event | category | flops | bytes accessed | tf_op | source)
XLA Modules:
  0.0 156.5 jit_solution(11464399146457347080)
XLA Ops:
  0.0 2.2 %own_part.1.refs_0_ = bf16[80,8192]{1,0:T(8,128)(2,1)S(1)} custom-call(s32[80]{0:T(128)} %start.3, s32[80]{0:T(128)} %end.3, bf16[640,32,256]{2,1,0:T(8,128)(2,1)} %x_ref.3), custom_call_target="tpu_custom_call" | custom-call | bytes 2621440 | tf_op jit(solution)/shard_map/own_part/pallas_call | solution.py:159
  2.2 2.1 %collective-permute-start = (bf16[80,8192]{1,0:T(8,128)(2,1)S(1)}, bf16[80,8192]{1,0:T(8,128)(2,1)S(1)}, u32[]{:S(2)}, u32[]{:S(2)}) collective-permute-start(bf16[80,8192]{1,0:T(8,128)(2,1)S(1)} %own_part.1.refs_0_), channel_id=1, source_target_pairs={{0,8},{1,33},{2,10},{3,35},{4,12},{5,37},{6,14},{7,39},{8,16},{9,4... | collective-permute-start | bytes 3932168 | tf_op jit(solution)/shard_map/ppermute | solution.py:484
  9.8 6.5 %own_rows.1 = (bf16[8,640,1024]{2,1,0:T(8,128)(2,1)S(1)}, f32[8,128]{1,0:T(8,128)S(1)}) custom-call(s32[108]{0:T(128)} %dynamic-slice_bitcast_fusion.tab, s32[80]{0:T(128)} %start.3, s32[80]{0:T(128)} %end.3, bf16[640,32,256]{2,1,0:T(8,128)(2,1)} %x_ref.3), custom_call_target="tpu_custom_call" | custom-call | bytes 20971520 | tf_op jit(solution)/shard_map/own_rows/pallas_call | solution.py:201
  16.3 15.8 %collective-permute-done.refs_1_.odd_ref = bf16[80,8192]{1,0:T(8,128)(2,1)S(1)} collective-permute-done((bf16[80,8192]{1,0:T(8,128)(2,1)S(1)}, bf16[80,8192]{1,0:T(8,128)(2,1)S(1)}, u32[]{:S(2)}, u32[]{:S(2)}) %collective-permute-start) | collective-permute-done | bytes 1310752 | tf_op jit(solution)/shard_map/ppermute | solution.py:484
  32.1 3.9 %collective-permute-done.1.refs_2_.even_ref = bf16[80,8192]{1,0:T(8,128)(2,1)} collective-permute-done((bf16[80,8192]{1,0:T(8,128)(2,1)S(1)}, bf16[80,8192]{1,0:T(8,128)(2,1)}, u32[]{:S(2)}, u32[]{:S(2)}) %collective-permute-start.1) | collective-permute-done | bytes 1310752 | tf_op jit(solution)/shard_map/ppermute | solution.py:484
  40.9 7.4 %products.4 = (f32[80,640]{1,0:T(8,128)S(1)}, f32[80,640]{1,0:T(8,128)S(1)}, f32[80,640]{1,0:T(8,128)S(1)}, f32[80,640]{1,0:T(8,128)S(1)}, f32[80,640]{1,0:T(8,128)S(1)}, /*index=5*/f32[8,128]{1,0:T(8,128)S(1)}) custom-call(bf16[80,8192]{1,0:T(8,128)(2,1)S(1)} %own_part.1.refs_0_, bf16[80,8192]{1,0:T(8,128)(2,1)S(1)} %collective-permute-done.refs_1_.odd_ref, ...), custom_call_target="tpu_custom_call" | custom-call | flops 4194304000 | bytes 18350080 | tf_op jit(solution)/shard_map/products/pallas_call | solution.py:234
  48.2 5.9 %collective-permute-done.4.refs_0_ = bf16[80,8192]{1,0:T(8,128)(2,1)} collective-permute-done((bf16[80,8192]{1,0:T(8,128)(2,1)S(1)}, bf16[80,8192]{1,0:T(8,128)(2,1)}, u32[]{:S(2)}, u32[]{:S(2)}) %collective-permute-start.4) | collective-permute-done | bytes 1310752 | tf_op jit(solution)/shard_map/ppermute | solution.py:484
  55.1 4.7 %products.5 = (f32[80,640]{1,0:T(8,128)S(1)}, f32[8,128]{1,0:T(8,128)S(1)}) custom-call(bf16[80,8192]{1,0:T(8,128)(2,1)} %collective-permute-done.4.refs_0_, bf16[8,640,1024]{2,1,0:T(8,128)(2,1)S(1)} %get-tuple-element.44.refs_5_.refs_1_.refs_2_.rows_ref.refs_3_, f32[8,128]{1,0:T(8,128)S(1)} %get-tuple-element.53.refs_2_), custom_call_target="tpu_custom_call" | custom-call | flops 838860800 | bytes 12058624 | tf_op jit(solution)/shard_map/products/pallas_call | solution.py:234
  59.8 4.3 %collective-permute-start.5 = (f32[80,640]{1,0:T(8,128)S(1)}, f32[80,640]{1,0:T(8,128)S(1)}, u32[]{:S(2)}, u32[]{:S(2)}) collective-permute-start(f32[80,640]{1,0:T(8,128)S(1)} %get-tuple-element.54.refs_5_), channel_id=1, source_target_pairs={{0,120},{1,121},{2,122},{3,123},{4,124},{5,125},{6,126},{7,127},{8... | collective-permute-start | bytes 614408 | tf_op jit(solution)/shard_map/ppermute | solution.py:493
  66.0 3.3 %products.6 = (f32[80,640]{1,0:T(8,128)S(1)}, f32[80,640]{1,0:T(8,128)S(1)}, f32[8,128]{1,0:T(8,128)S(1)}) custom-call(bf16[80,8192]{1,0:T(8,128)(2,1)S(1)} %collective-permute-done.6.refs_0_, bf16[80,8192]{1,0:T(8,128)(2,1)S(1)} %collective-permute-done.7.refs_1_, bf16[8,640,1024]{2,1,0:T(8,128)(2,1)S(1)} %get-tuple-element.44.refs_5_.refs_1_.refs_2_.rows_ref.refs_3_, ...), custom_call_target="tpu_custom_call" | custom-call | flops 1677721600 | bytes 13631488 | tf_op jit(solution)/shard_map/products/pallas_call | solution.py:234
  73.3 10.6 %all-to-all-start = ((f32[56,80,128]{2,1,0:T(8,128)}), f32[56,80,128]{2,1,0:T(8,128)S(1)}, u32[]{:S(2)}, u32[]{:S(2)}) async-start(f32[56,80,128]{2,1,0:T(8,128)} %get-tuple-element.59), calls=%async_computation | async-start | bytes 4587520 | tf_op jit(solution)/shard_map/all_to_all | solution.py:516
  86.6 2.5 %collective-permute-start.13 = (bf16[80,8192]{1,0:T(8,128)(2,1)}, bf16[80,8192]{1,0:T(8,128)(2,1)S(1)}, u32[]{:S(2)}, u32[]{:S(2)}) collective-permute-start(bf16[80,8192]{1,0:T(8,128)(2,1)} %collective-permute-done.9.refs_1_), channel_id=1, source_target_pairs={{0,32},{1,97},{2,34},{3,99},{4,36},{5,101},{6,38},{7,103},{8,40},{... | collective-permute-start | bytes 3932168 | tf_op jit(solution)/shard_map/ppermute | solution.py:484
  89.2 6.6 %stream_products.1 = (f32[80,640]{1,0:T(8,128)S(1)}, f32[80,640]{1,0:T(8,128)S(1)}, f32[8,128]{1,0:T(8,128)S(1)}) custom-call(bf16[80,8192]{1,0:T(8,128)(2,1)} %collective-permute-done.8.refs_0_, bf16[80,8192]{1,0:T(8,128)(2,1)} %collective-permute-done.9.refs_1_, bf16[8,640,1024]{2,1,0:T(8,128)(2,1)} %copy-done, f32[8,128]{1,0:T(8,128)S(1)} %get-tuple-element.63.refs_3_), custom_call_target="tpu_custom_call" | custom-call | flops 1677721600 | bytes 13631488 | tf_op jit(solution)/shard_map/stream_products/pallas_call | solution.py:278
  96.6 2.8 %collective-permute-start.14 = (f32[80,640]{1,0:T(8,128)S(1)}, f32[80,640]{1,0:T(8,128)S(1)}, u32[]{:S(2)}, u32[]{:S(2)}) collective-permute-start(f32[80,640]{1,0:T(8,128)S(1)} %get-tuple-element.66.refs_1_), channel_id=1, source_target_pairs={{0,88},{1,89},{2,90},{3,91},{4,92},{5,93},{6,94},{7,95},{8,64},{9,... | collective-permute-start | bytes 614408 | tf_op jit(solution)/shard_map/ppermute | solution.py:493
  99.4 3.3 %collective-permute-start.15 = (f32[80,640]{1,0:T(8,128)S(1)}, f32[80,640]{1,0:T(8,128)S(1)}, u32[]{:S(2)}, u32[]{:S(2)}) collective-permute-start(f32[80,640]{1,0:T(8,128)S(1)} %get-tuple-element.67.refs_2_), channel_id=1, source_target_pairs={{0,112},{1,113},{2,114},{3,115},{4,116},{5,117},{6,118},{7,119},{8... | collective-permute-start | bytes 614408 | tf_op jit(solution)/shard_map/ppermute | solution.py:493
  102.7 4.3 %collective-permute-done.12.refs_1_ = bf16[80,8192]{1,0:T(8,128)(2,1)S(1)} collective-permute-done((bf16[80,8192]{1,0:T(8,128)(2,1)}, bf16[80,8192]{1,0:T(8,128)(2,1)S(1)}, u32[]{:S(2)}, u32[]{:S(2)}) %collective-permute-start.12) | collective-permute-done | bytes 1310752 | tf_op jit(solution)/shard_map/ppermute | solution.py:524
  108.6 3.3 %products.7 = (f32[80,640]{1,0:T(8,128)S(1)}, f32[80,640]{1,0:T(8,128)S(1)}, f32[8,128]{1,0:T(8,128)S(1)}) custom-call(bf16[80,8192]{1,0:T(8,128)(2,1)S(1)} %collective-permute-done.11.refs_0_, bf16[80,8192]{1,0:T(8,128)(2,1)S(1)} %collective-permute-done.12.refs_1_, bf16[80,8192]{1,0:T(8,128)(2,1)S(1)} %collective-permute-done.13.refs_2_, ...), custom_call_target="tpu_custom_call" | custom-call | flops 1677721600 | bytes 13631488 | tf_op jit(solution)/shard_map/products/pallas_call | solution.py:234
  111.8 3.1 %collective-permute-done.10.refs_0_ = f32[80,640]{1,0:T(8,128)S(1)} collective-permute-done((f32[80,640]{1,0:T(8,128)S(1)}, f32[80,640]{1,0:T(8,128)S(1)}, u32[]{:S(2)}, u32[]{:S(2)}) %collective-permute-start.10) | collective-permute-done | bytes 204832 | tf_op jit(solution)/shard_map/ppermute | solution.py:493
  114.9 3.8 %collective-permute-done.15.refs_6_ = f32[80,640]{1,0:T(8,128)S(1)} collective-permute-done((f32[80,640]{1,0:T(8,128)S(1)}, f32[80,640]{1,0:T(8,128)S(1)}, u32[]{:S(2)}, u32[]{:S(2)}) %collective-permute-start.15) | collective-permute-done | bytes 204832 | tf_op jit(solution)/shard_map/ppermute | solution.py:493
  118.7 2.5 %pack.3 = (f32[48,80,128]{2,1,0:T(8,128)}, f32[8,128]{1,0:T(8,128)}) custom-call(s32[108]{0:T(128)S(1)} %copy-done.2, f32[80,640]{1,0:T(8,128)S(1)} %collective-permute-done.10.refs_0_, f32[80,640]{1,0:T(8,128)S(1)} %get-tuple-element.66.refs_1_, f32[80,640]{1,0:T(8,128)S(1)} %get-tuple-element.67.refs_2_, f32[80,640]{1,0:T(8,128)S(1)} %get-tuple-element.69.refs_3_, ...), custom_call_target="tpu_custom_call" | custom-call | bytes 3145728 | tf_op jit(solution)/shard_map/pack/pallas_call | solution.py:333
  122.6 4.6 %all-to-all-start.1 = ((f32[48,80,128]{2,1,0:T(8,128)}), f32[48,80,128]{2,1,0:T(8,128)}, u32[]{:S(2)}, u32[]{:S(2)}) async-start(f32[48,80,128]{2,1,0:T(8,128)} %get-tuple-element.72), calls=%async_computation.1 | async-start | bytes 3932160 | tf_op jit(solution)/shard_map/all_to_all | solution.py:516
  129.0 4.9 %place_early.1.early = f32[5,1280,128]{2,1,0:T(8,128)S(1)} custom-call(s32[108]{0:T(128)S(1)} %copy-done.2, s32[50]{0:T(128)S(1)} %listed_flags.1.flags, f32[56,80,128]{2,1,0:T(8,128)} %copy-done.4), custom_call_target="tpu_custom_call" | custom-call | bytes 6291456 | tf_op jit(solution)/shard_map/place_early/pallas_call | solution.py:379
  133.9 18.3 %all-to-all-done.1.piece = f32[48,80,128]{2,1,0:T(8,128)} async-done(((f32[48,80,128]{2,1,0:T(8,128)}), f32[48,80,128]{2,1,0:T(8,128)}, u32[]{:S(2)}, u32[]{:S(2)}) %all-to-all-start.1) | async-done | bytes 1966112 | tf_op jit(solution)/shard_map/all_to_all | solution.py:516
  152.2 4.2 %place_late.1 = f32[6400,128]{1,0:T(8,128)} custom-call(s32[108]{0:T(128)S(1)} %copy-done.2, s32[50]{0:T(128)S(1)} %listed_flags.1.flags, f32[5,1280,128]{2,1,0:T(8,128)S(1)} %place_early.1.early, f32[48,80,128]{2,1,0:T(8,128)} %all-to-all-done.1.piece), custom_call_target="tpu_custom_call" | custom-call | bytes 7340032 | tf_op jit(solution)/shard_map/place_late/pallas_call | solution.py:407
  (37 shorter events, 25.5 us)
Async XLA Ops:
  2.2 29.8 %collective-permute-start = (bf16[80,8192]{1,0:T(8,128)(2,1)S(1)}, bf16[80,8192]{1,0:T(8,128)(2,1)S(1)}, u32[]{:S(2)}, u32[]{:S(2)}) collective-permute-start(bf16[80,8192]{1,0:T(8,128)(2,1)S(1)} %own_part.1.refs_0_), channel_id=1, source_target_pairs={{0,8},{1,33},{2,10},{3,35},{4,12},{5,37},{6,14},{7,39},{8,16},{9,4... | collective-permute-start | bytes 3932168 | tf_op jit(solution)/shard_map/ppermute | solution.py:484
  4.3 31.7 %collective-permute-start.1 = (bf16[80,8192]{1,0:T(8,128)(2,1)S(1)}, bf16[80,8192]{1,0:T(8,128)(2,1)}, u32[]{:S(2)}, u32[]{:S(2)}) collective-permute-start(bf16[80,8192]{1,0:T(8,128)(2,1)S(1)} %own_part.1.refs_0_), channel_id=1, source_target_pairs={{0,32},{1,9},{2,34},{3,11},{4,36},{5,13},{6,38},{7,15},{8,40},{9,1... | collective-permute-start | bytes 3932168 | tf_op jit(solution)/shard_map/ppermute | solution.py:484
  5.6 30.4 %collective-permute-start.2 = (bf16[80,8192]{1,0:T(8,128)(2,1)S(1)}, bf16[80,8192]{1,0:T(8,128)(2,1)}, u32[]{:S(2)}, u32[]{:S(2)}) collective-permute-start(bf16[80,8192]{1,0:T(8,128)(2,1)S(1)} %own_part.1.refs_0_), channel_id=1, source_target_pairs={{0,96},{1,97},{2,98},{3,99},{4,100},{5,101},{6,102},{7,103},{8,104... | collective-permute-start | bytes 3932168 | tf_op jit(solution)/shard_map/ppermute | solution.py:484
  7.1 28.9 %collective-permute-start.3 = (bf16[80,8192]{1,0:T(8,128)(2,1)S(1)}, bf16[80,8192]{1,0:T(8,128)(2,1)}, u32[]{:S(2)}, u32[]{:S(2)}) collective-permute-start(bf16[80,8192]{1,0:T(8,128)(2,1)S(1)} %own_part.1.refs_0_), channel_id=1, source_target_pairs={{0,24},{1,25},{2,26},{3,27},{4,28},{5,29},{6,30},{7,31},{8,0},{9,1... | collective-permute-start | bytes 3932168 | tf_op jit(solution)/shard_map/ppermute | solution.py:484
  9.7 27.5 %copy-start.2 = (s32[108]{0:T(128)S(1)}, s32[108]{0:T(128)}, u32[]{:S(2)}) copy-start(s32[108]{0:T(128)} %dynamic-slice_bitcast_fusion.tab) | copy-start | bytes 1300
  16.2 49.8 %copy-start = (bf16[8,640,1024]{2,1,0:T(8,128)(2,1)}, bf16[8,640,1024]{2,1,0:T(8,128)(2,1)S(1)}, u32[]{:S(2)}) copy-start(bf16[8,640,1024]{2,1,0:T(8,128)(2,1)S(1)} %get-tuple-element.44.refs_5_.refs_1_.refs_2_.rows_ref.refs_3_) | copy-start | bytes 31457284
  36.0 18.1 %collective-permute-start.4 = (bf16[80,8192]{1,0:T(8,128)(2,1)S(1)}, bf16[80,8192]{1,0:T(8,128)(2,1)}, u32[]{:S(2)}, u32[]{:S(2)}) collective-permute-start(bf16[80,8192]{1,0:T(8,128)(2,1)S(1)} %collective-permute-done.refs_1_.odd_ref), channel_id=1, source_target_pairs={{0,32},{1,9},{2,34},{3,11},{4,36},{5,13},{6,38},{7,15},{8,40},{9,1... | collective-permute-start | bytes 3932168 | tf_op jit(solution)/shard_map/ppermute | solution.py:484
  37.9 27.8 %collective-permute-start.7 = (bf16[80,8192]{1,0:T(8,128)(2,1)S(1)}, bf16[80,8192]{1,0:T(8,128)(2,1)S(1)}, u32[]{:S(2)}, u32[]{:S(2)}) collective-permute-start(bf16[80,8192]{1,0:T(8,128)(2,1)S(1)} %choose.1), channel_id=1, source_target_pairs={{0,24},{1,25},{2,26},{3,27},{4,28},{5,29},{6,30},{7,31},{8,0},{9,1... | collective-permute-start | bytes 3932168 | tf_op jit(solution)/shard_map/ppermute | solution.py:484
  39.5 26.5 %collective-permute-start.6 = (bf16[80,8192]{1,0:T(8,128)(2,1)}, bf16[80,8192]{1,0:T(8,128)(2,1)S(1)}, u32[]{:S(2)}, u32[]{:S(2)}) collective-permute-start(bf16[80,8192]{1,0:T(8,128)(2,1)} %collective-permute-done.2.refs_3_), channel_id=1, source_target_pairs={{0,96},{1,97},{2,98},{3,99},{4,100},{5,101},{6,102},{7,103},{8,104... | collective-permute-start | bytes 3932168 | tf_op jit(solution)/shard_map/ppermute | solution.py:484
  54.2 30.4 %collective-permute-start.8 = (bf16[80,8192]{1,0:T(8,128)(2,1)}, bf16[80,8192]{1,0:T(8,128)(2,1)}, u32[]{:S(2)}, u32[]{:S(2)}) collective-permute-start(bf16[80,8192]{1,0:T(8,128)(2,1)} %collective-permute-done.4.refs_0_), channel_id=1, source_target_pairs={{0,32},{1,33},{2,34},{3,35},{4,36},{5,37},{6,38},{7,39},{8,40},{9,... | collective-permute-start | bytes 3932168 | tf_op jit(solution)/shard_map/ppermute | solution.py:484
  55.1 29.6 %collective-permute-start.9 = (bf16[80,8192]{1,0:T(8,128)(2,1)}, bf16[80,8192]{1,0:T(8,128)(2,1)}, u32[]{:S(2)}, u32[]{:S(2)}) collective-permute-start(bf16[80,8192]{1,0:T(8,128)(2,1)} %collective-permute-done.4.refs_0_), channel_id=1, source_target_pairs={{0,8},{1,9},{2,10},{3,11},{4,12},{5,13},{6,14},{7,15},{8,16},{9,17... | collective-permute-start | bytes 3932168 | tf_op jit(solution)/shard_map/ppermute | solution.py:484
  59.8 11.4 %collective-permute-start.5 = (f32[80,640]{1,0:T(8,128)S(1)}, f32[80,640]{1,0:T(8,128)S(1)}, u32[]{:S(2)}, u32[]{:S(2)}) collective-permute-start(f32[80,640]{1,0:T(8,128)S(1)} %get-tuple-element.54.refs_5_), channel_id=1, source_target_pairs={{0,120},{1,121},{2,122},{3,123},{4,124},{5,125},{6,126},{7,127},{8... | collective-permute-start | bytes 614408 | tf_op jit(solution)/shard_map/ppermute | solution.py:493
  73.3 47.9 %all-to-all-start = ((f32[56,80,128]{2,1,0:T(8,128)}), f32[56,80,128]{2,1,0:T(8,128)S(1)}, u32[]{:S(2)}, u32[]{:S(2)}) async-start(f32[56,80,128]{2,1,0:T(8,128)} %get-tuple-element.59), calls=%async_computation | async-start | bytes 4587520 | tf_op jit(solution)/shard_map/all_to_all | solution.py:516
  83.8 15.6 %collective-permute-start.11 = (bf16[80,8192]{1,0:T(8,128)(2,1)}, bf16[80,8192]{1,0:T(8,128)(2,1)S(1)}, u32[]{:S(2)}, u32[]{:S(2)}) collective-permute-start(bf16[80,8192]{1,0:T(8,128)(2,1)} %collective-permute-done.3.refs_4_), channel_id=1, source_target_pairs={{0,24},{2,26},{4,28},{6,30},{8,0},{10,2},{12,4},{14,6},{16,8},{18,... | collective-permute-start | bytes 3932168 | tf_op jit(solution)/shard_map/ppermute | solution.py:524
  84.7 22.2 %collective-permute-start.12 = (bf16[80,8192]{1,0:T(8,128)(2,1)}, bf16[80,8192]{1,0:T(8,128)(2,1)S(1)}, u32[]{:S(2)}, u32[]{:S(2)}) collective-permute-start(bf16[80,8192]{1,0:T(8,128)(2,1)} %collective-permute-done.8.refs_0_), channel_id=1, source_target_pairs={{1,9},{3,11},{5,13},{7,15},{9,17},{11,19},{13,21},{15,23},{17,25},... | collective-permute-start | bytes 3932168 | tf_op jit(solution)/shard_map/ppermute | solution.py:524
  86.6 21.9 %collective-permute-start.13 = (bf16[80,8192]{1,0:T(8,128)(2,1)}, bf16[80,8192]{1,0:T(8,128)(2,1)S(1)}, u32[]{:S(2)}, u32[]{:S(2)}) collective-permute-start(bf16[80,8192]{1,0:T(8,128)(2,1)} %collective-permute-done.9.refs_1_), channel_id=1, source_target_pairs={{0,32},{1,97},{2,34},{3,99},{4,36},{5,101},{6,38},{7,103},{8,40},{... | collective-permute-start | bytes 3932168 | tf_op jit(solution)/shard_map/ppermute | solution.py:484
  89.2 13.5 %copy-start.1 = (bf16[8,640,1024]{2,1,0:T(8,128)(2,1)S(1)}, bf16[8,640,1024]{2,1,0:T(8,128)(2,1)}, u32[]{:S(2)}) copy-start(bf16[8,640,1024]{2,1,0:T(8,128)(2,1)} %copy-done) | copy-start | bytes 31457284
  95.8 19.1 %collective-permute-start.10 = (f32[80,640]{1,0:T(8,128)S(1)}, f32[80,640]{1,0:T(8,128)S(1)}, u32[]{:S(2)}, u32[]{:S(2)}) collective-permute-start(f32[80,640]{1,0:T(8,128)S(1)} %get-tuple-element.65.refs_8_), channel_id=1, source_target_pairs={{0,104},{1,105},{2,106},{3,107},{4,108},{5,109},{6,110},{7,111},{8... | collective-permute-start | bytes 614408 | tf_op jit(solution)/shard_map/ppermute | solution.py:493
  96.6 18.3 %collective-permute-start.14 = (f32[80,640]{1,0:T(8,128)S(1)}, f32[80,640]{1,0:T(8,128)S(1)}, u32[]{:S(2)}, u32[]{:S(2)}) collective-permute-start(f32[80,640]{1,0:T(8,128)S(1)} %get-tuple-element.66.refs_1_), channel_id=1, source_target_pairs={{0,88},{1,89},{2,90},{3,91},{4,92},{5,93},{6,94},{7,95},{8,64},{9,... | collective-permute-start | bytes 614408 | tf_op jit(solution)/shard_map/ppermute | solution.py:493
  99.4 19.3 %collective-permute-start.15 = (f32[80,640]{1,0:T(8,128)S(1)}, f32[80,640]{1,0:T(8,128)S(1)}, u32[]{:S(2)}, u32[]{:S(2)}) collective-permute-start(f32[80,640]{1,0:T(8,128)S(1)} %get-tuple-element.67.refs_2_), channel_id=1, source_target_pairs={{0,112},{1,113},{2,114},{3,115},{4,116},{5,117},{6,118},{7,119},{8... | collective-permute-start | bytes 614408 | tf_op jit(solution)/shard_map/ppermute | solution.py:493
  121.2 1.4 copy-start.4
  121.2 5.9 %copy-start.3 = (s32[1976,2]{0,1:T(2,128)S(1)}, s32[1976,2]{0,1:T(2,128)}, u32[]{:S(2)}) copy-start(s32[1976,2]{0,1:T(2,128)} %param.8) | copy-start | bytes 47428
  122.6 29.6 %all-to-all-start.1 = ((f32[48,80,128]{2,1,0:T(8,128)}), f32[48,80,128]{2,1,0:T(8,128)}, u32[]{:S(2)}, u32[]{:S(2)}) async-start(f32[48,80,128]{2,1,0:T(8,128)} %get-tuple-element.72), calls=%async_computation.1 | async-start | bytes 3932160 | tf_op jit(solution)/shard_map/all_to_all | solution.py:516
